TPU v7x, 32 devices: a whole 2x2x4 slice. The times are simulated.
32 devices in a mesh: dp: 4 (over y, x), mp: 8 (over z, core).
Axes of the slice: x: 2, y: 2, z: 4, core: 2. Of those that a mesh axis runs over, the one named last changes fastest.
Arguments:
- x_in: bfloat16 [16384, 2048], P(('dp', 'mp')), may hold values from -6 to 6
- seq_lengths: int32 [4, 4], P('dp'), may hold values from 1 to 3585, as said below
- norm1_gain: bfloat16 [2048], P(('dp', 'mp')), may hold values from 0.5 to 1.5
- w_query: bfloat16 [2048, 256], P(('dp', 'mp')), may hold values from -0.125 to 0.125
- w_key: bfloat16 [2048, 256], P(('dp', 'mp')), may hold values from -0.125 to 0.125
- w_value: bfloat16 [2048, 2048], P(('dp', 'mp')), may hold values from -0.125 to 0.125
- w_out: bfloat16 [2048, 2048], P(('dp', 'mp')), may hold values from -4 to 4
- norm2_gain: bfloat16 [2048], P(('dp', 'mp')), may hold values from 0.5 to 1.5
- w_gate: bfloat16 [2048, 5632], P(None, 'mp'), may hold values from -0.125 to 0.125
- w_up: bfloat16 [2048, 5632], P(None, 'mp'), may hold values from -0.125 to 0.125
- w_down: bfloat16 [5632, 2048], P('mp'), may hold values from -0.078125 to 0.078125
- cotangent: bfloat16 [16384, 2048], P(('dp', 'mp')), may hold values from -6 to 6
Outputs:
- output: bfloat16 [16384, 2048], P(('dp', 'mp'))
- input_grad: bfloat16 [16384, 2048], P(('dp', 'mp'))
- norm1_gain_grad: float32 [2048], P(('dp', 'mp'))
- w_query_grad: float32 [2048, 256], P(('dp', 'mp'))
- w_key_grad: float32 [2048, 256], P(('dp', 'mp'))
- w_value_grad: float32 [2048, 2048], P(('dp', 'mp'))
- w_out_grad: float32 [2048, 2048], P(('dp', 'mp'))
- norm2_gain_grad: float32 [2048], P(('dp', 'mp'))
- w_gate_grad: float32 [2048, 5632], P(None, 'mp')
- w_up_grad: float32 [2048, 5632], P(None, 'mp')
- w_down_grad: float32 [5632, 2048], P('mp')
Inputs may be any that keep to these rules, and one draw needn't show every extreme that they name: `seq_lengths`: in every group one sequence, which one is drawn, has exactly 3585 tokens; every other sequence has at most 128; the other sequences and the padding after the last sequence together take fewer than 512 positions.
All inputs are finite; a program needn't handle non-finite values.
Results may differ from a plain program's by a relative error of at most 0.02.
Values may be sent and summed in bfloat16 or wider, within the bound.
No kernel may reach another device: no remote copies, remote signals or barrier semaphores. Data moves between devices by JAX's collectives and lax.ppermute only.
A program may use at most 768 MiB of HBM per device.

v0:
```python
import jax
import jax.numpy as jnp
from jax import lax
from jax.sharding import PartitionSpec as P

D = 2048
HEADS = 16
FEAT = 16
HEAD_V = 128


EPSILON = 1e-05
PRECISE = lax.Precision.HIGHEST


def entering(array, axis, combine, identity):
    size, place = (lax.axis_size(axis), lax.axis_index(axis))
    everything = jax.tree.map(
        lambda part, kind: lax.all_gather(part.astype(kind), axis),
        array,
        (jnp.bfloat16, jnp.bfloat16, jnp.bfloat16),
    )
    start = jax.tree.map(
        lambda part, zero: jnp.broadcast_to(jnp.asarray(zero, part.dtype), part.shape),
        array,
        identity,
    )

    def turn(k, before):
        reached = k < place
        new = combine(
            before, jax.tree.map(lambda part, own: part[k].astype(own.dtype), everything, array)
        )
        return jax.tree.map(lambda a, b: jnp.where(reached, a, b), new, before)

    return lax.fori_loop(0, size, turn, start)


def carried_in(array, axis, join, neutral):
    count = lax.axis_size(axis)
    place = lax.axis_index(axis)
    ahead = count - 1 - place
    gathered = jax.tree.map(
        lambda a, kind: lax.all_gather(a.astype(kind), axis),
        array,
        jax.tree.map(lambda a: jnp.bfloat16 if a.dtype == jnp.float32 else a.dtype, array),
    )
    state = jax.tree.map(lambda a, e: jnp.zeros_like(a) + jnp.asarray(e, a.dtype), array, neutral)

    def one(turn, state):
        source = count - 1 - turn
        return join(
            state,
            jax.tree.map(
                lambda a, own: lax.dynamic_index_in_dim(a, source, 0, False).astype(own.dtype),
                gathered,
                array,
            ),
        )

    return lax.fori_loop(0, ahead, one, state)


def taylor_map(scaled):
    row_count, head_count, feat_count = scaled.shape
    square = (scaled[:, :, :, None] * scaled[:, :, None, :]).reshape(
        row_count, head_count, feat_count * feat_count
    )
    return jnp.concatenate(
        [jnp.ones((row_count, head_count, 1), jnp.float32), scaled, square * 0.5**0.5], axis=2
    )


def block_mix(query_heads, key_heads, value_heads, prefix_state, prefix_norm, segments, reading):
    positions = jnp.arange(segments.shape[0], dtype=jnp.int32)
    kernel_dot = jnp.einsum("ihf,jhf->hij", query_heads, key_heads, precision=PRECISE)
    same_doc = (
        (segments[:, None] == segments[None, :]) & (positions[None, :] <= positions[:, None])
    ).astype(jnp.float32)
    weight = (1.0 + kernel_dot + 0.5 * kernel_dot * kernel_dot) * same_doc[None]
    feat_query = taylor_map(query_heads)
    numerator = jnp.einsum("hij,jhd->ihd", weight, value_heads, precision=PRECISE) + reading[
        :, None, None
    ] * jnp.einsum("ihe,hed->ihd", feat_query, prefix_state, precision=PRECISE)
    denominator = jnp.sum(weight, axis=2).T + reading[:, None] * jnp.einsum(
        "ihe,he->ih", feat_query, prefix_norm, precision=PRECISE
    )
    return numerator / denominator[:, :, None]


def block_state(key_heads, value_heads, last_doc):
    feat_key = taylor_map(key_heads) * last_doc[:, None, None]
    return (
        jnp.einsum("jhe,jhd->hed", feat_key, value_heads, precision=PRECISE),
        jnp.sum(feat_key, axis=0),
    )


def chain_join(earlier, later):
    return (
        later[0] + later[2] * earlier[0],
        later[1] + later[2] * earlier[1],
        earlier[2] * later[2],
    )


def norm_forward(inputs):
    inverse = lax.rsqrt(jnp.mean(inputs * inputs, axis=-1, keepdims=True) + EPSILON)
    return (inputs * inverse, inverse)


def norm_backward(grad_normed, unit_rows, inverse, gain_vec):
    gain_grad = jnp.sum(grad_normed * unit_rows, axis=0)
    grad_unit = grad_normed * gain_vec
    return (
        inverse * (grad_unit - unit_rows * jnp.mean(grad_unit * unit_rows, axis=-1, keepdims=True)),
        gain_grad,
    )


def contract_rows(left, right):
    return lax.dot_general(
        left, right, (((0,), (0,)), ((), ())), preferred_element_type=jnp.float32
    )


def contract_cols(left, right):
    return lax.dot_general(
        left, right, (((1,), (1,)), ((), ())), preferred_element_type=jnp.float32
    )


def gate_backward(grad_hidden, gate_rows, up_rows):
    sigma_gate = jax.nn.sigmoid(gate_rows)
    grad_wide = grad_hidden.astype(jnp.float32)
    grad_gate = grad_wide * up_rows * sigma_gate * (1.0 + gate_rows * (1.0 - sigma_gate))
    grad_up = grad_wide * gate_rows * sigma_gate
    return (grad_gate.astype(jnp.bfloat16), grad_up.astype(jnp.bfloat16))


def row_fold(normed_two, update, initial):
    return update(initial, lax.all_gather(normed_two, "mp", axis=0, tiled=True), jnp.int32(0))


def row_sums(make_term, row_count):
    return lax.psum_scatter(
        make_term(jnp.int32(0), row_count * lax.axis_size("mp")).astype(jnp.bfloat16),
        "mp",
        scatter_dimension=0,
        tiled=True,
    ).astype(jnp.float32)


def body(
    x_in,
    seq_lengths,
    norm1_gain,
    w_query,
    w_key,
    w_value,
    w_out,
    norm2_gain,
    w_gate,
    w_up,
    w_down,
    cotangent,
):
    row_count = x_in.shape[0]
    hidden_width = w_gate.shape[1]
    feat_scale = FEAT ** (-0.25)
    gains_one, gains_two, full_query, full_key, full_value, full_out = (
        lax.all_gather(norm1_gain, ("dp", "mp"), axis=0, tiled=True),
        lax.all_gather(norm2_gain, ("dp", "mp"), axis=0, tiled=True),
        lax.all_gather(w_query, ("dp", "mp"), axis=0, tiled=True),
        lax.all_gather(w_key, ("dp", "mp"), axis=0, tiled=True),
        lax.all_gather(w_value, ("dp", "mp"), axis=0, tiled=True),
        lax.all_gather(w_out, ("dp", "mp"), axis=0, tiled=True),
    )
    gain_one = gains_one.astype(jnp.float32)
    gain_two = gains_two.astype(jnp.float32)
    row_start = lax.axis_index("mp") * row_count
    seq_ends = jnp.cumsum(seq_lengths[0], dtype=jnp.int32)
    positions = row_start + jnp.arange(row_count, dtype=jnp.int32)
    segments = jnp.sum((positions[:, None] >= seq_ends[None, :]).astype(jnp.int32), axis=1)
    seg_before = jnp.sum((row_start - 1 >= seq_ends).astype(jnp.int32))
    opened = row_start > 0
    reading = ((segments == seg_before) & opened).astype(jnp.float32)
    last_doc = (segments == segments[-1]).astype(jnp.float32)
    carried = ((segments[-1] == seg_before) & opened).astype(jnp.float32)
    inputs = x_in.astype(jnp.float32)
    unit_one, inverse_one = norm_forward(inputs)
    normed_one = (unit_one * gain_one).astype(jnp.bfloat16)
    queries = jnp.dot(normed_one, full_query, preferred_element_type=jnp.float32).astype(
        jnp.bfloat16
    )
    keys_out = jnp.dot(normed_one, full_key, preferred_element_type=jnp.float32).astype(
        jnp.bfloat16
    )
    values_out = jnp.dot(normed_one, full_value, preferred_element_type=jnp.float32).astype(
        jnp.bfloat16
    )
    query_heads = queries.astype(jnp.float32).reshape(row_count, HEADS, FEAT) * feat_scale
    key_heads = keys_out.astype(jnp.float32).reshape(row_count, HEADS, FEAT) * feat_scale
    value_heads = values_out.astype(jnp.float32).reshape(row_count, HEADS, HEAD_V)
    own_state, own_norm = block_state(key_heads, value_heads, last_doc)
    identity = (jnp.zeros_like(own_state), jnp.zeros_like(own_norm), jnp.ones((), jnp.float32))
    prefix_state, prefix_norm, unused_pass = entering(
        (own_state, own_norm, carried), "mp", chain_join, identity
    )
    mixed_rows = block_mix(
        query_heads, key_heads, value_heads, prefix_state, prefix_norm, segments, reading
    )
    attended = mixed_rows.reshape(row_count, D).astype(jnp.bfloat16)
    hidden_in = inputs + jnp.dot(attended, full_out, preferred_element_type=jnp.float32)
    unit_two, inverse_two = norm_forward(hidden_in)
    normed_two = (unit_two * gain_two).astype(jnp.bfloat16)
    group_rows = row_count * lax.axis_size("mp")
    blank_rows = jnp.zeros((group_rows, hidden_width), jnp.float32)

    def project_rows(totals, shard_rows, offset):
        gate_part = jnp.dot(shard_rows, w_gate, preferred_element_type=jnp.float32)
        up_part = jnp.dot(shard_rows, w_up, preferred_element_type=jnp.float32)
        return (gate_part, up_part)

    gate_rows, up_rows = row_fold(normed_two, project_rows, (blank_rows, blank_rows))
    hidden = (jax.nn.silu(gate_rows) * up_rows).astype(jnp.bfloat16)

    def down_rows(first_row, row_total):
        return jnp.dot(hidden, w_down, preferred_element_type=jnp.float32)

    ffn_out = row_sums(down_rows, row_count)
    shard_rows = lax.all_gather(cotangent, "mp", axis=0, tiled=True)
    grad_hidden = contract_cols(shard_rows, w_down)
    down_grad = contract_rows(hidden, shard_rows)
    grad_gate, grad_up = gate_backward(grad_hidden.astype(jnp.bfloat16), gate_rows, up_rows)

    def weight_rows(totals, shard_rows, offset):
        return (contract_rows(shard_rows, grad_gate), contract_rows(shard_rows, grad_up))

    blank_weights = jnp.zeros((D, hidden_width), jnp.float32)
    gate_grad, up_grad = row_fold(normed_two, weight_rows, (blank_weights, blank_weights))

    def input_rows(first_row, row_total):
        return contract_cols(grad_gate, w_gate) + contract_cols(grad_up, w_up)

    grad_normed_two = row_sums(input_rows, row_count)
    output = (hidden_in + ffn_out).astype(jnp.bfloat16)
    gate_grad, up_grad, down_grad = (
        lax.psum(gate_grad.astype(jnp.bfloat16), "dp").astype(jnp.float32),
        lax.psum(up_grad.astype(jnp.bfloat16), "dp").astype(jnp.float32),
        lax.psum(down_grad.astype(jnp.bfloat16), "dp").astype(jnp.float32),
    )
    grad_two, gain_two_grad = norm_backward(grad_normed_two, unit_two, inverse_two, gain_two)
    grad_hidden_in = cotangent.astype(jnp.float32) + grad_two
    grad_branch = grad_hidden_in.astype(jnp.bfloat16)
    out_grad = contract_rows(attended, grad_branch)
    grad_attended = contract_cols(grad_branch, full_out).astype(jnp.bfloat16)

    def mix_only(query_in, key_in, value_in, state_in, norm_in):
        return block_mix(query_in, key_in, value_in, state_in, norm_in, segments, reading)

    unused_rows, mix_pull = jax.vjp(
        mix_only, query_heads, key_heads, value_heads, prefix_state, prefix_norm
    )
    grad_query, grad_key, grad_value, state_grad, norm_grad = mix_pull(
        grad_attended.astype(jnp.float32).reshape(row_count, HEADS, HEAD_V)
    )
    later_state, later_norm, unused_later = carried_in(
        (state_grad, norm_grad, carried), "mp", chain_join, identity
    )

    def state_only(key_in, value_in):
        return block_state(key_in, value_in, last_doc)

    unused_state, state_pull = jax.vjp(state_only, key_heads, value_heads)
    more_key, more_value = state_pull((later_state, later_norm))
    grad_queries = (grad_query * feat_scale).reshape(row_count, HEADS * FEAT).astype(jnp.bfloat16)
    grad_keys = (
        ((grad_key + more_key) * feat_scale).reshape(row_count, HEADS * FEAT).astype(jnp.bfloat16)
    )
    grad_values = (grad_value + more_value).reshape(row_count, D).astype(jnp.bfloat16)
    grad_normed_one = (
        contract_cols(grad_queries, full_query)
        + contract_cols(grad_keys, full_key)
        + contract_cols(grad_values, full_value)
    )
    grad_one, gain_one_grad = norm_backward(grad_normed_one, unit_one, inverse_one, gain_one)
    input_grad = (grad_hidden_in + grad_one).astype(jnp.bfloat16)
    mixer_sums = (
        lax.psum_scatter(gain_one_grad, ("dp", "mp"), scatter_dimension=0, tiled=True),
        lax.psum_scatter(
            contract_rows(normed_one, grad_queries), ("dp", "mp"), scatter_dimension=0, tiled=True
        ),
        lax.psum_scatter(
            contract_rows(normed_one, grad_keys), ("dp", "mp"), scatter_dimension=0, tiled=True
        ),
        lax.psum_scatter(
            contract_rows(normed_one, grad_values), ("dp", "mp"), scatter_dimension=0, tiled=True
        ),
        lax.psum_scatter(out_grad, ("dp", "mp"), scatter_dimension=0, tiled=True),
        lax.psum_scatter(gain_two_grad, ("dp", "mp"), scatter_dimension=0, tiled=True),
    )
    return (
        output,
        input_grad,
        mixer_sums[0],
        mixer_sums[1],
        mixer_sums[2],
        mixer_sums[3],
        mixer_sums[4],
        mixer_sums[5],
        gate_grad,
        up_grad,
        down_grad,
    )


def solution(mesh):
    placed = (
        P(("dp", "mp"), None),
        P("dp", None),
        P(("dp", "mp")),
        P(("dp", "mp"), None),
        P(("dp", "mp"), None),
        P(("dp", "mp"), None),
        P(("dp", "mp"), None),
        P(("dp", "mp")),
        P(None, "mp"),
        P(None, "mp"),
        P("mp", None),
        P(("dp", "mp"), None),
    )
    return jax.shard_map(
        body,
        mesh=mesh,
        in_specs=placed,
        out_specs=(
            P(("dp", "mp"), None),
            P(("dp", "mp"), None),
            P(("dp", "mp")),
            P(("dp", "mp"), None),
            P(("dp", "mp"), None),
            P(("dp", "mp"), None),
            P(("dp", "mp"), None),
            P(("dp", "mp")),
            P(None, "mp"),
            P(None, "mp"),
            P("mp", None),
        ),
        check_vma=False,
    )
```

profile of v0, /device:TPU:0, one launch (start us, length us, event | category | flops | bytes accessed | tf_op | source)
XLA Modules:
  0.0 2064.1 jit_solution(12957474670523662745)
XLA Ops:
  15.4 42.1 %all-reduce.6 = (bf16[2048]{0:T(1024)(128)(2,1)S(1)}, bf16[2048]{0:T(1024)(128)(2,1)S(1)}) all-reduce(bf16[2048]{0:T(1024)(128)(2,1)S(1)} %dynamic-update-slice, bf16[2048]{0:T(1024)(128)(2,1)S(1)} %dynamic-update-slice.2), channel_id=1, replica_groups=mesh['dp'=4,'mp'=8] {'dp','mp'}, use_global_device_ids=true, to_apply=%add | all-reduce | flops 4096 | bytes 16384
  75.1 72.0 %all-gather.13.cloned.1.call-done = bf16[2048,2048]{1,0:T(8,128)(2,1)} async-done(((bf16[64,2048]{1,0:T(8,128)(2,1)}), bf16[2048,2048]{1,0:T(8,128)(2,1)}) %all-gather.13.cloned.1.call-update) | async-done | bytes 8388624 | tf_op jit(solution)/shard_map/all_gather | solution.py:176
  210.2 19.3 fusion.16
  244.0 46.7 %all-gather.25.cloned.1.call-done = bf16[128,273,128]{2,0,1:T(8,128)(2,1)} async-done(((bf16[16,273,128]{2,0,1:T(8,128)(2,1)}), bf16[128,273,128]{2,0,1:T(8,128)(2,1)}) %all-gather.25.cloned.1.call-update) | async-done | bytes 8945680 | tf_op jit(solution)/shard_map/all_gather | solution.py:19
  290.8 47.6 %while.33 = (s32[]{:T(128)}, f32[16,273,128]{2,1,0:T(8,128)}, f32[16,273]{1,0:T(8,128)S(1)}, s32[]{:T(128)}, bf16[8,16,273,128]{3,1,0,2:T(8,128)(2,1)}, /*index=...) while((s32[]{:T(128)}, f32[16,273,128]{2,1,0:T(8,128)}, ...), condition=%wide.region_6.7_spmd.clone, body=%wide.region_5.6_spmd.clone.sunk | while | flops 2817365 | bytes 7871289 | solution.py:36
  383.4 137.2 %all-gather.23.cloned.1.call-done = bf16[4096,2048]{1,0:T(8,128)(2,1)} async-done(((bf16[512,2048]{1,0:T(8,128)(2,1)}), bf16[4096,2048]{1,0:T(8,128)(2,1)}) %all-gather.23.cloned.1.call-update) | async-done | bytes 16777232 | tf_op jit(solution)/shard_map/all_gather | solution.py:232
  539.1 133.0 %all-gather.21.cloned.1.call-done = bf16[4096,2048]{1,0:T(8,128)(2,1)} async-done(((bf16[512,2048]{1,0:T(8,128)(2,1)}), bf16[4096,2048]{1,0:T(8,128)(2,1)}) %all-gather.21.cloned.1.call-update) | async-done | bytes 16777232 | tf_op jit(solution)/shard_map/all_gather | solution.py:142
  672.1 19.0 fusion.105
  691.1 26.9 %fusion.7 = (bf16[4096,704]{0,1:T(8,128)(2,1)}, bf16[4096,704]{0,1:T(8,128)(2,1)}) fusion(bf16[4096,704]{0,1:T(8,128)(2,1)} %convolution_convert_fusion.1, f32[4096,704]{0,1:T(8,128)} %fusion.105, bf16[4096,2048]{1,0:T(8,128)(2,1)} %all-gather.21.cloned.1.call-done, bf16[2048,704]{0,1:T(8,128)(2,1)S(1)} %copy-done), kind=kOutput, calls=%fused_computation.21 | convolution fusion | flops 11851530240 | bytes 48496640 | tf_op jit(solution)/shard_map/dot_general | solution.py:222
  718.0 22.1 %fusion.106 = f32[4096,2048]{1,0:T(8,128)} fusion(bf16[4096,704]{0,1:T(8,128)(2,1)} %get-tuple-element.350, bf16[2048,704]{0,1:T(8,128)(2,1)} %param.24), kind=kOutput, calls=%fused_computation.158 | convolution fusion | flops 11811160064 | bytes 42205184 | tf_op jit(solution)/shard_map/dot_general | solution.py:128
  740.1 28.3 %add_convert_fusion = bf16[4096,2048]{1,0:T(8,128)(2,1)} fusion(f32[4096,2048]{1,0:T(8,128)} %fusion.106, bf16[2048,704]{0,1:T(8,128)(2,1)S(1)} %copy-done, f32[4096,704]{0,1:T(8,128)} %fusion.105, bf16[4096,704]{0,1:T(8,128)(2,1)S(1)} %copy-done.59), kind=kOutput, calls=%fused_computation.10 | convolution fusion | flops 11848122368 | bytes 70516736 | tf_op jit(solution)/shard_map/dot_general | solution.py:128
  770.2 19.7 convolution_convert_fusion
  790.0 145.1 %reduce-scatter.9.cloned.1.call-done = bf16[512,2048]{1,0:T(8,128)(2,1)} async-done(((bf16[4096,2048]{1,0:T(8,128)(2,1)}), bf16[512,2048]{1,0:T(8,128)(2,1)}) %reduce-scatter.9.cloned.1.call-update) | async-done | bytes 2097168 | tf_op jit(solution)/shard_map/reduce_scatter | solution.py:146
  939.6 164.4 %reduce-scatter.7.cloned.1.call-done = bf16[512,2048]{1,0:T(8,128)(2,1)} async-done(((bf16[4096,2048]{1,0:T(8,128)(2,1)}), bf16[512,2048]{1,0:T(8,128)(2,1)}) %reduce-scatter.7.cloned.1.call-update) | async-done | bytes 2097168 | tf_op jit(solution)/shard_map/reduce_scatter | solution.py:146
  1141.9 18.9 convolution_convert_fusion.4
  1179.5 20.7 %convolution_convert_fusion.2 = bf16[2048,704]{0,1:T(8,128)(2,1)} fusion(bf16[4096,2048]{1,0:T(8,128)(2,1)} %all-gather.21.cloned.1.call-done, f32[4096,704]{0,1:T(8,128)} %fusion.105, bf16[4096,704]{0,1:T(8,128)(2,1)S(1)} %bitcast.233), kind=kOutput, calls=%fused_computation.83 | convolution fusion | flops 11832786944 | bytes 36962304 | tf_op jit(solution)/shard_map/dot_general | solution.py:122
  1249.4 20.3 fusion.4
  1286.9 24.0 %while.32 = (s32[]{:T(128)}, f32[16,273,128]{2,1,0:T(8,128)S(1)}, f32[16,273]{1,0:T(8,128)S(1)}, s32[]{:T(128)}, bf16[8,16,273,128]{3,1,0,2:T(8,128)(2,1)}, /*in...) while((s32[]{:T(128)}, f32[16,273,128]{2,1,0:T(8,128)S(1)}, ...), condition=%wide.region_16.17_spmd, body=%wide.region_15.16_spmd.sunk | while | flops 1690423 | bytes 7871329 | solution.py:61
  1360.7 23.2 %fusion.14 = f32[16,128,512]{2,1,0:T(8,128)S(1)} fusion(f32[16,512,512]{1,2,0:T(8,128)} %get-tuple-element.357, f32[512,512]{0,1:T(8,128)} %fusion.78, f32[512,16]{0,1:T(8,128)S(1)} %copy-done.48, f32[512,2048]{0,1:T(8,128)} %copy.54), kind=kOutput, calls=%fused_computation.46 | convolution fusion | flops 6464471040 | bytes 26247168 | tf_op jit(solution)/shard_map/transpose(jvp(hij,jhd->ihd))/dot_general | solution.py:82
  1431.2 39.6 %all-reduce.5 = (f32[2048]{0:T(1024)S(1)}, f32[2048]{0:T(1024)S(1)}) all-reduce(f32[2048]{0:T(1024)S(1)} %get-tuple-element.307, f32[2048]{0:T(1024)S(1)} %copy-done.44), channel_id=8, replica_groups=mesh['dp'=4,'mp'=8] {'dp','mp'}, use_global_device_ids=true, to_apply=%region_21.22.clone | all-reduce | flops 4096 | bytes 32768
  1478.7 69.2 %reduce-scatter.11.cloned.1.call-done = f32[64,256]{1,0:T(8,128)} async-done(((f32[2048,256]{1,0:T(8,128)}), f32[64,256]{1,0:T(8,128)}) %reduce-scatter.11.cloned.1.call-update) | async-done | bytes 65552 | tf_op jit(solution)/shard_map/reduce_scatter | solution.py:291
  1547.8 135.9 %reduce-scatter.13.cloned.1.call-done = f32[64,256]{1,0:T(8,128)} async-done(((f32[2048,256]{1,0:T(8,128)}), f32[64,256]{1,0:T(8,128)}) %reduce-scatter.13.cloned.1.call-update) | async-done | bytes 65552 | tf_op jit(solution)/shard_map/reduce_scatter | solution.py:294
  1683.8 186.2 %reduce-scatter.17.cloned.1.call-done = f32[64,2048]{1,0:T(8,128)} async-done(((f32[2048,2048]{1,0:T(8,128)}), f32[64,2048]{1,0:T(8,128)}) %reduce-scatter.17.cloned.1.call-update) | async-done | bytes 524304 | tf_op jit(solution)/shard_map/reduce_scatter | solution.py:300
  1869.9 187.2 %reduce-scatter.15.cloned.1.call-done = f32[64,2048]{1,0:T(8,128)} async-done(((f32[2048,2048]{1,0:T(8,128)}), f32[64,2048]{1,0:T(8,128)}) %reduce-scatter.15.cloned.1.call-update) | async-done | bytes 524304 | tf_op jit(solution)/shard_map/reduce_scatter | solution.py:297
  (304 shorter events, 460.5 us)
Async XLA Ops:
  7.2 683.9 %copy-start = (bf16[2048,704]{0,1:T(8,128)(2,1)S(1)}, bf16[2048,704]{0,1:T(8,128)(2,1)}, u32[]{:S(2)}) copy-start(bf16[2048,704]{0,1:T(8,128)(2,1)} %param.25) | copy-start | bytes 8650756
  7.2 60.4 %all-gather.17.cloned.1.call-start = ((), (), s32[]{:S(2)}) async-start(), calls=%async_computation.8 | async-start | bytes 1081344 | tf_op jit(solution)/shard_map/all_gather | solution.py:175
  7.9 139.2 %all-gather.13.cloned.1.call-start = ((), (), s32[]{:S(2)}) async-start(), calls=%async_computation.6 | async-start | bytes 8650752 | tf_op jit(solution)/shard_map/all_gather | solution.py:176
  8.7 194.3 %all-gather.15.cloned.1.call-start = ((), (), s32[]{:S(2)}) async-start(), calls=%async_computation.7 | async-start | bytes 1081344 | tf_op jit(solution)/shard_map/all_gather | solution.py:174
  9.4 281.4 %all-gather.25.cloned.1.call-start = ((), (), s32[]{:S(2)}) async-start(), calls=%async_computation.18 | async-start | bytes 10063872 | tf_op jit(solution)/shard_map/all_gather | solution.py:19
  57.6 145.4 %copy-start.38 = (f32[2048]{0:T(1024)}, f32[2048]{0:T(1024)S(1)}, u32[]{:S(2)}) copy-start(f32[2048]{0:T(1024)S(1)} %convert_element_type.241) | copy-start | bytes 24580
  57.6 291.0 %copy-start.50 = (f32[273]{0:T(512)}, f32[273]{0:T(512)S(1)}, u32[]{:S(2)}) copy-start(f32[273]{0:T(512)S(1)} %pad.3.clone) | copy-start | bytes 3280
  58.9 289.6 %copy-start.45 = (f32[512]{0:T(512)}, f32[512]{0:T(512)S(1)}, u32[]{:S(2)}) copy-start(f32[512]{0:T(512)S(1)} %get-tuple-element.354) | copy-start | bytes 6148
  162.5 206.9 %all-gather.19.cloned.1.call-start = ((), (), s32[]{:S(2)}) async-start(), calls=%async_computation.9 | async-start | bytes 8650752 | tf_op jit(solution)/shard_map/all_gather | solution.py:177
  163.1 357.5 %all-gather.23.cloned.1.call-start = ((), (), s32[]{:S(2)}) async-start(), calls=%async_computation.12 | async-start | bytes 18874368 | tf_op jit(solution)/shard_map/all_gather | solution.py:232
  163.7 508.4 %all-gather.21.cloned.1.call-start = ((), (), s32[]{:S(2)}) async-start(), calls=%async_computation.10 | async-start | bytes 18874368 | tf_op jit(solution)/shard_map/all_gather | solution.py:142
  182.6 196.6 %copy-start.35 = (f32[2048]{0:T(1024)}, f32[2048]{0:T(1024)S(1)}, u32[]{:S(2)}) copy-start(f32[2048]{0:T(1024)S(1)} %convert_element_type.260) | copy-start | bytes 24580
  383.3 551.8 %reduce-scatter.9.cloned.1.call-start = ((), (), s32[]{:S(2)}) async-start(), calls=%async_computation.13 | async-start | bytes 18874368 | tf_op jit(solution)/shard_map/reduce_scatter | solution.py:146
  768.4 335.6 %reduce-scatter.7.cloned.1.call-start = ((), (), s32[]{:S(2)}) async-start(), calls=%async_computation.11 | async-start | bytes 18874368 | tf_op jit(solution)/shard_map/reduce_scatter | solution.py:146
  789.9 145.2 %copy-start.36 = (f32[2048]{0:T(1024)S(1)}, f32[2048]{0:T(1024)}, u32[]{:S(2)}) copy-start(f32[2048]{0:T(1024)} %copy-done.35) | copy-start | bytes 24580
  789.9 145.2 %copy-start.43 = (f32[512]{0:T(512)S(1)}, f32[512]{0:T(512)}, u32[]{:S(2)}) copy-start(f32[512]{0:T(512)} %copy-done.42) | copy-start | bytes 6148
  789.9 314.1 %copy-start.18 = (bf16[512,2048]{1,0:T(8,128)(2,1)S(1)}, bf16[512,2048]{1,0:T(8,128)(2,1)}, u32[]{:S(2)}) copy-start(bf16[512,2048]{1,0:T(8,128)(2,1)} %param.27) | copy-start | bytes 6291460
  789.9 496.4 %all-gather.27.cloned.1.call-start = ((), (), s32[]{:S(2)}) async-start(), calls=%async_computation.19 | async-start | bytes 10063872 | tf_op jit(solution)/shard_map/all_gather | solution.py:44
  1141.9 265.8 %all-reduce.10.cloned.1.call-start = ((), (), s32[]{:S(2)}) async-start(), calls=%async_computation.20 | async-start | bytes 17301504 | tf_op jit(solution)/shard_map/psum | solution.py:249
  1200.3 347.5 %reduce-scatter.11.cloned.1.call-start = ((), (), s32[]{:S(2)}) async-start(), calls=%async_computation.14 | async-start | bytes 2162688 | tf_op jit(solution)/shard_map/reduce_scatter | solution.py:291
  1286.3 397.5 %reduce-scatter.13.cloned.1.call-start = ((), (), s32[]{:S(2)}) async-start(), calls=%async_computation.15 | async-start | bytes 2162688 | tf_op jit(solution)/shard_map/reduce_scatter | solution.py:294
  1346.1 523.8 %reduce-scatter.17.cloned.1.call-start = ((), (), s32[]{:S(2)}) async-start(), calls=%async_computation.17 | async-start | bytes 17301504 | tf_op jit(solution)/shard_map/reduce_scatter | solution.py:300
  1360.4 696.7 %reduce-scatter.15.cloned.1.call-start = ((), (), s32[]{:S(2)}) async-start(), calls=%async_computation.16 | async-start | bytes 17301504 | tf_op jit(solution)/shard_map/reduce_scatter | solution.py:297
  1472.0 585.2 %copy-start.1 = (bf16[2048,704]{0,1:T(8,128)(2,1)S(1)}, bf16[2048,704]{0,1:T(8,128)(2,1)}, u32[]{:S(2)}) copy-start(bf16[2048,704]{0,1:T(8,128)(2,1)} %param.25) | copy-start | bytes 8650756
  (55 other events, 972.7 us)
Sparse Core Ops, SparseCore 0:
  11.0 56.5 all-gather.16
  70.6 76.5 all-gather.12
  150.2 52.3 all-gather.14
  204.6 86.1 all-gather.24
  293.6 75.7 all-gather.18
  370.8 149.6 all-gather.22
  522.7 149.3 all-gather.20
  768.5 166.4 reduce-scatter.8
  937.4 166.5 reduce-scatter.6
  1142.0 86.0 all-gather.26
  1232.5 175.1 all-reduce.9
  1410.5 137.2 reduce-scatter.10
  1550.6 133.0 reduce-scatter.12
  1686.6 183.2 reduce-scatter.16
  1872.7 184.3 reduce-scatter.14
where the time goes:
time: 2080 us; the launch traced here: 2060 us
  waiting for transfers between devices  1300 us (62%)
  matrix products  451 us (22%)
  blocking collectives  127 us (6%)
  other arithmetic  101 us (5%)
  local copies, waits for them, and re-layouts  58.5 us (3%)
    reduce_scatter x2, waiting for transfers between devices, row_sums(): lax.psum_scatter(make_term(jnp.int32(0), row_count * lax.axis_size('mp'))...  309 us
    reduce_scatter x1, waiting for transfers between devices, body(): lax.psum_scatter(contract_rows(normed_one, grad_values), ('dp', 'mp'), sc...  187 us
    reduce_scatter x1, waiting for transfers between devices, body(): lax.psum_scatter(out_grad, ('dp', 'mp'), scatter_dimension=0, tiled=True)  186 us
    all_gather x1, waiting for transfers between devices, body(): shard_rows = lax.all_gather(cotangent, 'mp', axis=0, tiled=True)  137 us
    reduce_scatter x1, waiting for transfers between devices, body(): lax.psum_scatter(contract_rows(normed_one, grad_keys), ('dp', 'mp'), scat...  136 us
    all_gather x1, waiting for transfers between devices, row_fold(): lax.all_gather(normed_two, 'mp', axis=0, tiled=True)  133 us
    unnamed x3, blocking collectives  98 us
    dot_general x7, matrix products, contract_cols(): lax.dot_general(left, right, (((1,), (1,)), ((), ())), preferred_element_...  87.8 us
  transfers between devices with their start and end apart: 15, of which 13 were waited for; matrix products, arithmetic and copies ran while one was open for 23% of the time, Pallas kernels for 0%

commit v1 on v0

v1 whole, which is shorter than its diff:
```python
import functools
import numpy as np
import jax
import jax.numpy as jnp
from jax import lax
from jax.experimental import pallas as pl
from jax.experimental.pallas import tpu as pltpu

HEADS = 16
FEAT = 16
HEAD_V = 128
WIDE = 256
STATE = 160
SQUARES = FEAT * (FEAT + 1) // 2
LINEAR = SQUARES + FEAT
HALF_HEADS = 128 // FEAT
STEP_HEADS = 8


def feature_tables():
    pairs = [(a, b) for a in range(FEAT) for b in range(a, FEAT)]
    pick = np.zeros((3, WIDE, WIDE), np.float32)
    for row in range(128):
        for entry, (a, b) in enumerate(pairs):
            if row % FEAT == a:
                pick[0, row, entry] = 1.0
                pick[1, row, entry] = 0.5 if a == b else 1.0
            if row % FEAT == b:
                pick[2, row, entry] = 1.0
        pick[0:2, row, SQUARES + row % FEAT] = 1.0
    pick[0:2, 128, LINEAR] = 1.0
    pick[2, 128, SQUARES : LINEAR + 1] = 1.0
    back = np.stack([np.concatenate([pick[n, :128], pick[2, :128]], axis=1) for n in (0, 1)])
    return jnp.asarray(pick, jnp.bfloat16), jnp.asarray(back, jnp.bfloat16)


def mul(left, right, kind="nn"):
    dims = {"nn": ((1,), (0,)), "nt": ((1,), (1,)), "tn": ((0,), (0,))}[kind]
    return lax.dot_general(left, right, (dims, ((), ())), preferred_element_type=jnp.float32)


def head_lanes(head, rows):
    lane = lax.broadcasted_iota(jnp.int32, (rows, 128), 1)
    return lane // FEAT == lax.rem(head, HALF_HEADS)


def own_lanes(block, head):
    scaled = block * jnp.asarray(FEAT**-0.25, jnp.bfloat16)
    return jnp.where(head_lanes(head, block.shape[0]), scaled, jnp.zeros_like(scaled))


def first_lanes(*columns):
    lane = lax.broadcasted_iota(jnp.int32, (columns[0].shape[0], 128), 1)
    out = jnp.zeros(lane.shape, jnp.float32)
    for n, column in enumerate(columns):
        out = jnp.where(lane == n, column, out)
    return out.astype(jnp.bfloat16)


def factors(own, pick_ref, which, kept):
    ones = first_lanes(jnp.ones_like(kept))
    plain = jnp.concatenate([own, ones], axis=1)
    masked = jnp.concatenate(
        [own * kept.astype(jnp.bfloat16), ones * kept.astype(jnp.bfloat16)], axis=1
    )
    first = mul(masked, pick_ref[which]).astype(jnp.bfloat16)
    second = mul(plain, pick_ref[2]).astype(jnp.bfloat16)
    return first, second


def pack_state(state, norm_rows):
    row = lax.broadcasted_iota(jnp.int32, (STATE, HEAD_V), 0)
    out = jnp.where(row == LINEAR + 1, norm_rows[0:1, :HEAD_V], state[:STATE])
    return jnp.where(row == LINEAR + 2, norm_rows[0:1, HEAD_V:], out)


def widen(packed):
    padded = jnp.concatenate([packed, jnp.zeros((WIDE - STATE, HEAD_V), packed.dtype)], axis=0)
    norm = jnp.concatenate(
        [packed[LINEAR + 1 : LINEAR + 2, :], packed[LINEAR + 2 : LINEAR + 3, :]], axis=1
    )
    return padded, norm


def step_heads():
    first = pl.program_id(0) * STEP_HEADS
    return [
        (first + n, n, slice(n * HEAD_V, (n + 1) * HEAD_V)) for n in range(STEP_HEADS)
    ]


def state_kernel(k_ref, v_ref, pick_ref, last_ref, out_ref):
    keys, last = k_ref[...], last_ref[...]
    ones = jnp.ones((16, keys.shape[0]), jnp.bfloat16)
    for head, n, lanes in step_heads():
        first, second = factors(own_lanes(keys, head), pick_ref, 0, last)
        phi = first * second
        state = mul(phi, v_ref[:, lanes], "tn")
        out_ref[n] = pack_state(state, mul(ones, phi)).astype(out_ref.dtype)


def causal_mask(seg_col_ref, seg_row_ref, mask_ref):
    rows = mask_ref.shape[0]
    i = lax.broadcasted_iota(jnp.int32, (rows, rows), 0)
    j = lax.broadcasted_iota(jnp.int32, (rows, rows), 1)
    keep = (seg_col_ref[...] == seg_row_ref[0:1, :]) & (j <= i)
    mask_ref[...] = keep.astype(jnp.float32).astype(jnp.bfloat16)


def triangle(rows):
    half = rows // 2
    return ((slice(0, half), slice(0, half)), (slice(half, rows), slice(0, rows)))


def local_kernel(q_ref, k_ref, v_ref, seg_col_ref, seg_row_ref, num_ref, den_ref, mask_ref):
    @pl.when(pl.program_id(0) == 0)
    def _():
        causal_mask(seg_col_ref, seg_row_ref, mask_ref)

    queries = q_ref[...]
    scaled = k_ref[...] * jnp.asarray(FEAT**-0.25, jnp.bfloat16)
    for head, _, lanes in step_heads():
        own_q = own_lanes(queries, head)
        value = v_ref[:, lanes]
        wide = jnp.concatenate([value, jnp.ones_like(value)], axis=1)
        for at, upto in triangle(own_q.shape[0]):
            up = 1.0 + mul(own_q[at], scaled[upto], "nt")
            kappa = (0.5 * up * up + 0.5).astype(jnp.bfloat16) * mask_ref[at, upto]
            both = mul(kappa, wide[upto])
            num_ref[at, lanes] = both[:, :HEAD_V]
            den_ref[at, lanes] = both[:, HEAD_V:]


def prefix_kernel(
    q_ref, num_ref, den_ref, state_ref, pick_ref, reading_ref, out_ref, inverse_ref
):
    queries, reading = q_ref[...], reading_ref[...]
    for head, n, lanes in step_heads():
        first, second = factors(own_lanes(queries, head), pick_ref, 1, reading)
        phi = first * second
        state, norm = widen(state_ref[n])
        num = num_ref[:, lanes] + mul(phi, state)
        norm = mul(phi, jnp.broadcast_to(norm, (HEAD_V, WIDE)), "nt")
        inverse = 1.0 / (den_ref[:, lanes] + norm)
        out_ref[:, lanes] = (num * inverse).astype(jnp.bfloat16)
        inverse_ref[:, lanes] = inverse


def scaled_grad(g_ref, att_ref, inverse_ref, lanes):
    gn = (g_ref[:, lanes].astype(jnp.float32) * inverse_ref[:, lanes]).astype(jnp.bfloat16)
    mixed = att_ref[:, lanes].astype(jnp.float32)
    gd = -jnp.sum(gn.astype(jnp.float32) * mixed, axis=1, keepdims=True)
    return gn, gd


def state_grad_kernel(q_ref, g_ref, att_ref, inverse_ref, pick_ref, reading_ref, out_ref):
    queries, reading = q_ref[...], reading_ref[...]
    for head, n, lanes in step_heads():
        gn, gd = scaled_grad(g_ref, att_ref, inverse_ref, lanes)
        first, second = factors(own_lanes(queries, head), pick_ref, 1, reading)
        phi = first * second
        state = mul(phi, gn, "tn")
        wide = jnp.broadcast_to(gd, gn.shape).astype(jnp.bfloat16)
        out_ref[n] = pack_state(state, mul(wide, phi, "tn")).astype(out_ref.dtype)


def chain(grad_phi, first, second, back_ref, which, head):
    both = jnp.concatenate([grad_phi * second, grad_phi * first], axis=1)
    grad = mul(both, back_ref[which], "nt")
    return jnp.where(head_lanes(head, grad_phi.shape[0]), grad, 0.0)


def local_grad_kernel(
    q_ref, k_ref, v_ref, g_ref, att_ref, inverse_ref, state_ref, pick_ref, back_ref,
    reading_ref, seg_col_ref, seg_row_ref, gq_ref, gk_ref, gv_ref, mask_ref, acc_ref,
):
    start = pl.program_id(0) * STEP_HEADS

    @pl.when(start == 0)
    def _():
        causal_mask(seg_col_ref, seg_row_ref, mask_ref)

    @pl.when(lax.rem(start, HALF_HEADS) == 0)
    def _():
        acc_ref[...] = jnp.zeros_like(acc_ref)
        gk_ref[...] = jnp.zeros_like(gk_ref)

    queries, keys, reading = q_ref[...], k_ref[...], reading_ref[...]
    half = queries.shape[0] // 2
    query_sums = jnp.zeros_like(acc_ref)
    key_sums = jnp.zeros_like(gk_ref)
    for head, n, lanes in step_heads():
        gn, gd = scaled_grad(g_ref, att_ref, inverse_ref, lanes)
        high = gd.astype(jnp.bfloat16).astype(jnp.float32)
        gn_wide = jnp.concatenate([gn, first_lanes(high, gd - high)], axis=1)
        ones = jnp.ones_like(gd)
        v_wide = jnp.concatenate([v_ref[:, lanes], first_lanes(ones, ones)], axis=1)
        own_q = own_lanes(queries, head)
        own_k = own_lanes(keys, head)
        parts, query_parts, key_parts = [], [], []
        for at, upto in triangle(own_q.shape[0]):
            keep = mask_ref[at, upto]
            up = 1.0 + mul(own_q[at], own_k[upto], "nt")
            kappa = (0.5 * up * up + 0.5).astype(jnp.bfloat16) * keep
            grad_t = mul(gn_wide[at], v_wide[upto], "nt").astype(jnp.bfloat16)
            grad_t = grad_t * up.astype(jnp.bfloat16) * keep
            query_parts.append(mul(grad_t, own_k[upto]))
            key_parts.append(mul(grad_t, own_q[at], "tn"))
            parts.append(mul(kappa, gn[at], "tn"))
        gv_ref[:half, lanes] = parts[0] + parts[1][:half]
        gv_ref[half:, lanes] = parts[1][half:]
        key_sums += key_parts[1] + jnp.concatenate(
            [key_parts[0], jnp.zeros_like(key_parts[0])], axis=0
        )
        first, second = factors(own_q, pick_ref, 1, reading)
        state, norm = widen(state_ref[n])
        grad_phi = mul(gn, state, "nt") + gd * norm.astype(jnp.float32)
        grad_phi = (grad_phi * reading).astype(jnp.bfloat16)
        query_sums += jnp.concatenate(query_parts, axis=0)
        query_sums += chain(grad_phi, first, second, back_ref, 1, head)
    acc_ref[...] += query_sums
    gk_ref[...] += key_sums

    @pl.when(lax.rem(start + STEP_HEADS, HALF_HEADS) == 0)
    def _():
        gq_ref[...] = (acc_ref[...] * FEAT**-0.25).astype(jnp.bfloat16)


def later_grad_kernel(
    k_ref, v_ref, gk_in_ref, gv_in_ref, state_ref, pick_ref, back_ref, last_ref,
    gk_ref, gv_ref, acc_ref,
):
    start = pl.program_id(0) * STEP_HEADS

    @pl.when(lax.rem(start, HALF_HEADS) == 0)
    def _():
        acc_ref[...] = gk_in_ref[...]

    keys, last = k_ref[...], last_ref[...]
    total = jnp.zeros_like(acc_ref)
    for head, n, lanes in step_heads():
        first, second = factors(own_lanes(keys, head), pick_ref, 0, last)
        state, norm = widen(state_ref[n])
        values = gv_in_ref[:, lanes] + mul(first * second, state)
        gv_ref[:, lanes] = values.astype(jnp.bfloat16)
        grad_phi = mul(v_ref[:, lanes], state, "nt") + norm.astype(jnp.float32)
        grad_phi = (grad_phi * last).astype(jnp.bfloat16)
        total = total + chain(grad_phi, first, second, back_ref, 0, head)
    acc_ref[...] += total

    @pl.when(lax.rem(start + STEP_HEADS, HALF_HEADS) == 0)
    def _():
        gk_ref[...] = (acc_ref[...] * FEAT**-0.25).astype(jnp.bfloat16)


def specs(rows):
    return dict(
        pair=pl.BlockSpec((rows, 128), lambda h: (0, h * STEP_HEADS // HALF_HEADS)),
        head=pl.BlockSpec((rows, STEP_HEADS * HEAD_V), lambda h: (0, h)),
        state=pl.BlockSpec((STEP_HEADS, STATE, HEAD_V), lambda h: (h, 0, 0)),
        pick=pl.BlockSpec((3, WIDE, WIDE), lambda h: (0, 0, 0)),
        back=pl.BlockSpec((2, 128, 2 * WIDE), lambda h: (0, 0, 0)),
        column=pl.BlockSpec((rows, 1), lambda h: (0, 0)),
        row=pl.BlockSpec((8, rows), lambda h: (0, 0)),
    )


def heads_call(kernel, rows, ins, outs, scratch=(), name=None):
    table = specs(rows)
    shapes = {
        "pair": (rows, HEADS * FEAT),
        "head": (rows, HEADS * HEAD_V),
        "state": (HEADS, STATE, HEAD_V),
    }
    return pl.pallas_call(
        kernel,
        grid=(HEADS // STEP_HEADS,),
        in_specs=[table[kind] for kind in ins],
        out_specs=[table[kind] for kind, _ in outs],
        out_shape=[jax.ShapeDtypeStruct(shapes[kind], kept) for kind, kept in outs],
        scratch_shapes=list(scratch),
        compiler_params=pltpu.CompilerParams(
            dimension_semantics=("arbitrary",), vmem_limit_bytes=32 * 2**20
        ),
        cost_estimate=pl.CostEstimate(flops=2**20, bytes_accessed=2**16, transcendentals=0),
        name=name,
    )


f32, bf = jnp.float32, jnp.bfloat16


def mix_state(k, v, tables, last):
    rows = k.shape[0]
    return heads_call(state_kernel, rows, ["pair", "head", "pick", "column"],
        [("state", bf)], name="mix_state")(k, v, tables[0], last)[0]


def mix_local(q, k, v, seg_col, seg_row):
    rows = k.shape[0]
    return heads_call(local_kernel, rows, ["pair", "pair", "head", "column", "row"],
        [("head", f32), ("head", f32)], [pltpu.VMEM((rows, rows), bf)], name="mix_local")(q, k, v, seg_col, seg_row)


def mix_prefix(q, num, den, state, tables, reading):
    rows = q.shape[0]
    return heads_call(prefix_kernel, rows, ["pair", "head", "head", "state", "pick", "column"],
        [("head", bf), ("head", f32)], name="mix_prefix")(q, num, den, state, tables[0], reading)


def mix_state_grad(q, g, att, inverse, tables, reading):
    rows = q.shape[0]
    return heads_call(state_grad_kernel, rows, ["pair", "head", "head", "head", "pick", "column"],
        [("state", bf)], name="mix_state_grad")(q, g, att, inverse, tables[0], reading)[0]


def mix_local_grad(q, k, v, g, att, inverse, state, tables, reading, seg_col, seg_row):
    rows = q.shape[0]
    return heads_call(local_grad_kernel, rows,
        ["pair", "pair", "head", "head", "head", "head", "state", "pick", "back", "column", "column", "row"],
        [("pair", bf), ("pair", f32), ("head", f32)],
        [pltpu.VMEM((rows, rows), bf), pltpu.VMEM((rows, 128), f32)], name="mix_local_grad")(
        q, k, v, g, att, inverse, state, *tables, reading, seg_col, seg_row)


def mix_later_grad(k, v, gk, gv, state, tables, last):
    rows = k.shape[0]
    return heads_call(later_grad_kernel, rows,
        ["pair", "head", "pair", "head", "state", "pick", "back", "column"],
        [("pair", bf), ("head", bf)], [pltpu.VMEM((rows, 128), f32)], name="mix_later_grad")(
        k, v, gk, gv, state, *tables, last)


from jax.sharding import PartitionSpec as P

D = 2048
EPSILON = 1e-05
LIMIT = 36 * 2**20
TILE = 352


def cost(flops, moved):
    return pl.CostEstimate(flops=flops, bytes_accessed=moved, transcendentals=0)


def whole(*shape):
    return pl.BlockSpec(shape, lambda *_: (0,) * len(shape), pipeline_mode=pl.Buffered(1))


def tiling(parts, rows):
    if parts == 1:
        taken = TILE if rows % TILE == 0 else rows
        return 1, taken, rows // taken
    taken = max(1, TILE // rows)
    taken = taken if parts % taken == 0 else parts
    return taken, rows, parts // taken


def gate_kernel(x_ref, c_ref, *refs):
    count = len(refs) // 3
    half = x_ref.shape[0] // 2
    for n in range(count):
        both_ref, down_ref, out_ref = refs[2 * n], refs[2 * n + 1], refs[2 * count + n]
        parts, _, rows, _ = both_ref.shape
        gate_w, up_w = [both_ref[:, k].reshape(parts * rows, D) for k in range(2)]
        down_w = down_ref[:, 0].reshape(parts * rows, D)
        for at in (slice(0, half), slice(half, 2 * half)):
            x, c = x_ref[at, :], c_ref[at, :]
            gate = mul(gate_w, x, "nt")
            up = mul(up_w, x, "nt")
            grad = mul(down_w, c, "nt").astype(bf).astype(f32)
            sig = 1.0 / (1.0 + jnp.exp(-gate))
            act = gate * sig
            out_ref[0, :, at] = (grad * up * sig * (1.0 + gate * (1.0 - sig))).astype(bf)
            out_ref[1, :, at] = (grad * act).astype(bf)
            out_ref[2, :, at] = (act * up).astype(bf)


def ffn_gates(x, c, weights):
    rows, count = x.shape[0], len(weights)
    hidden = weights[0][1].shape[0] * weights[0][1].shape[2]
    ins, outs = [whole(rows, D)] * 2, []
    for pair in weights:
        for w in pair:
            taken, height, steps = tiling(w.shape[0], w.shape[2])
            at = (lambda i: (0, 0, i, 0)) if w.shape[0] == 1 else (lambda i: (i, 0, 0, 0))
            ins.append(pl.BlockSpec((taken, w.shape[1], height, D), at))
        outs.append(pl.BlockSpec((3, taken * height, rows), lambda i: (0, i, 0)))
    return pl.pallas_call(
        gate_kernel,
        grid=(steps,),
        in_specs=ins,
        out_specs=outs,
        out_shape=[jax.ShapeDtypeStruct((3, hidden, rows), bf)] * count,
        compiler_params=pltpu.CompilerParams(vmem_limit_bytes=LIMIT),
        cost_estimate=cost(
            6 * rows * D * hidden * count,
            2 * (2 * rows * D + 3 * count * hidden * (D + rows)),
        ),
        name="ffn_gates",
    )(x, c, *[w for pair in weights for w in pair])


def back_kernel(count, *refs):
    made, weights, out_ref, turned = (
        refs[:count], refs[count : 2 * count], refs[-count - 1], refs[-count:]
    )
    added = refs[2 * count : -count - 1]

    @pl.when(pl.program_id(0) == 0)
    def _():
        for block, kept in zip(made, turned):
            kinds, hidden, rows = block.shape
            kept[...] = block[...].reshape(kinds * hidden, rows).T

    total = None
    for kept, w_ref in zip(turned, weights):
        parts, kinds, rows, columns = w_ref.shape
        right = jnp.concatenate(
            [w_ref[:, k].reshape(parts * rows, columns) for k in range(kinds)], axis=0
        )
        part = mul(kept[...], right)
        total = part if total is None else total + part
    for more in added:
        total = total + more[...].astype(f32)
    out_ref[...] = total.astype(out_ref.dtype)


def ffn_back(made, weights, which, added=(), columns=512):
    count = len(weights)
    weights = [pair[which] for pair in weights]
    kinds = weights[0].shape[1]
    _, hidden, rows = made[0].shape
    out = pl.BlockSpec((rows, columns), lambda j: (0, j))
    ins = [
        pl.BlockSpec(
            (kinds, hidden, rows), lambda j: (2 * which // kinds, 0, 0), pipeline_mode=pl.Buffered(1)
        )
    ] * count
    for w in weights:
        ins.append(pl.BlockSpec((w.shape[0], kinds, w.shape[2], columns), lambda j: (0, 0, 0, j)))
    ins += [out] * len(added)
    return pl.pallas_call(
        functools.partial(back_kernel, count),
        grid=(D // columns,),
        in_specs=ins,
        out_specs=out,
        out_shape=jax.ShapeDtypeStruct((rows, D), bf),
        scratch_shapes=[pltpu.VMEM((rows, kinds * hidden), bf)] * count,
        compiler_params=pltpu.CompilerParams(vmem_limit_bytes=LIMIT),
        cost_estimate=cost(
            2 * rows * D * hidden * kinds * count,
            2 * (count * kinds * hidden * (D + rows) + rows * D),
        ),
        name="ffn_back",
    )(*made, *weights, *added)


def grad_kernel(blocks, *refs):
    made, xs, cs = refs[:blocks], refs[blocks : 2 * blocks], refs[2 * blocks : 3 * blocks]
    added, out_ref = refs[3 * blocks : -1], refs[-1]
    parts, _, rows, _ = out_ref.shape

    def write(rights):
        total = None
        for left, right in zip(made, rights):
            part = mul(left[0], right[...])
            total = part if total is None else total + part
        for more in added:
            total = total + more[...].reshape(parts * rows, D).astype(f32)
        out_ref[...] = total.astype(bf).reshape(parts, 1, rows, D)

    kind = pl.program_id(0)

    @pl.when(kind < 2)
    def _():
        write(xs)

    @pl.when(kind == 2)
    def _():
        write(cs)


def ffn_grad(made, xs, cs, parts, height, added=None):
    blocks = len(made)
    rows = xs[0].shape[0]
    hidden = made[0].shape[1]
    taken, rise, steps = tiling(parts, height)
    left = pl.BlockSpec((1, taken * rise, rows), lambda k, i: (k, i, 0))
    at = (lambda k, i: (0, k, i, 0)) if parts == 1 else (lambda k, i: (i, k, 0, 0))
    out = pl.BlockSpec((taken, 1, rise, D), at)
    more = [] if added is None else [added]
    return pl.pallas_call(
        functools.partial(grad_kernel, blocks),
        grid=(3, steps),
        in_specs=[left] * blocks + [whole(rows, D)] * (2 * blocks) + [out] * len(more),
        out_specs=out,
        out_shape=jax.ShapeDtypeStruct((parts, 3, height, D), bf),
        compiler_params=pltpu.CompilerParams(vmem_limit_bytes=LIMIT),
        cost_estimate=cost(
            6 * rows * D * hidden * blocks,
            2 * (2 * blocks * rows * D + 3 * hidden * (rows * blocks + D * (1 + len(more)))),
        ),
        name="ffn_grad",
    )(*made, *xs, *cs, *more)


def widen_kernel(sum_ref, *out_refs):
    for kind, out_ref in enumerate(out_refs):
        out_ref[...] = sum_ref[0, kind].astype(f32)


def widened(sums):
    parts, _, height, _ = sums.shape
    return pl.pallas_call(
        widen_kernel,
        grid=(parts,),
        in_specs=[pl.BlockSpec((1, 3, height, D), lambda i: (i, 0, 0, 0))],
        out_specs=[pl.BlockSpec((height, D), lambda i: (i, 0))] * 3,
        out_shape=[jax.ShapeDtypeStruct((parts * height, D), f32)] * 3,
        compiler_params=pltpu.CompilerParams(vmem_limit_bytes=LIMIT),
        cost_estimate=cost(0, 6 * parts * 3 * height * D),
        name="widened",
    )(sums)


def qkv_grad_kernel(n_ref, gq_ref, gk_ref, gv_ref, out_ref):
    turned = n_ref[...].T
    qk = gq_ref.shape[1]
    out_ref[:, :qk] = mul(turned, gq_ref[...]).astype(bf)
    out_ref[:, qk : 2 * qk] = mul(turned, gk_ref[...]).astype(bf)
    out_ref[:, 2 * qk :] = mul(turned, gv_ref[...]).astype(bf)


def qkv_grad(normed, gq, gk, gv):
    rows, qk = gq.shape
    columns = 2 * qk + D
    tile = 256
    return pl.pallas_call(
        qkv_grad_kernel,
        grid=(D // tile,),
        in_specs=[
            pl.BlockSpec((rows, tile), lambda i: (0, i)), whole(rows, qk), whole(rows, qk), whole(rows, D)
        ],
        out_specs=pl.BlockSpec((tile, columns), lambda i: (i, 0)),
        out_shape=jax.ShapeDtypeStruct((D, columns), bf),
        compiler_params=pltpu.CompilerParams(vmem_limit_bytes=LIMIT),
        cost_estimate=cost(2 * rows * D * columns, 2 * (rows * (D + columns) + D * columns)),
        name="qkv_grad",
    )(normed, gq, gk, gv)


def norm_forward(inputs):
    inverse = lax.rsqrt(jnp.mean(inputs * inputs, axis=-1, keepdims=True) + EPSILON)
    return (inputs * inverse, inverse)


def norm_backward(grad_normed, unit_rows, inverse, gain_vec):
    gain_grad = jnp.sum(grad_normed * unit_rows, axis=0)
    grad_unit = grad_normed * gain_vec
    return (
        inverse * (grad_unit - unit_rows * jnp.mean(grad_unit * unit_rows, axis=-1, keepdims=True)),
        gain_grad,
    )


def move(array, target, axis="mp"):
    size = lax.axis_size(axis)
    pairs = [(m, target(m)) for m in range(size)]
    return lax.ppermute(array, axis, [(m, t) for m, t in pairs if t is not None])


def then(value, *before):
    return lax.optimization_barrier((value, before))[0]


def beside(array, mover, *works):
    ends = [array.shape[0] * n // len(works) // 16 * 16 for n in range(len(works))] + [array.shape[0]]
    moved, made = [], []
    for n, work in enumerate(works):
        share = array[ends[n] : ends[n + 1]]
        if made:
            share = then(share, made[-1])
        result = work(share, made)
        arrived, result = lax.optimization_barrier((mover(share), result))
        moved.append(arrived)
        made.append(result)
    return jnp.concatenate(moved, axis=0), made


def to_mate(array):
    return move(array, lambda m: m ^ 1)


def to_half(array):
    size = lax.axis_size("mp")
    return move(array, lambda m: (m + size // 2) % size)


def to_peer(array, step):
    half = lax.axis_size("mp") // 2

    def target(m):
        low = m % half
        return m - low + (low + 2 * step) % half

    return move(array, target)


def to_chip(array, step):
    size = lax.axis_size("mp")
    return move(array, lambda m: m + 2 * step if 0 <= m + 2 * step < size else None)


def sums_before(own, sign, *beside, made=None):
    core = lax.axis_index("mp") % 2
    chips = lax.axis_size("mp") // 2
    wire = own.astype(bf)
    mate = to_mate(wire).astype(f32)
    half = own.shape[0] // 2
    both = wire.astype(f32) + mate
    running = lax.dynamic_slice_in_dim(both, core * half, half, 0)
    before = jnp.zeros_like(running)
    step, beside, made = 1, list(beside), [] if made is None else made
    while step < chips:
        came = to_chip(running.astype(bf), sign * step)
        if beside:
            came, result = lax.optimization_barrier((came, beside.pop(0)(running)))
            made.append(result)
        came = came.astype(f32)
        before = before + came
        running = running + came
        step *= 2
    before = before.astype(bf)
    other = to_mate(before)
    first = jnp.where(core == 0, before, other)
    second = jnp.where(core == 0, other, before)
    total = jnp.concatenate([first, second], axis=0).astype(f32)
    inner = core == (1 if sign > 0 else 0)
    return (total + jnp.where(inner, mate, 0.0)).astype(bf), made


def pick(array, index, dim=0):
    return lax.dynamic_index_in_dim(array, index, dim, keepdims=False)


def chip_halves(array):
    groups, size = lax.axis_size("dp"), lax.axis_size("mp")
    core = lax.axis_index("mp") % 2
    rows, columns = array.shape[0] // (groups * size), array.shape[1]
    blocks = array.reshape(groups, size // 2, 2, rows, columns)
    return pick(blocks, core, 2), pick(blocks, 1 - core, 2)


def add(first, *more, kept=bf):
    total = first.astype(f32)
    for array in more:
        total = total + array.astype(f32)
    return total.astype(kept)


def placed(shares, places):
    out = jnp.zeros((len(shares),) + shares[0].shape, shares[0].dtype)
    for share, at in zip(shares, places):
        out = lax.dynamic_update_index_in_dim(out, share, at, 0)
    return out


def chip_shares(array):
    steps = range(1, lax.axis_size("mp") // 2)
    return [move(array, lambda m: m ^ (2 * step)) for step in steps]


def by_chip(array, shares):
    chip = lax.axis_index("mp") // 2
    return placed([array] + shares, [chip ^ step for step in range(len(shares) + 1)])


def first_groups(array):
    return [move(array, lambda m: m ^ step, "dp") for step in (1, 2)]


def third_group(first, second):
    half = first.shape[0] // 2
    return [
        move(second[:half], lambda m: m ^ 1, "dp"),
        move(first[half:], lambda m: m ^ 2, "dp"),
    ]


def assembled(pieces, groups, chips, out=None):
    group, core = lax.axis_index("dp"), lax.axis_index("mp") % 2
    shape = pieces[0][2].shape[1:]
    if out is None:
        out = jnp.zeros((groups, chips, 2) + shape, bf)
    for step, at, own, other in pieces:
        both = jnp.where(core == 0, jnp.stack([own, other], 1), jnp.stack([other, own], 1))
        start = (group ^ step, at) + (0,) * (len(shape) + 1)
        out = lax.dynamic_update_slice(out, both[None], start)
    return out


def group_move(array, step):
    return move(pick(array, lax.axis_index("dp") ^ step), lambda m: m ^ step, "dp")


def chip_moves(array):
    chip = lax.axis_index("mp") // 2
    return [
        move(pick(array, chip ^ step), lambda m: m ^ (2 * step))
        for step in range(1, lax.axis_size("mp") // 2)
    ]


def sum_everywhere(array):
    for axis in ("mp", "dp"):
        step = 1
        while step < lax.axis_size(axis):
            array = array + move(array, lambda m: m ^ step, axis)
            step *= 2
    return array


def body(
    x_in,
    seq_lengths,
    norm1_gain,
    w_query,
    w_key,
    w_value,
    w_out,
    norm2_gain,
    w_gate,
    w_up,
    w_down,
    cotangent,
):
    rows = x_in.shape[0]
    groups = lax.axis_size("dp")
    size = lax.axis_size("mp")
    peers = size // 4
    hidden = w_gate.shape[1]
    piece = hidden // groups
    place = lax.axis_index("mp")
    group = lax.axis_index("dp")
    everywhere = ("dp", "mp")
    qk = w_query.shape[1]
    aligned = piece % 16 == 0

    own_rows = w_query.shape[0]
    gain_block = jnp.concatenate(
        [norm1_gain[:, None], norm2_gain[:, None], jnp.zeros((own_rows, 126), bf)], axis=1
    )
    packed = jnp.concatenate([w_query, w_key, w_value, gain_block], axis=1)
    in_chips, packed = lax.optimization_barrier((chip_shares(packed), packed))
    in_chips = by_chip(packed, in_chips)

    full_out = lax.all_gather(w_out, everywhere, axis=0, tiled=True)
    half_chips = size // 4
    mine_both = jnp.concatenate(then([w_gate.T, w_up.T], in_chips), axis=0)
    mine = (mine_both.reshape(1, 2, hidden, D), then(w_down, in_chips).reshape(1, 1, hidden, D))
    far_down = lax.dynamic_slice_in_dim(mine[1][0, 0], group * piece, piece, 0)
    far_both = lax.dynamic_slice_in_dim(mine[0][0], group * piece, piece, 1).reshape(2 * piece, D)
    cot_ends = [rows * n // 16 for n in (0, 6, 10, 13, 16)]
    cot_shares = [cotangent[a:b] for a, b in zip(cot_ends, cot_ends[1:])]

    def peers_of(array):
        return [to_peer(array, step) for step in range(1, peers)]

    def beside_one(array, mover, work):
        return lax.optimization_barrier((mover(array), work(array)))

    both_cut, down_cut = 2 * piece * 8 // 11, piece * 7 // 11
    in_near, in_mate, cot_first, both_first = lax.optimization_barrier(
        (
            first_groups(in_chips),
            to_mate(in_chips),
            peers_of(then(cot_shares[0], in_chips)),
            to_half(then(far_both[:both_cut], in_chips)),
        )
    )
    in_third, in_mates, both_second = lax.optimization_barrier(
        (
            third_group(*in_near),
            [to_mate(share) for share in in_near],
            to_half(then(far_both[both_cut:], in_near)),
        )
    )
    in_mates = [in_mate, *in_mates] + [to_mate(share) for share in in_third]
    far_both = jnp.concatenate([both_first, both_second], axis=0)
    far_both = lax.all_gather(far_both, "dp", axis=0, tiled=True).reshape(groups, 2, piece, D)
    down_first = to_half(then(far_down[:down_cut], in_third))
    mate_down = to_mate(then(mine[1], in_third))
    cot_second = peers_of(then(cot_shares[1], in_third))
    in_pieces = [
        (step, at, own, other)
        for (step, at, own), other in zip(
            (
                (0, 0, in_chips),
                (1, 0, in_near[0]),
                (2, 0, in_near[1]),
                (3, 0, in_third[0]),
                (3, half_chips, in_third[1]),
            ),
            in_mates,
        )
    ]
    full_in = assembled(in_pieces, groups, size // 2).reshape(D, packed.shape[1])

    row_start = place * rows
    seq_ends = jnp.cumsum(seq_lengths[0], dtype=jnp.int32)
    positions = row_start + jnp.arange(rows, dtype=jnp.int32)
    segments = jnp.sum((positions[:, None] >= seq_ends[None, :]).astype(jnp.int32), axis=1)
    seg_before = jnp.sum((row_start - 1 >= seq_ends).astype(jnp.int32))
    reading = ((segments == seg_before) & (row_start > 0)).astype(f32)[:, None]
    last_doc = (segments == segments[-1]).astype(f32)[:, None]
    seg_col = segments[:, None]
    seg_row = jnp.broadcast_to(segments[None, :], (8, rows))
    tables = feature_tables()

    inputs = x_in.astype(f32)
    inverse_one = norm_forward(inputs)[1]
    early = (full_out, mine, down_first, mate_down, cot_second, inverse_one, reading, last_doc, seg_col, seg_row)
    full_in, early = lax.optimization_barrier((full_in, early))
    full_out, mine, down_first, mate_down, cot_second, inverse_one, reading, last_doc, seg_col, seg_row = early
    gain_one = full_in[:, 2 * qk + D].astype(f32)
    gain_two = full_in[:, 2 * qk + D + 1].astype(f32)
    full_qkv = full_in[:, : 2 * qk + D]
    unit_one = inputs * inverse_one
    normed_one = (unit_one * gain_one).astype(bf)
    (got, mate_gate, down_second), qkv = beside_one(
        then(cot_shares[2], full_in),
        lambda ready: (
            peers_of(ready),
            to_mate(then(mine[0][:, :1], ready)),
            to_half(then(far_down[down_cut:], ready)),
        ),
        lambda ready: mul(then(normed_one, ready), full_qkv).astype(bf),
    )
    cot_got = [cot_first, cot_second, got]
    queries, keys, values = qkv[:, :qk], qkv[:, qk : 2 * qk], qkv[:, 2 * qk :]
    far_down = jnp.concatenate([down_first, down_second], axis=0)
    far_down = lax.all_gather(far_down, "dp", axis=0, tiled=True).reshape(groups, 1, piece, D)
    (got, mate_up), own_state = beside_one(
        then(cot_shares[3], qkv),
        lambda ready: (peers_of(ready), to_mate(then(mine[0][:, 1:], ready))),
        lambda ready: mix_state(then(keys, ready), values, tables, last_doc),
    )
    cot_got.append(got)

    def local_work(ready):
        local = mix_local(then(queries, ready), keys, values, seg_col, seg_row)
        return local

    def pack_work(ready):
        gate, up = then((mate_gate, mate_up), ready)
        return jnp.concatenate([gate, up], axis=1)

    prefix, [(num, den), mate_both] = sums_before(own_state, 1, local_work, pack_work)
    attended, inverse_den = mix_prefix(queries, num, den, prefix, tables, reading)
    mate = (mate_both, mate_down)
    near = [mine, mate]
    hidden_in = inputs + mul(attended, full_out)
    unit_two, inverse_two = norm_forward(hidden_in)
    normed_two = (unit_two * gain_two).astype(bf)
    came = [to_peer(normed_two, step) for step in range(1, peers)]

    near_own = ffn_gates(normed_two, cotangent, near)
    far_mine = then((far_both, far_down), normed_two)
    if not aligned:
        far_mine = tuple(jnp.swapaxes(w, 0, 1).reshape(1, -1, hidden, D) for w in far_mine)
    far_mate = then(tuple(to_mate(w) for w in far_mine), near_own)
    far = [tuple(far_mine), far_mate]
    weights = near + far
    shape = (groups, piece) if aligned else (1, hidden)
    far_own = ffn_gates(normed_two, cotangent, far)
    made_own = list(near_own) + list(far_own)
    grad_own = ffn_back(made_own, weights, 0)
    out_own = ffn_back(then(made_own, grad_own), weights, 1)
    normed = [normed_two] + then(came, out_own)
    cot_got = then(cot_got, near_own)
    cots = [cotangent] + [jnp.concatenate(parts, axis=0) for parts in zip(*cot_got)]
    near_made = [near_own] + [ffn_gates(x, c, near) for x, c in zip(normed[1:], cots[1:])]
    far_made = [far_own] + [
        ffn_gates(x, c, then(far, near_made)) for x, c in zip(normed[1:], cots[1:])
    ]
    made = [list(a) + list(b) for a, b in zip(near_made, far_made)]

    def weight_grads(made, ready, added=None):
        return ffn_grad(then(made, ready), normed, cots, *shape, added)

    def over_groups(grad):
        if not aligned:
            grad = jnp.swapaxes(grad.reshape(3, groups, piece, D), 0, 1)
        return lax.psum_scatter(
            grad.reshape(groups * 3 * piece, D), "dp", scatter_dimension=0, tiled=True
        )

    def back(block, which, ready):
        return ffn_back(then(block, ready), weights, which)

    far_given = weight_grads([block[1] for block in far_made], far_made)
    far_sent = to_mate(far_given)
    grad_parts = [back(block, 0, far_given) for block in made[1:]]

    def owners(parts):
        return [to_peer(part, peers - step) for step, part in enumerate(parts, 1)]

    def stacked(parts):
        return jnp.concatenate([part[:, None] for part in parts], axis=1)

    def to_owners(parts):
        return stacked(owners([parts[:, n] for n in range(peers - 1)]))

    def near_work(ready, _):
        given = weight_grads([block[1] for block in near_made], ready)
        return given

    def far_work(ready, done):
        kept = weight_grads([block[0] for block in far_made], ready, far_sent)
        return kept, to_mate(then(done[0], ready))

    def last_work(ready, done):
        return weight_grads([block[0] for block in near_made], ready, done[1][1])

    grad_sent, (_, (far_kept, _), near_kept) = beside(
        stacked(grad_parts), to_owners, near_work, far_work, last_work
    )
    far_part = over_groups(far_kept)
    near_part = over_groups(near_kept)
    grad_normed_two = jnp.sum(grad_sent.astype(f32), axis=1) + grad_own.astype(f32)

    grad_two, gain_two_grad = norm_backward(grad_normed_two, unit_two, inverse_two, gain_two)
    grad_hidden_in = cotangent.astype(f32) + grad_two
    grad_branch = grad_hidden_in.astype(bf)
    grad_attended = mul(grad_branch, full_out, "nt").astype(bf)
    state_grad = mix_state_grad(queries, grad_attended, attended, inverse_den, tables, reading)

    def local_grads(ready):
        local = mix_local_grad(
            then(queries, ready), keys, values, grad_attended, attended, inverse_den, prefix, tables,
            reading, seg_col, seg_row,
        )
        return local, to_mate(then(out_halves[1], ready))

    out_halves = []

    def out_work(ready):
        halves = chip_halves(mul(then(attended, ready), grad_branch, "tn").astype(bf))
        out_halves.extend(halves)
        return halves

    later, [_, (local, out_came)] = sums_before(state_grad, -1, out_work, local_grads)
    grad_queries, part_keys, part_values = local
    out_kept = add(out_halves[0], out_came)
    out_kept, far_part = then((out_kept, far_part), later)
    ends = [far_part.shape[0] * n // 33 for n in (0, 3, 7, 12, 33)]
    far_shares = [far_part[a:b] for a, b in zip(ends, ends[1:])]
    out_first, out_second, out_diag = [pick(out_kept, group ^ step) for step in range(1, groups)]
    low, high = slice(None, half_chips), slice(half_chips, None)

    def by_first(block):
        return move(block, lambda m: m ^ 1, "dp")

    def by_second(block):
        return move(block, lambda m: m ^ 2, "dp")

    (far_first, for_second, for_first), (grad_keys, grad_values) = beside_one(
        then(far_shares[0], out_kept),
        lambda ready: (
            to_half(ready), by_first(then(out_diag[low], ready)), by_second(then(out_diag[high], ready))
        ),
        lambda ready: mix_later_grad(
            then(keys, ready), values, part_keys, part_values, later, tables, last_doc
        ),
    )
    out_second = [add(out_second[low], for_second), out_second[high]]
    out_first = [out_first[low], add(out_first[high], for_first)]
    (far_second, out_low), in_grad = beside_one(
        then(far_shares[1], grad_keys),
        lambda ready: (
            to_half(ready), [by_first(then(out_first[0], ready)), by_second(then(out_second[0], ready))]
        ),
        lambda ready: qkv_grad(then(normed_one, ready), grad_queries, grad_keys, grad_values),
    )
    in_keep, in_give = chip_halves(in_grad)
    in_came = to_mate(in_give)
    far_third = to_half(then(far_shares[2], in_grad))
    out_high = [by_first(then(out_first[1], in_grad)), by_second(then(out_second[1], in_grad))]
    far_third, in_came, out_high = lax.optimization_barrier((far_third, in_came, out_high))
    in_shares = [
        add(pick(in_keep, group ^ step), pick(in_came, group ^ step)) for step in range(1, groups)
    ]
    out_parts = [back(block, 1, in_shares) for block in made[1:]]
    in_moved = [
        move(share, lambda m: m ^ step, "dp") for step, share in enumerate(in_shares, 1)
    ]
    far_last = to_half(then(far_shares[3], in_came))
    grad_queries, grad_keys, grad_values = then(
        (grad_queries, grad_keys, grad_values), in_shares
    )
    grad_normed_one = (
        mul(grad_queries, full_qkv[:, :qk], "nt")
        + mul(grad_keys, full_qkv[:, qk : 2 * qk], "nt")
        + mul(grad_values, full_qkv[:, 2 * qk :], "nt")
    )
    grad_one, gain_one_grad = norm_backward(grad_normed_one, unit_one, inverse_one, gain_one)
    input_grad = (grad_hidden_in + grad_one).astype(bf)
    out_parts, input_grad, gain_one_grad, in_moved, far_last = lax.optimization_barrier(
        (out_parts, input_grad, gain_one_grad, in_moved, far_last)
    )
    far_sum = jnp.concatenate([far_first, far_second, far_third, far_last], axis=0)
    ffn_sum = lax.all_gather(add(near_part, far_sum), "dp", axis=0, tiled=True)
    ffn_sum = ffn_sum.reshape(groups, 3, piece, D)
    out_sent = to_owners(stacked(out_parts))
    output = (hidden_in + jnp.sum(out_sent.astype(f32), axis=1) + out_own.astype(f32)).astype(bf)
    chip = place // 2

    def over_chips(blocks, kept):
        shares = [
            add(*[pick(block, chip ^ step) for block in blocks]) for step in range(1, size // 2)
        ]
        moved = [move(share, lambda m: m ^ (2 * step)) for step, share in enumerate(shares, 1)]
        return add(*[pick(block, chip) for block in blocks], *moved, kept=kept)

    in_sum = over_chips([pick(in_keep, group), pick(in_came, group), *in_moved], f32)
    out_blocks = [jnp.concatenate(pair, axis=0) for pair in zip(out_low, out_high)]
    out_blocks = then([pick(out_kept, group), *out_blocks], in_moved)
    out_sum = over_chips(out_blocks, f32)
    if not aligned:
        ffn_sum = jnp.swapaxes(ffn_sum, 0, 1).reshape(1, 3, hidden, D)
    gate_grad, up_grad, down_grad = widened(ffn_sum)
    gain_sums = sum_everywhere(jnp.stack([gain_one_grad, gain_two_grad]))
    gain_sums = lax.dynamic_slice_in_dim(
        gain_sums, (group * size + place) * own_rows, own_rows, 1
    )
    return (
        output,
        input_grad,
        gain_sums[0],
        in_sum[:, :qk],
        in_sum[:, qk : 2 * qk],
        in_sum[:, 2 * qk :],
        out_sum,
        gain_sums[1],
        gate_grad.T,
        up_grad.T,
        down_grad,
    )


def solution(mesh):
    rows, vector = P(("dp", "mp"), None), P(("dp", "mp"))
    columns, down = P(None, "mp"), P("mp", None)
    return jax.shard_map(
        body,
        mesh=mesh,
        in_specs=(rows, P("dp", None), vector, rows, rows, rows, rows, vector, columns, columns, down, rows),
        out_specs=(rows, rows, vector, rows, rows, rows, rows, vector, columns, columns, down),
        check_vma=False,
    )
```

time: 2080 us -> 889 us (0.43)
  waiting for transfers between devices: 1300 us -> 259 us
  matrix products: 451 us -> 57.8 us
  Pallas kernels: 0 us -> 234 us
  blocking collectives: 127 us -> 0 us
  starting transfers between devices: 0.78 us -> 94.6 us
  local copies, waits for them, and re-layouts: 58.5 us -> 133 us
    reduce_scatter x6 -> x2, waiting for transfers between devices: 888 us -> 0.02 us  [over_groups(): lax.psum_scatter(grad.reshape(groups * 3 * piece, D), 'dp', scatter_dimen...]
    all_gather x8 -> x4, waiting for transfers between devices: 406 us -> 0.03 us  [the longest x1 0.02 us: body(): full_out = lax.all_gather(w_out, everywhere, axis=0, tiled=True)]
    dot_general x35 -> x7, matrix products: 451 us -> 57.8 us  [mul(): lax.dot_general(left, right, (dims, ((), ())), preferred_element_type=jnp...]
    ppermute x0 -> x66, waiting for transfers between devices: none -> 258 us  [move(): lax.ppermute(array, axis, [(m, t) for m, t in pairs if t is not None])]
    pallas_call x0 -> x20, Pallas kernels: none -> 234 us  [the longest x4 57.3 us: ffn_back(): pl.pallas_call(functools.partial(back_kernel, count), grid=(D // columns,...]
    unnamed x3 -> x0, blocking collectives: 98 us -> none
    ppermute x0 -> x66, starting transfers between devices: none -> 94 us  [move(): lax.ppermute(array, axis, [(m, t) for m, t in pairs if t is not None])]
    unnamed x137 -> x298, local copies, waits for them, and re-layouts: 18.5 us -> 84.5 us
  transfers between devices with their start and end apart: 15 -> 72, of which waited for: 13 -> 28; matrix products, arithmetic and copies ran while one was open for 23% -> 22% of each run, Pallas kernels for 0% -> 21%
where the time goes in v1:
time: 889 us; the launch traced here: 883 us
  waiting for transfers between devices  259 us (29%)
  Pallas kernels  234 us (26%)
  local copies, waits for them, and re-layouts  133 us (15%)
  starting transfers between devices  94.6 us (11%)
  other arithmetic  88.7 us (10%)
  matrix products  57.8 us (7%)
  between operations  15.9 us (2%)
    ppermute x66, waiting for transfers between devices, move(): lax.ppermute(array, axis, [(m, t) for m, t in pairs if t is not None])  258 us
    ppermute x66, starting transfers between devices, move(): lax.ppermute(array, axis, [(m, t) for m, t in pairs if t is not None])  94 us
    unnamed x298, local copies, waits for them, and re-layouts  84.5 us
    dot_general x7, matrix products, mul(): lax.dot_general(left, right, (dims, ((), ())), preferred_element_type=jnp...  57.8 us
    pallas_call x4, Pallas kernels, ffn_back(): pl.pallas_call(functools.partial(back_kernel, count), grid=(D // columns,...  57.3 us
    pallas_call x4, Pallas kernels, ffn_gates(): pl.pallas_call(gate_kernel, grid=(steps,), in_specs=ins, out_specs=outs,...  54.9 us
    pallas_call x4, Pallas kernels, ffn_grad(): pl.pallas_call(functools.partial(grad_kernel, blocks), grid=(3, steps), i...  54.4 us
    convert_element_type x6, other arithmetic, add(): return total.astype(kept)  22.7 us
  transfers between devices with their start and end apart: 72, of which 28 were waited for; matrix products, arithmetic and copies ran while one was open for 22% of the time, Pallas kernels for 21%

profile of v1, /device:TPU:0, one launch (start us, length us, event | category | flops | bytes accessed | tf_op | source)
XLA Modules:
  0.0 882.6 jit_solution(15372392608747955149)
XLA Ops:
  16.3 13.3 %collective-permute-done = bf16[64,2688]{1,0:T(8,128)(2,1)S(1)} collective-permute-done((bf16[64,2688]{1,0:T(8,128)(2,1)S(1)}, bf16[64,2688]{1,0:T(8,128)(2,1)S(1)}, u32[]{:S(2)}, u32[]{:S(2)}) %collective-permute-start) | collective-permute-done | bytes 344096 | tf_op jit(solution)/shard_map/ppermute | solution.py:570
  29.6 13.8 %collective-permute-done.1 = bf16[64,2688]{1,0:T(8,128)(2,1)S(1)} collective-permute-done((bf16[64,2688]{1,0:T(8,128)(2,1)S(1)}, bf16[64,2688]{1,0:T(8,128)(2,1)S(1)}, u32[]{:S(2)}, u32[]{:S(2)}) %collective-permute-start.1) | collective-permute-done | bytes 344096 | tf_op jit(solution)/shard_map/ppermute | solution.py:570
  51.3 10.2 %collective-permute-start.7 = (bf16[256,2048]{1,0:T(8,128)(2,1)}, bf16[256,2048]{1,0:T(8,128)(2,1)}, u32[]{:S(2)}, u32[]{:S(2)}) collective-permute-start(bf16[256,2048]{1,0:T(8,128)(2,1)} %slice.190), channel_id=1, source_target_pairs={{0,4},{1,5},{2,6},{3,7},{4,0},{5,1},{6,2},{7,3},{8,12},{9,13},{10,... | collective-permute-start | bytes 3145736 | tf_op jit(solution)/shard_map/ppermute | solution.py:570
  65.6 49.0 %collective-permute-done.6 = bf16[192,2048]{1,0:T(8,128)(2,1)} collective-permute-done((bf16[192,2048]{1,0:T(8,128)(2,1)}, bf16[192,2048]{1,0:T(8,128)(2,1)}, u32[]{:S(2)}, u32[]{:S(2)}) %collective-permute-start.6) | collective-permute-done | bytes 786464 | tf_op jit(solution)/shard_map/ppermute | solution.py:570
  114.6 23.2 %collective-permute-done.7 = bf16[256,2048]{1,0:T(8,128)(2,1)} collective-permute-done((bf16[256,2048]{1,0:T(8,128)(2,1)}, bf16[256,2048]{1,0:T(8,128)(2,1)}, u32[]{:S(2)}, u32[]{:S(2)}) %collective-permute-start.7) | collective-permute-done | bytes 1048608 | tf_op jit(solution)/shard_map/ppermute | solution.py:570
  147.4 17.6 %collective-permute-done.12 = bf16[96,2048]{1,0:T(8,128)(2,1)S(1)} collective-permute-done((bf16[96,2048]{1,0:T(8,128)(2,1)S(1)}, bf16[96,2048]{1,0:T(8,128)(2,1)S(1)}, u32[]{:S(2)}, u32[]{:S(2)}) %collective-permute-start.12) | collective-permute-done | bytes 393248 | tf_op jit(solution)/shard_map/ppermute | solution.py:570
  306.7 13.3 %ffn_gates.4 = (bf16[3,704,512]{2,1,0:T(8,128)(2,1)S(1)}, bf16[3,704,512]{2,1,0:T(8,128)(2,1)S(1)}) custom-call(bf16[512,2048]{1,0:T(8,128)(2,1)S(1)} %copy-done.67, bf16[512,2048]{1,0:T(8,128)(2,1)S(1)} %copy-done.25, bf16[1,2,704,2048]{3,2,1,0:T(8,128)(2,1)} %bitcast.187, bf16[1,1,704,2048]{3,2,1,0:T(8,128)(2,1)S(1)} %bitcast.196, ...), custom_call_target="tpu_custom_call" | custom-call | flops 8858370048 | bytes 25821184 | tf_op jit(solution)/shard_map/ffn_gates/pallas_call | solution.py:389
  331.4 13.1 %ffn_gates.5 = (bf16[3,704,512]{2,1,0:T(8,128)(2,1)S(1)}, bf16[3,704,512]{2,1,0:T(8,128)(2,1)S(1)}) custom-call(bf16[512,2048]{1,0:T(8,128)(2,1)S(1)} %copy-done.68, bf16[512,2048]{1,0:T(8,128)(2,1)S(1)} %copy-done.26, bf16[4,2,176,2048]{3,2,1,0:T(8,128)(2,1)} %bitcast.239, bf16[4,1,176,2048]{3,2,1,0:T(8,128)(2,1)S(1)} %bitcast.203, ...), custom_call_target="tpu_custom_call" | custom-call | flops 8858370048 | bytes 25821184 | tf_op jit(solution)/shard_map/ffn_gates/pallas_call | solution.py:389
  351.9 18.1 %ffn_back.4 = bf16[512,2048]{1,0:T(8,128)(2,1)S(1)} custom-call(bf16[3,704,512]{2,1,0:T(8,128)(2,1)S(1)} %get-tuple-element.283.refs_0_, bf16[3,704,512]{2,1,0:T(8,128)(2,1)S(1)} %copy-done.56, bf16[3,704,512]{2,1,0:T(8,128)(2,1)S(1)} %copy-done.60, bf16[3,704,512]{2,1,0:T(8,128)(2,1)S(1)} %copy-done.64, bf16[1,2,704,2048]{3,2,1,0:T(8,128)(2,1)S(1)} %bitcast.191, ...), custom_call_target="tpu_custom_call" | custom-call | flops 11811160064 | bytes 30932992 | tf_op jit(solution)/shard_map/ffn_back/pallas_call | solution.py:443
  374.9 10.6 %ffn_back.5 = bf16[512,2048]{1,0:T(8,128)(2,1)S(1)} custom-call(bf16[3,704,512]{2,1,0:T(8,128)(2,1)S(1)} %get-tuple-element.283.refs_0_, bf16[3,704,512]{2,1,0:T(8,128)(2,1)S(1)} %copy-done.57, bf16[3,704,512]{2,1,0:T(8,128)(2,1)S(1)} %copy-done.61, bf16[3,704,512]{2,1,0:T(8,128)(2,1)S(1)} %copy-done.65, bf16[1,1,704,2048]{3,2,1,0:T(8,128)(2,1)S(1)} %bitcast.197, ...), custom_call_target="tpu_custom_call" | custom-call | flops 5905580032 | bytes 16515072 | tf_op jit(solution)/shard_map/ffn_back/pallas_call | solution.py:443
  388.6 14.4 %ffn_gates.6 = (bf16[3,704,512]{2,1,0:T(8,128)(2,1)S(1)}, bf16[3,704,512]{2,1,0:T(8,128)(2,1)S(1)}) custom-call(bf16[512,2048]{1,0:T(8,128)(2,1)} %collective-permute-done.27.x_ref.refs_3_, bf16[512,2048]{1,0:T(8,128)(2,1)S(1)} %copy-done.81, bf16[1,2,704,2048]{3,2,1,0:T(8,128)(2,1)} %bitcast.188, bf16[1,1,704,2048]{3,2,1,0:T(8,128)(2,1)S(1)} %bitcast.198, ...), custom_call_target="tpu_custom_call" | custom-call | flops 8858370048 | bytes 25821184 | tf_op jit(solution)/shard_map/ffn_gates/pallas_call | solution.py:389
  404.4 14.2 %ffn_gates.7 = (bf16[3,704,512]{2,1,0:T(8,128)(2,1)S(1)}, bf16[3,704,512]{2,1,0:T(8,128)(2,1)S(1)}) custom-call(bf16[512,2048]{1,0:T(8,128)(2,1)} %collective-permute-done.27.x_ref.refs_3_, bf16[512,2048]{1,0:T(8,128)(2,1)S(1)} %copy-done.81, bf16[4,2,176,2048]{3,2,1,0:T(8,128)(2,1)} %bitcast.241, bf16[4,1,176,2048]{3,2,1,0:T(8,128)(2,1)S(1)} %bitcast.204, ...), custom_call_target="tpu_custom_call" | custom-call | flops 8858370048 | bytes 25821184 | tf_op jit(solution)/shard_map/ffn_gates/pallas_call | solution.py:389
  426.2 13.0 %ffn_grad.4 = bf16[4,3,176,2048]{3,2,1,0:T(8,128)(2,1)} custom-call(bf16[3,704,512]{2,1,0:T(8,128)(2,1)S(1)} %copy-done.66, bf16[3,704,512]{2,1,0:T(8,128)(2,1)S(1)} %copy-done.51, bf16[512,2048]{1,0:T(8,128)(2,1)S(1)} %copy-done.69, bf16[512,2048]{1,0:T(8,128)(2,1)} %collective-permute-done.27.x_ref.refs_3_, bf16[512,2048]{1,0:T(8,128)(2,1)S(1)} %copy-done.26, ...), custom_call_target="tpu_custom_call" | custom-call | flops 8858370048 | bytes 21364736 | tf_op jit(solution)/shard_map/ffn_grad/pallas_call | solution.py:493
  440.9 18.3 %ffn_back.6 = bf16[512,2048]{1,0:T(8,128)(2,1)S(1)} custom-call(bf16[3,704,512]{2,1,0:T(8,128)(2,1)S(1)} %get-tuple-element.320.refs_0_.refs_1_, bf16[3,704,512]{2,1,0:T(8,128)(2,1)S(1)} %copy-done.44, bf16[3,704,512]{2,1,0:T(8,128)(2,1)S(1)} %copy-done.47, bf16[3,704,512]{2,1,0:T(8,128)(2,1)S(1)} %copy-done.51, bf16[1,2,704,2048]{3,2,1,0:T(8,128)(2,1)S(1)} %bitcast.194, ...), custom_call_target="tpu_custom_call" | custom-call | flops 11811160064 | bytes 30932992 | tf_op jit(solution)/shard_map/ffn_back/pallas_call | solution.py:443
  462.6 13.0 %ffn_grad.5 = bf16[4,3,176,2048]{3,2,1,0:T(8,128)(2,1)} custom-call(bf16[3,704,512]{2,1,0:T(8,128)(2,1)S(1)} %copy-done.58, bf16[3,704,512]{2,1,0:T(8,128)(2,1)S(1)} %copy-done.44, bf16[512,2048]{1,0:T(8,128)(2,1)S(1)} %copy-done.70, bf16[512,2048]{1,0:T(8,128)(2,1)} %collective-permute-done.27.x_ref.refs_3_, bf16[512,2048]{1,0:T(8,128)(2,1)S(1)} %copy-done.26, ...), custom_call_target="tpu_custom_call" | custom-call | flops 8858370048 | bytes 21364736 | tf_op jit(solution)/shard_map/ffn_grad/pallas_call | solution.py:493
  478.8 13.8 %ffn_grad.6 = bf16[4,3,176,2048]{3,2,1,0:T(8,128)(2,1)} custom-call(bf16[3,704,512]{2,1,0:T(8,128)(2,1)S(1)} %copy-done.62, bf16[3,704,512]{2,1,0:T(8,128)(2,1)S(1)} %copy-done.48, bf16[512,2048]{1,0:T(8,128)(2,1)S(1)} %copy-done.70, bf16[512,2048]{1,0:T(8,128)(2,1)} %collective-permute-done.27.x_ref.refs_3_, bf16[512,2048]{1,0:T(8,128)(2,1)S(1)} %copy-done.26, ...), custom_call_target="tpu_custom_call" | custom-call | flops 8858370048 | bytes 30015488 | tf_op jit(solution)/shard_map/ffn_grad/pallas_call | solution.py:493
  505.9 14.6 %ffn_grad.7 = bf16[4,3,176,2048]{3,2,1,0:T(8,128)(2,1)} custom-call(bf16[3,704,512]{2,1,0:T(8,128)(2,1)S(1)} %copy-done.54, bf16[3,704,512]{2,1,0:T(8,128)(2,1)S(1)} %copy-done.41, bf16[512,2048]{1,0:T(8,128)(2,1)S(1)} %copy-done.71, bf16[512,2048]{1,0:T(8,128)(2,1)} %collective-permute-done.27.x_ref.refs_3_, bf16[512,2048]{1,0:T(8,128)(2,1)S(1)} %copy-done.27, ...), custom_call_target="tpu_custom_call" | custom-call | flops 8858370048 | bytes 30015488 | tf_op jit(solution)/shard_map/ffn_grad/pallas_call | solution.py:493
  573.9 18.2 %mix_local_grad.1 = (bf16[512,256]{1,0:T(8,128)(2,1)S(1)}, f32[512,256]{1,0:T(8,128)S(1)}, f32[512,2048]{1,0:T(8,128)S(1)}) custom-call(bf16[512,256]{1,0:T(8,128)(2,1)S(1)} %get-tuple-element.289.q_ref, bf16[512,256]{1,0:T(8,128)(2,1)S(1)} %get-tuple-element.301.k_ref, bf16[512,2048]{1,0:T(8,128)(2,1)S(1)} %slice.161.v_ref, ...), custom_call_target="tpu_custom_call" | custom-call | flops 1048576 | bytes 65536 | tf_op jit(solution)/shard_map/mix_local_grad/pallas_call | solution.py:319
  675.5 13.9 %collective-permute-done.46 = bf16[80,2048]{1,0:T(8,128)(2,1)} collective-permute-done((bf16[80,2048]{1,0:T(8,128)(2,1)}, bf16[80,2048]{1,0:T(8,128)(2,1)}, u32[]{:S(2)}, u32[]{:S(2)}) %collective-permute-start.46) | collective-permute-done | bytes 327712 | tf_op jit(solution)/shard_map/ppermute | solution.py:570
  713.1 14.2 %fusion.17 = (f32[2048]{0:T(1024)S(1)}, f32[512]{0:T(512)S(1)}, f32[512,2048]{1,0:T(8,128)}) fusion(bf16[512,2048]{1,0:T(8,128)(2,1)} %param.14, f32[512]{0:T(512)S(1)} %copy-done.141, f32[2048]{0:T(1024)S(1)} %copy-done.135, bf16[512,2048]{1,0:T(8,128)(2,1)} %copy-done.89, bf16[2048,2688]{1,0:T(8,128)(2,1)} %bitcast.214, f32[512,2048]{1,0:T(8,128)} %fusion.30, ...), kind=kOutput, calls=%fused_computation.23 | convolution fusion | flops 4304401920 | bytes 25186304 | tf_op jit(solution)/shard_map/dot_general | solution.py:39
  727.4 10.3 %ffn_back.7 = bf16[512,2048]{1,0:T(8,128)(2,1)S(1)} custom-call(bf16[3,704,512]{2,1,0:T(8,128)(2,1)S(1)} %copy-done.42, bf16[3,704,512]{2,1,0:T(8,128)(2,1)S(1)} %copy-done.45, bf16[3,704,512]{2,1,0:T(8,128)(2,1)S(1)} %copy-done.49, bf16[3,704,512]{2,1,0:T(8,128)(2,1)S(1)} %copy-done.52, bf16[1,1,704,2048]{3,2,1,0:T(8,128)(2,1)S(1)} %bitcast.199, ...), custom_call_target="tpu_custom_call" | custom-call | flops 5905580032 | bytes 16515072 | tf_op jit(solution)/shard_map/ffn_back/pallas_call | solution.py:443
  740.1 20.7 %collective-permute-done.51 = bf16[4,64,2560]{2,1,0:T(8,128)(2,1)} collective-permute-done((bf16[4,64,2560]{2,1,0:T(8,128)(2,1)}, bf16[4,64,2560]{2,1,0:T(8,128)(2,1)}, u32[]{:S(2)}, u32[]{:S(2)}) %collective-permute-start.51) | collective-permute-done | bytes 1310752 | tf_op jit(solution)/shard_map/ppermute | solution.py:570
  793.4 43.1 %collective-permute-done.65 = bf16[64,2048]{1,0:T(8,128)(2,1)S(1)} collective-permute-done((bf16[64,2048]{1,0:T(8,128)(2,1)S(1)}, bf16[64,2048]{1,0:T(8,128)(2,1)S(1)}, u32[]{:S(2)}, u32[]{:S(2)}) %collective-permute-start.65) | collective-permute-done | bytes 262176 | tf_op jit(solution)/shard_map/ppermute | solution.py:570
  842.8 12.4 %collective-permute-done.63 = bf16[64,2048]{1,0:T(8,128)(2,1)S(1)} collective-permute-done((bf16[64,2048]{1,0:T(8,128)(2,1)S(1)}, bf16[64,2048]{1,0:T(8,128)(2,1)S(1)}, u32[]{:S(2)}, u32[]{:S(2)}) %collective-permute-start.63) | collective-permute-done | bytes 262176 | tf_op jit(solution)/shard_map/ppermute | solution.py:570
  (549 shorter events, 450.5 us)
Async XLA Ops:
  7.2 188.9 %all-gather.5.cloned.1.call-start = ((), (), s32[]{:S(2)}) async-start(), calls=%async_computation.2 | async-start | bytes 8650752 | tf_op jit(solution)/shard_map/all_gather | solution.py:758
  7.9 286.6 %all-gather.7.cloned.1.call-start = ((), (), s32[]{:S(2)}) async-start(), calls=%async_computation.3 | async-start | bytes 7208960 | tf_op jit(solution)/shard_map/all_gather | solution.py:791
  43.7 94.1 %collective-permute-start.3 = (bf16[4,64,2688]{2,1,0:T(8,128)(2,1)S(1)}, bf16[4,64,2688]{2,1,0:T(8,128)(2,1)}, u32[]{:S(2)}, u32[]{:S(2)}) collective-permute-start(bf16[4,64,2688]{2,1,0:T(8,128)(2,1)S(1)} %bitcast_dynamic-update-slice_fusion), channel_id=1, source_target_pairs={{0,8},{8,0},{16,24},{24,16},{1,9},{9,1},{17,25},{25,17},{2,10},{10... | collective-permute-start | bytes 4128776 | tf_op jit(solution)/shard_map/ppermute | solution.py:570
  45.2 92.6 %collective-permute-start.4 = (bf16[4,64,2688]{2,1,0:T(8,128)(2,1)S(1)}, bf16[4,64,2688]{2,1,0:T(8,128)(2,1)}, u32[]{:S(2)}, u32[]{:S(2)}) collective-permute-start(bf16[4,64,2688]{2,1,0:T(8,128)(2,1)S(1)} %bitcast_dynamic-update-slice_fusion), channel_id=1, source_target_pairs={{0,16},{8,24},{16,0},{24,8},{1,17},{9,25},{17,1},{25,9},{2,18},{10... | collective-permute-start | bytes 4128776 | tf_op jit(solution)/shard_map/ppermute | solution.py:570
  46.7 91.1 %collective-permute-start.5 = (bf16[4,64,2688]{2,1,0:T(8,128)(2,1)S(1)}, bf16[4,64,2688]{2,1,0:T(8,128)(2,1)}, u32[]{:S(2)}, u32[]{:S(2)}) collective-permute-start(bf16[4,64,2688]{2,1,0:T(8,128)(2,1)S(1)} %bitcast_dynamic-update-slice_fusion), channel_id=1, source_target_pairs={{0,1},{1,0},{2,3},{3,2},{4,5},{5,4},{6,7},{7,6},{8,9},{9,8},{10,11... | collective-permute-start | bytes 4128776 | tf_op jit(solution)/shard_map/ppermute | solution.py:570
  51.3 86.5 %collective-permute-start.7 = (bf16[256,2048]{1,0:T(8,128)(2,1)}, bf16[256,2048]{1,0:T(8,128)(2,1)}, u32[]{:S(2)}, u32[]{:S(2)}) collective-permute-start(bf16[256,2048]{1,0:T(8,128)(2,1)} %slice.190), channel_id=1, source_target_pairs={{0,4},{1,5},{2,6},{3,7},{4,0},{5,1},{6,2},{7,3},{8,12},{9,13},{10,... | collective-permute-start | bytes 3145736 | tf_op jit(solution)/shard_map/ppermute | solution.py:570
  62.4 52.2 %collective-permute-start.6 = (bf16[192,2048]{1,0:T(8,128)(2,1)}, bf16[192,2048]{1,0:T(8,128)(2,1)}, u32[]{:S(2)}, u32[]{:S(2)}) collective-permute-start(bf16[192,2048]{1,0:T(8,128)(2,1)} %slice.145), channel_id=1, source_target_pairs={{0,2},{1,3},{2,0},{3,1},{4,6},{5,7},{6,4},{7,5},{8,10},{9,11},{10,... | collective-permute-start | bytes 2359304 | tf_op jit(solution)/shard_map/ppermute | solution.py:570
  171.4 123.1 %all-gather.9.cloned.1.call-start = ((), (), s32[]{:S(2)}) async-start(), calls=%async_computation.4 | async-start | bytes 3604480 | tf_op jit(solution)/shard_map/all_gather | solution.py:843
  243.9 360.0 %reduce-scatter.3.cloned.1.call-start = ((), (), s32[]{:S(2)}) async-start(), calls=%async_computation.5 | async-start | bytes 10813440 | tf_op jit(solution)/shard_map/reduce_scatter | solution.py:895
  294.5 32.9 %collective-permute-start.28 = (bf16[4,2,176,2048]{3,2,1,0:T(8,128)(2,1)}, bf16[4,2,176,2048]{3,2,1,0:T(8,128)(2,1)}, u32[]{:S(2)}, u32[]{:S(2)}) collective-permute-start(bf16[4,2,176,2048]{3,2,1,0:T(8,128)(2,1)} %bitcast.238), channel_id=1, source_target_pairs={{0,1},{1,0},{2,3},{3,2},{4,5},{5,4},{6,7},{7,6},{8,9},{9,8},{10,11... | collective-permute-start | bytes 17301512 | tf_op jit(solution)/shard_map/ppermute | solution.py:570
  294.7 31.2 %collective-permute-start.29 = (bf16[4,1,176,2048]{3,2,1,0:T(8,128)(2,1)}, bf16[4,1,176,2048]{3,2,1,0:T(8,128)(2,1)S(1)}, u32[]{:S(2)}, u32[]{:S(2)}) collective-permute-start(bf16[4,1,176,2048]{3,2,1,0:T(8,128)(2,1)} %bitcast.200), channel_id=1, source_target_pairs={{0,1},{1,0},{2,3},{3,2},{4,5},{5,4},{6,7},{7,6},{8,9},{9,8},{10,11... | collective-permute-start | bytes 8650760 | tf_op jit(solution)/shard_map/ppermute | solution.py:570
  295.0 91.8 %collective-permute-start.27 = (bf16[512,2048]{1,0:T(8,128)(2,1)}, bf16[512,2048]{1,0:T(8,128)(2,1)}, u32[]{:S(2)}, u32[]{:S(2)}) collective-permute-start(bf16[512,2048]{1,0:T(8,128)(2,1)} %multiply_convert_fusion.x_ref.refs_2_), channel_id=1, source_target_pairs={{0,2},{1,3},{2,0},{3,1},{4,6},{5,7},{6,4},{7,5},{8,10},{9,11},{10,... | collective-permute-start | bytes 6291464 | tf_op jit(solution)/shard_map/ppermute | solution.py:570
  439.2 39.5 %collective-permute-start.32 = (bf16[4,3,176,2048]{3,2,1,0:T(8,128)(2,1)}, bf16[4,3,176,2048]{3,2,1,0:T(8,128)(2,1)}, u32[]{:S(2)}, u32[]{:S(2)}) collective-permute-start(bf16[4,3,176,2048]{3,2,1,0:T(8,128)(2,1)} %ffn_grad.4), channel_id=1, source_target_pairs={{0,1},{1,0},{2,3},{3,2},{4,5},{5,4},{6,7},{7,6},{8,9},{9,8},{10,11... | collective-permute-start | bytes 25952264 | tf_op jit(solution)/shard_map/ppermute | solution.py:570
  495.5 267.4 %reduce-scatter.5.cloned.1.call-start = ((), (), s32[]{:S(2)}) async-start(), calls=%async_computation.6 | async-start | bytes 10813440 | tf_op jit(solution)/shard_map/reduce_scatter | solution.py:895
  564.7 301.3 %all-gather.11.cloned.1.call-start = ((), (), s32[]{:S(2)}) async-start(), calls=%async_computation.7 | async-start | bytes 10813440 | tf_op jit(solution)/shard_map/all_gather | solution.py:1013
  696.2 43.9 %collective-permute-start.50 = (bf16[4,64,2560]{2,1,0:T(8,128)(2,1)}, bf16[4,64,2560]{2,1,0:T(8,128)(2,1)}, u32[]{:S(2)}, u32[]{:S(2)}) collective-permute-start(bf16[4,64,2560]{2,1,0:T(8,128)(2,1)} %get-tuple-element.364), channel_id=1, source_target_pairs={{0,8},{8,0},{16,24},{24,16},{1,9},{9,1},{17,25},{25,17},{2,10},{10... | collective-permute-start | bytes 3932168 | tf_op jit(solution)/shard_map/ppermute | solution.py:570
  696.5 64.3 %collective-permute-start.51 = (bf16[4,64,2560]{2,1,0:T(8,128)(2,1)}, bf16[4,64,2560]{2,1,0:T(8,128)(2,1)}, u32[]{:S(2)}, u32[]{:S(2)}) collective-permute-start(bf16[4,64,2560]{2,1,0:T(8,128)(2,1)} %get-tuple-element.363), channel_id=1, source_target_pairs={{0,16},{8,24},{16,0},{24,8},{1,17},{9,25},{17,1},{25,9},{2,18},{10... | collective-permute-start | bytes 3932168 | tf_op jit(solution)/shard_map/ppermute | solution.py:570
  698.6 63.0 %collective-permute-start.52 = (bf16[4,64,2560]{2,1,0:T(8,128)(2,1)}, bf16[4,64,2560]{2,1,0:T(8,128)(2,1)}, u32[]{:S(2)}, u32[]{:S(2)}) collective-permute-start(bf16[4,64,2560]{2,1,0:T(8,128)(2,1)} %get-tuple-element.362), channel_id=1, source_target_pairs={{0,24},{8,16},{16,8},{24,0},{1,25},{9,17},{17,9},{25,1},{2,26},{10... | collective-permute-start | bytes 3932168 | tf_op jit(solution)/shard_map/ppermute | solution.py:570
  700.0 62.8 %collective-permute-start.53 = (bf16[336,2048]{1,0:T(8,128)(2,1)}, bf16[336,2048]{1,0:T(8,128)(2,1)S(1)}, u32[]{:S(2)}, u32[]{:S(2)}) collective-permute-start(bf16[336,2048]{1,0:T(8,128)(2,1)} %slice.184), channel_id=1, source_target_pairs={{0,4},{1,5},{2,6},{3,7},{4,0},{5,1},{6,2},{7,3},{8,12},{9,13},{10,... | collective-permute-start | bytes 4128776 | tf_op jit(solution)/shard_map/ppermute | solution.py:570
  775.6 87.9 %collective-permute-start.54 = (bf16[512,2048]{1,0:T(8,128)(2,1)S(1)}, bf16[512,2048]{1,0:T(8,128)(2,1)S(1)}, u32[]{:S(2)}, u32[]{:S(2)}) collective-permute-start(bf16[512,2048]{1,0:T(8,128)(2,1)S(1)} %copy-done.75), channel_id=1, source_target_pairs={{0,2},{1,3},{2,0},{3,1},{4,6},{5,7},{6,4},{7,5},{8,10},{9,11},{10,... | collective-permute-start | bytes 6291464 | tf_op jit(solution)/shard_map/ppermute | solution.py:570
  782.4 73.8 %collective-permute-start.62 = (bf16[64,2560]{1,0:T(8,128)(2,1)S(1)}, bf16[64,2560]{1,0:T(8,128)(2,1)S(1)}, u32[]{:S(2)}, u32[]{:S(2)}) collective-permute-start(bf16[64,2560]{1,0:T(8,128)(2,1)S(1)} %get-tuple-element.360), channel_id=1, source_target_pairs={{0,6},{1,7},{2,4},{3,5},{4,2},{5,3},{6,0},{7,1},{8,14},{9,15},{10,... | collective-permute-start | bytes 983048 | tf_op jit(solution)/shard_map/ppermute | solution.py:570
  788.4 48.1 %collective-permute-start.65 = (bf16[64,2048]{1,0:T(8,128)(2,1)S(1)}, bf16[64,2048]{1,0:T(8,128)(2,1)S(1)}, u32[]{:S(2)}, u32[]{:S(2)}) collective-permute-start(bf16[64,2048]{1,0:T(8,128)(2,1)S(1)} %get-tuple-element.376), channel_id=1, source_target_pairs={{0,6},{1,7},{2,4},{3,5},{4,2},{5,3},{6,0},{7,1},{8,14},{9,15},{10,... | collective-permute-start | bytes 786440 | tf_op jit(solution)/shard_map/ppermute | solution.py:570
  788.5 53.7 %collective-permute-start.64 = (bf16[64,2048]{1,0:T(8,128)(2,1)S(1)}, bf16[64,2048]{1,0:T(8,128)(2,1)S(1)}, u32[]{:S(2)}, u32[]{:S(2)}) collective-permute-start(bf16[64,2048]{1,0:T(8,128)(2,1)S(1)} %get-tuple-element.377), channel_id=1, source_target_pairs={{0,4},{1,5},{2,6},{3,7},{4,0},{5,1},{6,2},{7,3},{8,12},{9,13},{10,... | collective-permute-start | bytes 786440 | tf_op jit(solution)/shard_map/ppermute | solution.py:570
  790.5 64.6 %collective-permute-start.63 = (bf16[64,2048]{1,0:T(8,128)(2,1)S(1)}, bf16[64,2048]{1,0:T(8,128)(2,1)S(1)}, u32[]{:S(2)}, u32[]{:S(2)}) collective-permute-start(bf16[64,2048]{1,0:T(8,128)(2,1)S(1)} %get-tuple-element.375), channel_id=1, source_target_pairs={{0,2},{1,3},{2,0},{3,1},{4,6},{5,7},{6,4},{7,5},{8,10},{9,11},{10,... | collective-permute-start | bytes 786440 | tf_op jit(solution)/shard_map/ppermute | solution.py:570
  (195 other events, 2431.5 us)
Sparse Core Ops, SparseCore 0:
  11.0 131.0 all-gather.4
  171.5 64.6 all-gather.6
  244.0 40.0 all-gather.8
  495.6 90.8 reduce-scatter.2
  589.5 123.8 reduce-scatter.4
  767.0 91.8 all-gather.10

commit v2 on v1

--- a/solution.py
+++ b/solution.py
@@ -280,7 +280,7 @@
         out_shape=[jax.ShapeDtypeStruct(shapes[kind], kept) for kind, kept in outs],
         scratch_shapes=list(scratch),
         compiler_params=pltpu.CompilerParams(
-            dimension_semantics=("arbitrary",), vmem_limit_bytes=32 * 2**20
+            dimension_semantics=("arbitrary",), vmem_limit_bytes=48 * 2**20
         ),
         cost_estimate=pl.CostEstimate(flops=2**20, bytes_accessed=2**16, transcendentals=0),
         name=name,
@@ -335,7 +335,7 @@
 
 D = 2048
 EPSILON = 1e-05
-LIMIT = 36 * 2**20
+LIMIT = 58 * 2**20
 TILE = 352
 
 
@@ -761,7 +761,7 @@
     mine = (mine_both.reshape(1, 2, hidden, D), then(w_down, in_chips).reshape(1, 1, hidden, D))
     far_down = lax.dynamic_slice_in_dim(mine[1][0, 0], group * piece, piece, 0)
     far_both = lax.dynamic_slice_in_dim(mine[0][0], group * piece, piece, 1).reshape(2 * piece, D)
-    cot_ends = [rows * n // 16 for n in (0, 6, 10, 13, 16)]
+    cot_ends = [rows * n // 16 for n in (0, 3, 6, 10, 13, 16)]
     cot_shares = [cotangent[a:b] for a, b in zip(cot_ends, cot_ends[1:])]
 
     def peers_of(array):
@@ -771,11 +771,10 @@
         return lax.optimization_barrier((mover(array), work(array)))
 
     both_cut, down_cut = 2 * piece * 8 // 11, piece * 7 // 11
-    in_near, in_mate, cot_first, both_first = lax.optimization_barrier(
+    in_near, in_mate, both_first = lax.optimization_barrier(
         (
             first_groups(in_chips),
             to_mate(in_chips),
-            peers_of(then(cot_shares[0], in_chips)),
             to_half(then(far_both[:both_cut], in_chips)),
         )
     )
@@ -791,7 +790,7 @@
     far_both = lax.all_gather(far_both, "dp", axis=0, tiled=True).reshape(groups, 2, piece, D)
     down_first = to_half(then(far_down[:down_cut], in_third))
     mate_down = to_mate(then(mine[1], in_third))
-    cot_second = peers_of(then(cot_shares[1], in_third))
+    cot_third = peers_of(then(cot_shares[2], in_third))
     in_pieces = [
         (step, at, own, other)
         for (step, at, own), other in zip(
@@ -820,16 +819,16 @@
 
     inputs = x_in.astype(f32)
     inverse_one = norm_forward(inputs)[1]
-    early = (full_out, mine, down_first, mate_down, cot_second, inverse_one, reading, last_doc, seg_col, seg_row)
+    early = (full_out, mine, down_first, mate_down, cot_third, inverse_one, reading, last_doc, seg_col, seg_row)
     full_in, early = lax.optimization_barrier((full_in, early))
-    full_out, mine, down_first, mate_down, cot_second, inverse_one, reading, last_doc, seg_col, seg_row = early
+    full_out, mine, down_first, mate_down, cot_third, inverse_one, reading, last_doc, seg_col, seg_row = early
     gain_one = full_in[:, 2 * qk + D].astype(f32)
     gain_two = full_in[:, 2 * qk + D + 1].astype(f32)
     full_qkv = full_in[:, : 2 * qk + D]
     unit_one = inputs * inverse_one
     normed_one = (unit_one * gain_one).astype(bf)
     (got, mate_gate, down_second), qkv = beside_one(
-        then(cot_shares[2], full_in),
+        then(cot_shares[3], full_in),
         lambda ready: (
             peers_of(ready),
             to_mate(then(mine[0][:, :1], ready)),
@@ -837,12 +836,12 @@
         ),
         lambda ready: mul(then(normed_one, ready), full_qkv).astype(bf),
     )
-    cot_got = [cot_first, cot_second, got]
+    cot_got = [cot_third, got]
     queries, keys, values = qkv[:, :qk], qkv[:, qk : 2 * qk], qkv[:, 2 * qk :]
     far_down = jnp.concatenate([down_first, down_second], axis=0)
     far_down = lax.all_gather(far_down, "dp", axis=0, tiled=True).reshape(groups, 1, piece, D)
     (got, mate_up), own_state = beside_one(
-        then(cot_shares[3], qkv),
+        then(cot_shares[4], qkv),
         lambda ready: (peers_of(ready), to_mate(then(mine[0][:, 1:], ready))),
         lambda ready: mix_state(then(keys, ready), values, tables, last_doc),
     )
@@ -857,10 +856,19 @@
         return jnp.concatenate([gate, up], axis=1)
 
     prefix, [(num, den), mate_both] = sums_before(own_state, 1, local_work, pack_work)
-    attended, inverse_den = mix_prefix(queries, num, den, prefix, tables, reading)
+    cot_first, (attended, inverse_den) = beside_one(
+        then(cot_shares[0], prefix),
+        peers_of,
+        lambda ready: mix_prefix(then(queries, ready), num, den, prefix, tables, reading),
+    )
     mate = (mate_both, mate_down)
     near = [mine, mate]
-    hidden_in = inputs + mul(attended, full_out)
+    cot_second, hidden_in = beside_one(
+        then(cot_shares[1], attended),
+        peers_of,
+        lambda ready: inputs + mul(then(attended, ready), full_out),
+    )
+    cot_got = [cot_first, cot_second] + cot_got
     unit_two, inverse_two = norm_forward(hidden_in)
     normed_two = (unit_two * gain_two).astype(bf)
     came = [to_peer(normed_two, step) for step in range(1, peers)]
@@ -876,8 +884,7 @@
     far_own = ffn_gates(normed_two, cotangent, far)
     made_own = list(near_own) + list(far_own)
     grad_own = ffn_back(made_own, weights, 0)
-    out_own = ffn_back(then(made_own, grad_own), weights, 1)
-    normed = [normed_two] + then(came, out_own)
+    normed = [normed_two] + then(came, grad_own)
     cot_got = then(cot_got, near_own)
     cots = [cotangent] + [jnp.concatenate(parts, axis=0) for parts in zip(*cot_got)]
     near_made = [near_own] + [ffn_gates(x, c, near) for x, c in zip(normed[1:], cots[1:])]
@@ -954,7 +961,7 @@
     grad_queries, part_keys, part_values = local
     out_kept = add(out_halves[0], out_came)
     out_kept, far_part = then((out_kept, far_part), later)
-    ends = [far_part.shape[0] * n // 33 for n in (0, 3, 7, 12, 33)]
+    ends = [far_part.shape[0] * n // 33 for n in (0, 3, 9, 16, 22, 33)]
     far_shares = [far_part[a:b] for a, b in zip(ends, ends[1:])]
     out_first, out_second, out_diag = [pick(out_kept, group ^ step) for step in range(1, groups)]
     low, high = slice(None, half_chips), slice(half_chips, None)
@@ -976,44 +983,60 @@
     )
     out_second = [add(out_second[low], for_second), out_second[high]]
     out_first = [out_first[low], add(out_first[high], for_first)]
-    (far_second, out_low), in_grad = beside_one(
-        then(far_shares[1], grad_keys),
+    (out_low, far_slot), in_grad = beside_one(
+        then((out_first[0], out_second[0]), grad_keys),
         lambda ready: (
-            to_half(ready), [by_first(then(out_first[0], ready)), by_second(then(out_second[0], ready))]
+            [by_first(ready[0]), by_second(ready[1])], to_half(then(far_shares[1], ready))
         ),
         lambda ready: qkv_grad(then(normed_one, ready), grad_queries, grad_keys, grad_values),
     )
     in_keep, in_give = chip_halves(in_grad)
-    in_came = to_mate(in_give)
-    far_third = to_half(then(far_shares[2], in_grad))
-    out_high = [by_first(then(out_first[1], in_grad)), by_second(then(out_second[1], in_grad))]
-    far_third, in_came, out_high = lax.optimization_barrier((far_third, in_came, out_high))
-    in_shares = [
-        add(pick(in_keep, group ^ step), pick(in_came, group ^ step)) for step in range(1, groups)
+    in_came, out_high, far_second = lax.optimization_barrier(
+        (
+            to_mate(in_give),
+            [by_first(then(out_first[1], in_grad)), by_second(then(out_second[1], in_grad))],
+            to_half(then(far_shares[2], in_grad)),
+        )
+    )
+    in_diag = add(pick(in_keep, group ^ 3), pick(in_came, group ^ 3))
+    in_first, in_second = [
+        add(pick(in_keep, group ^ step), pick(in_came, group ^ step)) for step in (1, 2)
     ]
-    out_parts = [back(block, 1, in_shares) for block in made[1:]]
-    in_moved = [
-        move(share, lambda m: m ^ step, "dp") for step, share in enumerate(in_shares, 1)
-    ]
-    far_last = to_half(then(far_shares[3], in_came))
     grad_queries, grad_keys, grad_values = then(
-        (grad_queries, grad_keys, grad_values), in_shares
+        (grad_queries, grad_keys, grad_values), (in_diag, in_first, in_second)
     )
     grad_normed_one = (
         mul(grad_queries, full_qkv[:, :qk], "nt")
         + mul(grad_keys, full_qkv[:, qk : 2 * qk], "nt")
         + mul(grad_values, full_qkv[:, 2 * qk :], "nt")
     )
+    for_second, for_first, far_third, grad_normed_one, in_first, in_second = (
+        lax.optimization_barrier(
+            (
+                by_first(in_diag[low]),
+                by_second(in_diag[high]),
+                to_half(then(far_shares[3], in_diag)),
+                grad_normed_one,
+                in_first,
+                in_second,
+            )
+        )
+    )
+    in_first = jnp.concatenate([in_first[low], add(in_first[high], for_first)], axis=0)
+    in_second = jnp.concatenate([add(in_second[low], for_second), in_second[high]], axis=0)
+    in_moved = [by_first(in_first), by_second(in_second)]
+    far_last = to_half(then(far_shares[4], in_first))
+    grad_normed_one = then(grad_normed_one, (in_first, in_second))
     grad_one, gain_one_grad = norm_backward(grad_normed_one, unit_one, inverse_one, gain_one)
     input_grad = (grad_hidden_in + grad_one).astype(bf)
+    out_parts = [back(block, 1, (in_first, in_second)) for block in made[1:]]
     out_parts, input_grad, gain_one_grad, in_moved, far_last = lax.optimization_barrier(
         (out_parts, input_grad, gain_one_grad, in_moved, far_last)
     )
-    far_sum = jnp.concatenate([far_first, far_second, far_third, far_last], axis=0)
+    out_own = back(made[0], 1, in_moved)
+    far_sum = jnp.concatenate([far_first, far_slot, far_second, far_third, far_last], axis=0)
     ffn_sum = lax.all_gather(add(near_part, far_sum), "dp", axis=0, tiled=True)
     ffn_sum = ffn_sum.reshape(groups, 3, piece, D)
-    out_sent = to_owners(stacked(out_parts))
-    output = (hidden_in + jnp.sum(out_sent.astype(f32), axis=1) + out_own.astype(f32)).astype(bf)
     chip = place // 2
 
     def over_chips(blocks, kept):
@@ -1034,6 +1057,8 @@
     gain_sums = lax.dynamic_slice_in_dim(
         gain_sums, (group * size + place) * own_rows, own_rows, 1
     )
+    out_sent = to_owners(then(stacked(out_parts), in_sum, gain_sums))
+    output = (hidden_in + jnp.sum(out_sent.astype(f32), axis=1) + out_own.astype(f32)).astype(bf)
     return (
         output,
         input_grad,

time: 889 us -> 879 us (0.989)
  Pallas kernels: 234 us -> 279 us
  local copies, waits for them, and re-layouts: 133 us -> 88 us
  other arithmetic: 88.7 us -> 102 us
  matrix products: 57.8 us -> 47.4 us
    unnamed x298 -> x175, local copies, waits for them, and re-layouts: 84.5 us -> 24.9 us
    dot_general x7, matrix products: 57.8 us -> 47.4 us  [mul(): lax.dot_general(left, right, (dims, ((), ())), preferred_element_type=jnp...]
    pallas_call x4, Pallas kernels: 54.9 us -> 65.2 us  [ffn_gates(): pl.pallas_call(gate_kernel, grid=(steps,), in_specs=ins, out_specs=outs,...]
    pallas_call x4, Pallas kernels: 54.4 us -> 63.5 us  [ffn_grad(): pl.pallas_call(functools.partial(grad_kernel, blocks), grid=(3, steps), i...]
    ppermute x66 -> x69, waiting for transfers between devices: 258 us -> 252 us  [move(): lax.ppermute(array, axis, [(m, t) for m, t in pairs if t is not None])]
    ppermute x66 -> x69, starting transfers between devices: 94 us -> 88.2 us  [move(): lax.ppermute(array, axis, [(m, t) for m, t in pairs if t is not None])]
    convert_element_type x6 -> x8, other arithmetic: 22.7 us -> 24.7 us  [add(): return total.astype(kept)]
  transfers between devices with their start and end apart: 72 -> 75, of which waited for: 28 -> 30; matrix products, arithmetic and copies ran while one was open for 22% -> 24% of each run, Pallas kernels for 21% -> 25%
where the time goes in v2:
time: 879 us; the launch traced here: 874 us
  Pallas kernels  279 us (32%)
  waiting for transfers between devices  253 us (29%)
  other arithmetic  102 us (12%)
  starting transfers between devices  88.9 us (10%)
  local copies, waits for them, and re-layouts  88 us (10%)
  matrix products  47.4 us (5%)
  between operations  15.6 us (2%)
    ppermute x69, waiting for transfers between devices, move(): lax.ppermute(array, axis, [(m, t) for m, t in pairs if t is not None])  252 us
    ppermute x69, starting transfers between devices, move(): lax.ppermute(array, axis, [(m, t) for m, t in pairs if t is not None])  88.2 us
    pallas_call x4, Pallas kernels, ffn_back(): pl.pallas_call(functools.partial(back_kernel, count), grid=(D // columns,...  66 us
    pallas_call x4, Pallas kernels, ffn_gates(): pl.pallas_call(gate_kernel, grid=(steps,), in_specs=ins, out_specs=outs,...  65.2 us
    pallas_call x4, Pallas kernels, ffn_grad(): pl.pallas_call(functools.partial(grad_kernel, blocks), grid=(3, steps), i...  63.5 us
    dot_general x7, matrix products, mul(): lax.dot_general(left, right, (dims, ((), ())), preferred_element_type=jnp...  47.4 us
    unnamed x175, local copies, waits for them, and re-layouts  24.9 us
    convert_element_type x8, other arithmetic, add(): return total.astype(kept)  24.7 us
  transfers between devices with their start and end apart: 75, of which 30 were waited for; matrix products, arithmetic and copies ran while one was open for 24% of the time, Pallas kernels for 25%

profile of v2, /device:TPU:0, one launch (start us, length us, event | category | flops | bytes accessed | tf_op | source)
XLA Modules:
  0.0 873.6 jit_solution(13026569957610127834)
XLA Ops:
  16.3 13.3 %collective-permute-done = bf16[64,2688]{1,0:T(8,128)(2,1)S(1)} collective-permute-done((bf16[64,2688]{1,0:T(8,128)(2,1)S(1)}, bf16[64,2688]{1,0:T(8,128)(2,1)S(1)}, u32[]{:S(2)}, u32[]{:S(2)}) %collective-permute-start) | collective-permute-done | bytes 344096 | tf_op jit(solution)/shard_map/ppermute | solution.py:570
  29.6 13.8 %collective-permute-done.1 = bf16[64,2688]{1,0:T(8,128)(2,1)S(1)} collective-permute-done((bf16[64,2688]{1,0:T(8,128)(2,1)S(1)}, bf16[64,2688]{1,0:T(8,128)(2,1)S(1)}, u32[]{:S(2)}, u32[]{:S(2)}) %collective-permute-start.1) | collective-permute-done | bytes 344096 | tf_op jit(solution)/shard_map/ppermute | solution.py:570
  53.8 10.2 %collective-permute-start.6 = (bf16[256,2048]{1,0:T(8,128)(2,1)}, bf16[256,2048]{1,0:T(8,128)(2,1)}, u32[]{:S(2)}, u32[]{:S(2)}) collective-permute-start(bf16[256,2048]{1,0:T(8,128)(2,1)} %slice.222), channel_id=1, source_target_pairs={{0,4},{1,5},{2,6},{3,7},{4,0},{5,1},{6,2},{7,3},{8,12},{9,13},{10,... | collective-permute-start | bytes 3145736 | tf_op jit(solution)/shard_map/ppermute | solution.py:570
  67.5 71.7 %collective-permute-done.6 = bf16[256,2048]{1,0:T(8,128)(2,1)} collective-permute-done((bf16[256,2048]{1,0:T(8,128)(2,1)}, bf16[256,2048]{1,0:T(8,128)(2,1)}, u32[]{:S(2)}, u32[]{:S(2)}) %collective-permute-start.6) | collective-permute-done | bytes 1048608 | tf_op jit(solution)/shard_map/ppermute | solution.py:570
  151.2 17.0 %collective-permute-done.11 = bf16[96,2048]{1,0:T(8,128)(2,1)S(1)} collective-permute-done((bf16[96,2048]{1,0:T(8,128)(2,1)S(1)}, bf16[96,2048]{1,0:T(8,128)(2,1)S(1)}, u32[]{:S(2)}, u32[]{:S(2)}) %collective-permute-start.11) | collective-permute-done | bytes 393248 | tf_op jit(solution)/shard_map/ppermute | solution.py:570
  308.4 15.9 %ffn_gates.4 = (bf16[3,704,512]{2,1,0:T(8,128)(2,1)}, bf16[3,704,512]{2,1,0:T(8,128)(2,1)}) custom-call(bf16[512,2048]{1,0:T(8,128)(2,1)} %multiply_convert_fusion.x_ref.refs_2_, bf16[512,2048]{1,0:T(8,128)(2,1)} %refs_4_.7, bf16[1,2,704,2048]{3,2,1,0:T(8,128)(2,1)} %bitcast.188, bf16[1,1,704,2048]{3,2,1,0:T(8,128)(2,1)} %bitcast.22.refs_1_.refs_4_, ...), custom_call_target="tpu_custom_call" | custom-call | flops 8858370048 | bytes 25821184 | tf_op jit(solution)/shard_map/ffn_gates/pallas_call | solution.py:389
  326.8 16.6 %ffn_gates.5 = (bf16[3,704,512]{2,1,0:T(8,128)(2,1)}, bf16[3,704,512]{2,1,0:T(8,128)(2,1)}) custom-call(bf16[512,2048]{1,0:T(8,128)(2,1)} %multiply_convert_fusion.x_ref.refs_2_, bf16[512,2048]{1,0:T(8,128)(2,1)} %refs_4_.7, bf16[4,2,176,2048]{3,2,1,0:T(8,128)(2,1)} %bitcast.225, bf16[4,1,176,2048]{3,2,1,0:T(8,128)(2,1)} %bitcast.193, ...), custom_call_target="tpu_custom_call" | custom-call | flops 8858370048 | bytes 25821184 | tf_op jit(solution)/shard_map/ffn_gates/pallas_call | solution.py:389
  343.4 20.9 %ffn_back.4 = bf16[512,2048]{1,0:T(8,128)(2,1)} custom-call(bf16[3,704,512]{2,1,0:T(8,128)(2,1)} %get-tuple-element.360.refs_0_, bf16[3,704,512]{2,1,0:T(8,128)(2,1)} %get-tuple-element.361.refs_1_.refs_0_, bf16[3,704,512]{2,1,0:T(8,128)(2,1)} %get-tuple-element.362.refs_2_.refs_0_, bf16[3,704,512]{2,1,0:T(8,128)(2,1)} %get-tuple-element.363.refs_3_.refs_0_, ...), custom_call_target="tpu_custom_call" | custom-call | flops 11811160064 | bytes 30932992 | tf_op jit(solution)/shard_map/ffn_back/pallas_call | solution.py:443
  364.3 15.9 %ffn_gates.6 = (bf16[3,704,512]{2,1,0:T(8,128)(2,1)}, bf16[3,704,512]{2,1,0:T(8,128)(2,1)}) custom-call(bf16[512,2048]{1,0:T(8,128)(2,1)} %collective-permute-done.28.x_ref.refs_3_, bf16[512,2048]{1,0:T(8,128)(2,1)} %copy-done.73, bf16[1,2,704,2048]{3,2,1,0:T(8,128)(2,1)} %bitcast.190, bf16[1,1,704,2048]{3,2,1,0:T(8,128)(2,1)} %bitcast.22.refs_1_.refs_4_, ...), custom_call_target="tpu_custom_call" | custom-call | flops 8858370048 | bytes 25821184 | tf_op jit(solution)/shard_map/ffn_gates/pallas_call | solution.py:389
  380.2 16.8 %ffn_gates.7 = (bf16[3,704,512]{2,1,0:T(8,128)(2,1)}, bf16[3,704,512]{2,1,0:T(8,128)(2,1)}) custom-call(bf16[512,2048]{1,0:T(8,128)(2,1)} %collective-permute-done.28.x_ref.refs_3_, bf16[512,2048]{1,0:T(8,128)(2,1)} %copy-done.73, bf16[4,2,176,2048]{3,2,1,0:T(8,128)(2,1)} %bitcast.227, bf16[4,1,176,2048]{3,2,1,0:T(8,128)(2,1)} %bitcast.194, ...), custom_call_target="tpu_custom_call" | custom-call | flops 8858370048 | bytes 25821184 | tf_op jit(solution)/shard_map/ffn_gates/pallas_call | solution.py:389
  397.0 15.1 %ffn_grad.4 = bf16[4,3,176,2048]{3,2,1,0:T(8,128)(2,1)} custom-call(bf16[3,704,512]{2,1,0:T(8,128)(2,1)} %get-tuple-element.363.refs_3_.refs_0_, bf16[3,704,512]{2,1,0:T(8,128)(2,1)} %get-tuple-element.351.refs_1_.refs_3_, bf16[512,2048]{1,0:T(8,128)(2,1)} %multiply_convert_fusion.x_ref.refs_2_, bf16[512,2048]{1,0:T(8,128)(2,1)} %collective-permute-done.28.x_ref.refs_3_, ...), custom_call_target="tpu_custom_call" | custom-call | flops 8858370048 | bytes 21364736 | tf_op jit(solution)/shard_map/ffn_grad/pallas_call | solution.py:493
  412.1 20.9 %ffn_back.5 = bf16[512,2048]{1,0:T(8,128)(2,1)} custom-call(bf16[3,704,512]{2,1,0:T(8,128)(2,1)} %get-tuple-element.348.refs_0_.refs_1_, bf16[3,704,512]{2,1,0:T(8,128)(2,1)} %get-tuple-element.349.refs_1_, bf16[3,704,512]{2,1,0:T(8,128)(2,1)} %get-tuple-element.350.refs_2_.refs_1_, bf16[3,704,512]{2,1,0:T(8,128)(2,1)} %get-tuple-element.351.refs_1_.refs_3_, ...), custom_call_target="tpu_custom_call" | custom-call | flops 11811160064 | bytes 30932992 | tf_op jit(solution)/shard_map/ffn_back/pallas_call | solution.py:443
  435.0 15.0 %ffn_grad.5 = bf16[4,3,176,2048]{3,2,1,0:T(8,128)(2,1)} custom-call(bf16[3,704,512]{2,1,0:T(8,128)(2,1)} %get-tuple-element.361.refs_1_.refs_0_, bf16[3,704,512]{2,1,0:T(8,128)(2,1)} %get-tuple-element.349.refs_1_, bf16[512,2048]{1,0:T(8,128)(2,1)} %multiply_convert_fusion.x_ref.refs_2_, bf16[512,2048]{1,0:T(8,128)(2,1)} %collective-permute-done.28.x_ref.refs_3_, ...), custom_call_target="tpu_custom_call" | custom-call | flops 8858370048 | bytes 21364736 | tf_op jit(solution)/shard_map/ffn_grad/pallas_call | solution.py:493
  453.9 16.6 %ffn_grad.6 = bf16[4,3,176,2048]{3,2,1,0:T(8,128)(2,1)} custom-call(bf16[3,704,512]{2,1,0:T(8,128)(2,1)} %get-tuple-element.362.refs_2_.refs_0_, bf16[3,704,512]{2,1,0:T(8,128)(2,1)} %get-tuple-element.350.refs_2_.refs_1_, bf16[512,2048]{1,0:T(8,128)(2,1)} %multiply_convert_fusion.x_ref.refs_2_, bf16[512,2048]{1,0:T(8,128)(2,1)} %collective-permute-done.28.x_ref.refs_3_, ...), custom_call_target="tpu_custom_call" | custom-call | flops 8858370048 | bytes 30015488 | tf_op jit(solution)/shard_map/ffn_grad/pallas_call | solution.py:493
  472.5 16.8 %ffn_grad.7 = bf16[4,3,176,2048]{3,2,1,0:T(8,128)(2,1)} custom-call(bf16[3,704,512]{2,1,0:T(8,128)(2,1)} %get-tuple-element.360.refs_0_, bf16[3,704,512]{2,1,0:T(8,128)(2,1)} %get-tuple-element.348.refs_0_.refs_1_, bf16[512,2048]{1,0:T(8,128)(2,1)} %multiply_convert_fusion.x_ref.refs_2_, bf16[512,2048]{1,0:T(8,128)(2,1)} %collective-permute-done.28.x_ref.refs_3_, ...), custom_call_target="tpu_custom_call" | custom-call | flops 8858370048 | bytes 30015488 | tf_op jit(solution)/shard_map/ffn_grad/pallas_call | solution.py:493
  542.2 20.9 %mix_local_grad.1 = (bf16[512,256]{1,0:T(8,128)(2,1)S(1)}, f32[512,256]{1,0:T(8,128)S(1)}, f32[512,2048]{1,0:T(8,128)}) custom-call(bf16[512,256]{1,0:T(8,128)(2,1)S(1)} %get-tuple-element.309.q_ref, bf16[512,256]{1,0:T(8,128)(2,1)S(1)} %get-tuple-element.321.k_ref, bf16[512,2048]{1,0:T(8,128)(2,1)S(1)} %slice.185.v_ref, bf16[512,2048]{1,0:T(8,128)(2,1)} %copy-done.5, ...), custom_call_target="tpu_custom_call" | custom-call | flops 1048576 | bytes 65536 | tf_op jit(solution)/shard_map/mix_local_grad/pallas_call | solution.py:319
  584.0 10.1 %mix_later_grad.1 = (bf16[512,256]{1,0:T(8,128)(2,1)S(1)}, bf16[512,2048]{1,0:T(8,128)(2,1)S(1)}) custom-call(bf16[512,256]{1,0:T(8,128)(2,1)S(1)} %get-tuple-element.321.k_ref, bf16[512,2048]{1,0:T(8,128)(2,1)} %copy-done, f32[512,256]{1,0:T(8,128)S(1)} %copy-done.13, f32[512,2048]{1,0:T(8,128)} %get-tuple-element.323.gv_in_ref, ...), custom_call_target="tpu_custom_call" | custom-call | flops 1048576 | bytes 65536 | tf_op jit(solution)/shard_map/mix_later_grad/pallas_call | solution.py:328
  615.1 11.1 %qkv_grad.1 = bf16[2048,2560]{1,0:T(8,128)(2,1)} custom-call(bf16[512,2048]{1,0:T(8,128)(2,1)} %copy-done.44, bf16[512,256]{1,0:T(8,128)(2,1)} %copy-done.14, bf16[512,256]{1,0:T(8,128)(2,1)} %copy-done.16, bf16[512,2048]{1,0:T(8,128)(2,1)} %copy-done.18), custom_call_target="tpu_custom_call" | custom-call | flops 5368709120 | bytes 15204352 | tf_op jit(solution)/shard_map/qkv_grad/pallas_call | solution.py:539
  650.1 17.9 %collective-permute-done.50 = bf16[112,2048]{1,0:T(8,128)(2,1)S(1)} collective-permute-done((bf16[112,2048]{1,0:T(8,128)(2,1)S(1)}, bf16[112,2048]{1,0:T(8,128)(2,1)S(1)}, u32[]{:S(2)}, u32[]{:S(2)}) %collective-permute-start.50) | collective-permute-done | bytes 458784 | tf_op jit(solution)/shard_map/ppermute | solution.py:570
  707.4 12.0 %ffn_back.6 = bf16[512,2048]{1,0:T(8,128)(2,1)} custom-call(bf16[3,704,512]{2,1,0:T(8,128)(2,1)} %get-tuple-element.348.refs_0_.refs_1_, bf16[3,704,512]{2,1,0:T(8,128)(2,1)} %get-tuple-element.349.refs_1_, bf16[3,704,512]{2,1,0:T(8,128)(2,1)} %get-tuple-element.350.refs_2_.refs_1_, bf16[3,704,512]{2,1,0:T(8,128)(2,1)} %get-tuple-element.351.refs_1_.refs_3_, ...), custom_call_target="tpu_custom_call" | custom-call | flops 5905580032 | bytes 16515072 | tf_op jit(solution)/shard_map/ffn_back/pallas_call | solution.py:443
  725.4 11.5 %collective-permute-done.56 = bf16[176,2048]{1,0:T(8,128)(2,1)} collective-permute-done((bf16[176,2048]{1,0:T(8,128)(2,1)S(1)}, bf16[176,2048]{1,0:T(8,128)(2,1)}, u32[]{:S(2)}, u32[]{:S(2)}) %collective-permute-start.56) | collective-permute-done | bytes 720928 | tf_op jit(solution)/shard_map/ppermute | solution.py:570
  769.4 15.7 %collective-permute-done.58 = bf16[64,2560]{1,0:T(8,128)(2,1)S(1)} collective-permute-done((bf16[64,2560]{1,0:T(8,128)(2,1)S(1)}, bf16[64,2560]{1,0:T(8,128)(2,1)S(1)}, u32[]{:S(2)}, u32[]{:S(2)}) %collective-permute-start.58) | collective-permute-done | bytes 327712 | tf_op jit(solution)/shard_map/ppermute | solution.py:570
  795.1 12.1 %ffn_back.7 = bf16[512,2048]{1,0:T(8,128)(2,1)} custom-call(bf16[3,704,512]{2,1,0:T(8,128)(2,1)} %get-tuple-element.360.refs_0_, bf16[3,704,512]{2,1,0:T(8,128)(2,1)} %get-tuple-element.361.refs_1_.refs_0_, bf16[3,704,512]{2,1,0:T(8,128)(2,1)} %get-tuple-element.362.refs_2_.refs_0_, bf16[3,704,512]{2,1,0:T(8,128)(2,1)} %get-tuple-element.363.refs_3_.refs_0_, ...), custom_call_target="tpu_custom_call" | custom-call | flops 5905580032 | bytes 16515072 | tf_op jit(solution)/shard_map/ffn_back/pallas_call | solution.py:443
  807.8 33.2 %collective-permute-done.68 = bf16[64,2048]{1,0:T(8,128)(2,1)S(1)} collective-permute-done((bf16[64,2048]{1,0:T(8,128)(2,1)}, bf16[64,2048]{1,0:T(8,128)(2,1)S(1)}, u32[]{:S(2)}, u32[]{:S(2)}) %collective-permute-start.68) | collective-permute-done | bytes 262176 | tf_op jit(solution)/shard_map/ppermute | solution.py:570
  (440 shorter events, 416.6 us)
Async XLA Ops:
  7.2 192.6 %all-gather.5.cloned.1.call-start = ((), (), s32[]{:S(2)}) async-start(), calls=%async_computation.2 | async-start | bytes 8650752 | tf_op jit(solution)/shard_map/all_gather | solution.py:758
  7.9 298.6 %all-gather.7.cloned.1.call-start = ((), (), s32[]{:S(2)}) async-start(), calls=%async_computation.3 | async-start | bytes 7208960 | tf_op jit(solution)/shard_map/all_gather | solution.py:790
  43.7 95.6 %collective-permute-start.3 = (bf16[4,64,2688]{2,1,0:T(8,128)(2,1)S(1)}, bf16[4,64,2688]{2,1,0:T(8,128)(2,1)}, u32[]{:S(2)}, u32[]{:S(2)}) collective-permute-start(bf16[4,64,2688]{2,1,0:T(8,128)(2,1)S(1)} %bitcast_dynamic-update-slice_fusion), channel_id=1, source_target_pairs={{0,8},{8,0},{16,24},{24,16},{1,9},{9,1},{17,25},{25,17},{2,10},{10... | collective-permute-start | bytes 4128776 | tf_op jit(solution)/shard_map/ppermute | solution.py:570
  45.2 94.0 %collective-permute-start.4 = (bf16[4,64,2688]{2,1,0:T(8,128)(2,1)S(1)}, bf16[4,64,2688]{2,1,0:T(8,128)(2,1)}, u32[]{:S(2)}, u32[]{:S(2)}) collective-permute-start(bf16[4,64,2688]{2,1,0:T(8,128)(2,1)S(1)} %bitcast_dynamic-update-slice_fusion), channel_id=1, source_target_pairs={{0,16},{8,24},{16,0},{24,8},{1,17},{9,25},{17,1},{25,9},{2,18},{10... | collective-permute-start | bytes 4128776 | tf_op jit(solution)/shard_map/ppermute | solution.py:570
  46.7 92.5 %collective-permute-start.5 = (bf16[4,64,2688]{2,1,0:T(8,128)(2,1)S(1)}, bf16[4,64,2688]{2,1,0:T(8,128)(2,1)S(1)}, u32[]{:S(2)}, u32[]{:S(2)}) collective-permute-start(bf16[4,64,2688]{2,1,0:T(8,128)(2,1)S(1)} %bitcast_dynamic-update-slice_fusion), channel_id=1, source_target_pairs={{0,1},{1,0},{2,3},{3,2},{4,5},{5,4},{6,7},{7,6},{8,9},{9,8},{10,11... | collective-permute-start | bytes 4128776 | tf_op jit(solution)/shard_map/ppermute | solution.py:570
  53.8 85.5 %collective-permute-start.6 = (bf16[256,2048]{1,0:T(8,128)(2,1)}, bf16[256,2048]{1,0:T(8,128)(2,1)}, u32[]{:S(2)}, u32[]{:S(2)}) collective-permute-start(bf16[256,2048]{1,0:T(8,128)(2,1)} %slice.222), channel_id=1, source_target_pairs={{0,4},{1,5},{2,6},{3,7},{4,0},{5,1},{6,2},{7,3},{8,12},{9,13},{10,... | collective-permute-start | bytes 3145736 | tf_op jit(solution)/shard_map/ppermute | solution.py:570
  168.8 30.9 %collective-permute-start.14 = (bf16[112,2048]{1,0:T(8,128)(2,1)}, bf16[112,2048]{1,0:T(8,128)(2,1)}, u32[]{:S(2)}, u32[]{:S(2)}) collective-permute-start(bf16[112,2048]{1,0:T(8,128)(2,1)} %constant_dynamic-slice_fusion), channel_id=1, source_target_pairs={{0,4},{1,5},{2,6},{3,7},{4,0},{5,1},{6,2},{7,3},{8,12},{9,13},{10,... | collective-permute-start | bytes 1376264 | tf_op jit(solution)/shard_map/ppermute | solution.py:570
  168.9 30.9 %collective-permute-start.15 = (bf16[1,1,704,2048]{3,2,1,0:T(8,128)(2,1)}, bf16[1,1,704,2048]{3,2,1,0:T(8,128)(2,1)}, u32[]{:S(2)}, u32[]{:S(2)}) collective-permute-start(bf16[1,1,704,2048]{3,2,1,0:T(8,128)(2,1)} %bitcast.22.refs_1_.refs_4_), channel_id=1, source_target_pairs={{0,1},{1,0},{2,3},{3,2},{4,5},{5,4},{6,7},{7,6},{8,9},{9,8},{10,11... | collective-permute-start | bytes 8650760 | tf_op jit(solution)/shard_map/ppermute | solution.py:570
  168.9 30.8 %collective-permute-start.16 = (bf16[128,2048]{1,0:T(8,128)(2,1)}, bf16[128,2048]{1,0:T(8,128)(2,1)S(1)}, u32[]{:S(2)}, u32[]{:S(2)}) collective-permute-start(bf16[128,2048]{1,0:T(8,128)(2,1)} %slice.177), channel_id=1, source_target_pairs={{0,2},{1,3},{2,0},{3,1},{4,6},{5,7},{6,4},{7,5},{8,10},{9,11},{10,... | collective-permute-start | bytes 1572872 | tf_op jit(solution)/shard_map/ppermute | solution.py:570
  174.4 132.2 %all-gather.9.cloned.1.call-start = ((), (), s32[]{:S(2)}) async-start(), calls=%async_computation.4 | async-start | bytes 3604480 | tf_op jit(solution)/shard_map/all_gather | solution.py:842
  249.9 323.1 %reduce-scatter.3.cloned.1.call-start = ((), (), s32[]{:S(2)}) async-start(), calls=%async_computation.5 | async-start | bytes 10813440 | tf_op jit(solution)/shard_map/reduce_scatter | solution.py:902
  307.1 57.2 %collective-permute-start.28 = (bf16[512,2048]{1,0:T(8,128)(2,1)}, bf16[512,2048]{1,0:T(8,128)(2,1)}, u32[]{:S(2)}, u32[]{:S(2)}) collective-permute-start(bf16[512,2048]{1,0:T(8,128)(2,1)} %multiply_convert_fusion.x_ref.refs_2_), channel_id=1, source_target_pairs={{0,2},{1,3},{2,0},{3,1},{4,6},{5,7},{6,4},{7,5},{8,10},{9,11},{10,... | collective-permute-start | bytes 6291464 | tf_op jit(solution)/shard_map/ppermute | solution.py:570
  412.1 41.8 %collective-permute-start.33 = (bf16[4,3,176,2048]{3,2,1,0:T(8,128)(2,1)}, bf16[4,3,176,2048]{3,2,1,0:T(8,128)(2,1)}, u32[]{:S(2)}, u32[]{:S(2)}) collective-permute-start(bf16[4,3,176,2048]{3,2,1,0:T(8,128)(2,1)} %ffn_grad.4), channel_id=1, source_target_pairs={{0,1},{1,0},{2,3},{3,2},{4,5},{5,4},{6,7},{7,6},{8,9},{9,8},{10,11... | collective-permute-start | bytes 25952264 | tf_op jit(solution)/shard_map/ppermute | solution.py:570
  471.1 268.4 %reduce-scatter.5.cloned.1.call-start = ((), (), s32[]{:S(2)}) async-start(), calls=%async_computation.6 | async-start | bytes 10813440 | tf_op jit(solution)/shard_map/reduce_scatter | solution.py:902
  539.1 317.7 %all-gather.11.cloned.1.call-start = ((), (), s32[]{:S(2)}) async-start(), calls=%async_computation.7 | async-start | bytes 10813440 | tf_op jit(solution)/shard_map/all_gather | solution.py:1038
  637.8 30.3 %collective-permute-start.47 = (bf16[4,4,64,2560]{3,2,1,0:T(8,128)(2,1)}, bf16[4,4,64,2560]{3,2,1,0:T(8,128)(2,1)}, u32[]{:S(2)}, u32[]{:S(2)}) collective-permute-start(bf16[4,4,64,2560]{3,2,1,0:T(8,128)(2,1)} %dynamic-slice_bitcast_fusion), channel_id=1, source_target_pairs={{0,1},{1,0},{2,3},{3,2},{4,5},{5,4},{6,7},{7,6},{8,9},{9,8},{10,11... | collective-permute-start | bytes 15728648 | tf_op jit(solution)/shard_map/ppermute | solution.py:570
  637.9 30.2 %collective-permute-start.48 = (bf16[2,64,2048]{2,1,0:T(8,128)(2,1)}, bf16[2,64,2048]{2,1,0:T(8,128)(2,1)}, u32[]{:S(2)}, u32[]{:S(2)}) collective-permute-start(bf16[2,64,2048]{2,1,0:T(8,128)(2,1)} %get-tuple-element.336), channel_id=1, source_target_pairs={{0,8},{8,0},{16,24},{24,16},{1,9},{9,1},{17,25},{25,17},{2,10},{10... | collective-permute-start | bytes 1572872 | tf_op jit(solution)/shard_map/ppermute | solution.py:570
  699.4 37.5 %collective-permute-start.54 = (bf16[4,64,2560]{2,1,0:T(8,128)(2,1)}, bf16[4,64,2560]{2,1,0:T(8,128)(2,1)S(1)}, u32[]{:S(2)}, u32[]{:S(2)}) collective-permute-start(bf16[4,64,2560]{2,1,0:T(8,128)(2,1)} %pad_maximum_fusion.3), channel_id=1, source_target_pairs={{0,8},{8,0},{16,24},{24,16},{1,9},{9,1},{17,25},{25,17},{2,10},{10... | collective-permute-start | bytes 3932168 | tf_op jit(solution)/shard_map/ppermute | solution.py:570
  703.4 33.6 %collective-permute-start.55 = (bf16[4,64,2560]{2,1,0:T(8,128)(2,1)}, bf16[4,64,2560]{2,1,0:T(8,128)(2,1)S(1)}, u32[]{:S(2)}, u32[]{:S(2)}) collective-permute-start(bf16[4,64,2560]{2,1,0:T(8,128)(2,1)} %pad_maximum_fusion.4), channel_id=1, source_target_pairs={{0,16},{8,24},{16,0},{24,8},{1,17},{9,25},{17,1},{25,9},{2,18},{10... | collective-permute-start | bytes 3932168 | tf_op jit(solution)/shard_map/ppermute | solution.py:570
  704.5 32.4 %collective-permute-start.56 = (bf16[176,2048]{1,0:T(8,128)(2,1)S(1)}, bf16[176,2048]{1,0:T(8,128)(2,1)}, u32[]{:S(2)}, u32[]{:S(2)}) collective-permute-start(bf16[176,2048]{1,0:T(8,128)(2,1)S(1)} %slice.216), channel_id=1, source_target_pairs={{0,4},{1,5},{2,6},{3,7},{4,0},{5,1},{6,2},{7,3},{8,12},{9,13},{10,... | collective-permute-start | bytes 2162696 | tf_op jit(solution)/shard_map/ppermute | solution.py:570
  786.8 66.1 %collective-permute-start.65 = (bf16[512,2048]{1,0:T(8,128)(2,1)}, bf16[512,2048]{1,0:T(8,128)(2,1)}, u32[]{:S(2)}, u32[]{:S(2)}) collective-permute-start(bf16[512,2048]{1,0:T(8,128)(2,1)} %bitcast.78), channel_id=1, source_target_pairs={{0,2},{1,3},{2,0},{3,1},{4,6},{5,7},{6,4},{7,5},{8,10},{9,11},{10,... | collective-permute-start | bytes 6291464 | tf_op jit(solution)/shard_map/ppermute | solution.py:570
  790.7 50.2 %collective-permute-start.68 = (bf16[64,2048]{1,0:T(8,128)(2,1)}, bf16[64,2048]{1,0:T(8,128)(2,1)S(1)}, u32[]{:S(2)}, u32[]{:S(2)}) collective-permute-start(bf16[64,2048]{1,0:T(8,128)(2,1)} %get-tuple-element.408), channel_id=1, source_target_pairs={{0,6},{1,7},{2,4},{3,5},{4,2},{5,3},{6,0},{7,1},{8,14},{9,15},{10,... | collective-permute-start | bytes 786440 | tf_op jit(solution)/shard_map/ppermute | solution.py:570
  792.7 51.5 %collective-permute-start.67 = (bf16[64,2048]{1,0:T(8,128)(2,1)}, bf16[64,2048]{1,0:T(8,128)(2,1)}, u32[]{:S(2)}, u32[]{:S(2)}) collective-permute-start(bf16[64,2048]{1,0:T(8,128)(2,1)} %get-tuple-element.409), channel_id=1, source_target_pairs={{0,4},{1,5},{2,6},{3,7},{4,0},{5,1},{6,2},{7,3},{8,12},{9,13},{10,... | collective-permute-start | bytes 786440 | tf_op jit(solution)/shard_map/ppermute | solution.py:570
  794.2 55.0 %collective-permute-start.66 = (bf16[64,2048]{1,0:T(8,128)(2,1)}, bf16[64,2048]{1,0:T(8,128)(2,1)}, u32[]{:S(2)}, u32[]{:S(2)}) collective-permute-start(bf16[64,2048]{1,0:T(8,128)(2,1)} %get-tuple-element.407), channel_id=1, source_target_pairs={{0,2},{1,3},{2,0},{3,1},{4,6},{5,7},{6,4},{7,5},{8,10},{9,11},{10,... | collective-permute-start | bytes 786440 | tf_op jit(solution)/shard_map/ppermute | solution.py:570
  (134 other events, 2261.8 us)
Sparse Core Ops, SparseCore 0:
  11.0 131.4 all-gather.4
  174.5 64.3 all-gather.6
  250.0 40.0 all-gather.8
  471.2 89.9 reduce-scatter.2
  564.1 114.4 reduce-scatter.4
  744.2 87.9 all-gather.10

commit v3 on v2

--- a/solution.py
+++ b/solution.py
@@ -991,8 +991,10 @@
         lambda ready: qkv_grad(then(normed_one, ready), grad_queries, grad_keys, grad_values),
     )
     in_keep, in_give = chip_halves(in_grad)
-    in_came, out_high, far_second = lax.optimization_barrier(
+    out_parts = [back(block, 1, in_grad) for block in made[1:]]
+    out_parts, in_came, out_high, far_second = lax.optimization_barrier(
         (
+            out_parts,
             to_mate(in_give),
             [by_first(then(out_first[1], in_grad)), by_second(then(out_second[1], in_grad))],
             to_half(then(far_shares[2], in_grad)),
@@ -1010,9 +1012,11 @@
         + mul(grad_keys, full_qkv[:, qk : 2 * qk], "nt")
         + mul(grad_values, full_qkv[:, 2 * qk :], "nt")
     )
-    for_second, for_first, far_third, grad_normed_one, in_first, in_second = (
+    out_split = jnp.split(stacked(out_parts), [rows * 3 // 8], axis=0)
+    out_early, for_second, for_first, far_third, grad_normed_one, in_first, in_second = (
         lax.optimization_barrier(
             (
+                to_owners(then(out_split[0], in_diag)),
                 by_first(in_diag[low]),
                 by_second(in_diag[high]),
                 to_half(then(far_shares[3], in_diag)),
@@ -1029,9 +1033,8 @@
     grad_normed_one = then(grad_normed_one, (in_first, in_second))
     grad_one, gain_one_grad = norm_backward(grad_normed_one, unit_one, inverse_one, gain_one)
     input_grad = (grad_hidden_in + grad_one).astype(bf)
-    out_parts = [back(block, 1, (in_first, in_second)) for block in made[1:]]
-    out_parts, input_grad, gain_one_grad, in_moved, far_last = lax.optimization_barrier(
-        (out_parts, input_grad, gain_one_grad, in_moved, far_last)
+    input_grad, gain_one_grad, in_moved, far_last = lax.optimization_barrier(
+        (input_grad, gain_one_grad, in_moved, far_last)
     )
     out_own = back(made[0], 1, in_moved)
     far_sum = jnp.concatenate([far_first, far_slot, far_second, far_third, far_last], axis=0)
@@ -1057,7 +1060,8 @@
     gain_sums = lax.dynamic_slice_in_dim(
         gain_sums, (group * size + place) * own_rows, own_rows, 1
     )
-    out_sent = to_owners(then(stacked(out_parts), in_sum, gain_sums))
+    out_last = to_owners(then(out_split[1], in_sum, gain_sums))
+    out_sent = jnp.concatenate([out_early, out_last], axis=0)
     output = (hidden_in + jnp.sum(out_sent.astype(f32), axis=1) + out_own.astype(f32)).astype(bf)
     return (
         output,

time: 879 us -> 869 us (0.989)
  waiting for transfers between devices: 253 us -> 224 us
  starting transfers between devices: 88.9 us -> 113 us
    ppermute x69 -> x70, waiting for transfers between devices: 252 us -> 223 us  [move(): lax.ppermute(array, axis, [(m, t) for m, t in pairs if t is not None])]
    ppermute x69 -> x70, starting transfers between devices: 88.2 us -> 112 us  [move(): lax.ppermute(array, axis, [(m, t) for m, t in pairs if t is not None])]
    unnamed x175 -> x197, local copies, waits for them, and re-layouts: 24.9 us -> 26 us
  transfers between devices with their start and end apart: 75 -> 76, of which waited for: 30 -> 27; matrix products, arithmetic and copies ran while one was open for 24% -> 24% of each run, Pallas kernels for 25% -> 26%
where the time goes in v3:
time: 869 us; the launch traced here: 864 us
  Pallas kernels  280 us (32%)
  waiting for transfers between devices  224 us (26%)
  starting transfers between devices  113 us (13%)
  other arithmetic  95.6 us (11%)
  local copies, waits for them, and re-layouts  88.3 us (10%)
  matrix products  47.5 us (5%)
  between operations  15.7 us (2%)
    ppermute x70, waiting for transfers between devices, move(): lax.ppermute(array, axis, [(m, t) for m, t in pairs if t is not None])  223 us
    ppermute x70, starting transfers between devices, move(): lax.ppermute(array, axis, [(m, t) for m, t in pairs if t is not None])  112 us
    pallas_call x4, Pallas kernels, ffn_back(): pl.pallas_call(functools.partial(back_kernel, count), grid=(D // columns,...  66.7 us
    pallas_call x4, Pallas kernels, ffn_gates(): pl.pallas_call(gate_kernel, grid=(steps,), in_specs=ins, out_specs=outs,...  65 us
    pallas_call x4, Pallas kernels, ffn_grad(): pl.pallas_call(functools.partial(grad_kernel, blocks), grid=(3, steps), i...  63.5 us
    dot_general x7, matrix products, mul(): lax.dot_general(left, right, (dims, ((), ())), preferred_element_type=jnp...  47.5 us
    unnamed x197, local copies, waits for them, and re-layouts  26 us
    convert_element_type x8, other arithmetic, add(): return total.astype(kept)  25.5 us
  transfers between devices with their start and end apart: 76, of which 27 were waited for; matrix products, arithmetic and copies ran while one was open for 24% of the time, Pallas kernels for 26%

profile of v3, /device:TPU:0, one launch (start us, length us, event | category | flops | bytes accessed | tf_op | source)
XLA Modules:
  0.0 863.7 jit_solution(11138740076017496484)
XLA Ops:
  16.3 13.3 %collective-permute-done = bf16[64,2688]{1,0:T(8,128)(2,1)S(1)} collective-permute-done((bf16[64,2688]{1,0:T(8,128)(2,1)S(1)}, bf16[64,2688]{1,0:T(8,128)(2,1)S(1)}, u32[]{:S(2)}, u32[]{:S(2)}) %collective-permute-start) | collective-permute-done | bytes 344096 | tf_op jit(solution)/shard_map/ppermute | solution.py:570
  29.6 13.8 %collective-permute-done.1 = bf16[64,2688]{1,0:T(8,128)(2,1)S(1)} collective-permute-done((bf16[64,2688]{1,0:T(8,128)(2,1)S(1)}, bf16[64,2688]{1,0:T(8,128)(2,1)S(1)}, u32[]{:S(2)}, u32[]{:S(2)}) %collective-permute-start.1) | collective-permute-done | bytes 344096 | tf_op jit(solution)/shard_map/ppermute | solution.py:570
  53.8 10.2 %collective-permute-start.6 = (bf16[256,2048]{1,0:T(8,128)(2,1)}, bf16[256,2048]{1,0:T(8,128)(2,1)}, u32[]{:S(2)}, u32[]{:S(2)}) collective-permute-start(bf16[256,2048]{1,0:T(8,128)(2,1)} %slice.224), channel_id=1, source_target_pairs={{0,4},{1,5},{2,6},{3,7},{4,0},{5,1},{6,2},{7,3},{8,12},{9,13},{10,... | collective-permute-start | bytes 3145736 | tf_op jit(solution)/shard_map/ppermute | solution.py:570
  67.5 71.7 %collective-permute-done.6 = bf16[256,2048]{1,0:T(8,128)(2,1)} collective-permute-done((bf16[256,2048]{1,0:T(8,128)(2,1)}, bf16[256,2048]{1,0:T(8,128)(2,1)}, u32[]{:S(2)}, u32[]{:S(2)}) %collective-permute-start.6) | collective-permute-done | bytes 1048608 | tf_op jit(solution)/shard_map/ppermute | solution.py:570
  151.2 17.0 %collective-permute-done.11 = bf16[96,2048]{1,0:T(8,128)(2,1)S(1)} collective-permute-done((bf16[96,2048]{1,0:T(8,128)(2,1)S(1)}, bf16[96,2048]{1,0:T(8,128)(2,1)S(1)}, u32[]{:S(2)}, u32[]{:S(2)}) %collective-permute-start.11) | collective-permute-done | bytes 393248 | tf_op jit(solution)/shard_map/ppermute | solution.py:570
  308.6 15.8 %ffn_gates.4 = (bf16[3,704,512]{2,1,0:T(8,128)(2,1)}, bf16[3,704,512]{2,1,0:T(8,128)(2,1)}) custom-call(bf16[512,2048]{1,0:T(8,128)(2,1)} %multiply_convert_fusion.x_ref.refs_2_, bf16[512,2048]{1,0:T(8,128)(2,1)} %refs_4_.7, bf16[1,2,704,2048]{3,2,1,0:T(8,128)(2,1)} %bitcast.194, bf16[1,1,704,2048]{3,2,1,0:T(8,128)(2,1)} %bitcast.22.refs_1_.refs_4_, ...), custom_call_target="tpu_custom_call" | custom-call | flops 8858370048 | bytes 25821184 | tf_op jit(solution)/shard_map/ffn_gates/pallas_call | solution.py:389
  326.9 16.5 %ffn_gates.5 = (bf16[3,704,512]{2,1,0:T(8,128)(2,1)}, bf16[3,704,512]{2,1,0:T(8,128)(2,1)}) custom-call(bf16[512,2048]{1,0:T(8,128)(2,1)} %multiply_convert_fusion.x_ref.refs_2_, bf16[512,2048]{1,0:T(8,128)(2,1)} %refs_4_.7, bf16[4,2,176,2048]{3,2,1,0:T(8,128)(2,1)} %bitcast.231, bf16[4,1,176,2048]{3,2,1,0:T(8,128)(2,1)} %bitcast.199, ...), custom_call_target="tpu_custom_call" | custom-call | flops 8858370048 | bytes 25821184 | tf_op jit(solution)/shard_map/ffn_gates/pallas_call | solution.py:389
  343.4 20.9 %ffn_back.4 = bf16[512,2048]{1,0:T(8,128)(2,1)} custom-call(bf16[3,704,512]{2,1,0:T(8,128)(2,1)} %get-tuple-element.364.refs_0_, bf16[3,704,512]{2,1,0:T(8,128)(2,1)} %get-tuple-element.365.refs_1_.refs_0_, bf16[3,704,512]{2,1,0:T(8,128)(2,1)} %get-tuple-element.366.refs_2_.refs_0_, bf16[3,704,512]{2,1,0:T(8,128)(2,1)} %get-tuple-element.367.refs_3_.refs_0_, ...), custom_call_target="tpu_custom_call" | custom-call | flops 11811160064 | bytes 30932992 | tf_op jit(solution)/shard_map/ffn_back/pallas_call | solution.py:443
  364.4 15.9 %ffn_gates.6 = (bf16[3,704,512]{2,1,0:T(8,128)(2,1)}, bf16[3,704,512]{2,1,0:T(8,128)(2,1)}) custom-call(bf16[512,2048]{1,0:T(8,128)(2,1)} %collective-permute-done.28.x_ref.refs_3_, bf16[512,2048]{1,0:T(8,128)(2,1)} %copy-done.84, bf16[1,2,704,2048]{3,2,1,0:T(8,128)(2,1)} %bitcast.196, bf16[1,1,704,2048]{3,2,1,0:T(8,128)(2,1)} %bitcast.22.refs_1_.refs_4_, ...), custom_call_target="tpu_custom_call" | custom-call | flops 8858370048 | bytes 25821184 | tf_op jit(solution)/shard_map/ffn_gates/pallas_call | solution.py:389
  380.3 16.8 %ffn_gates.7 = (bf16[3,704,512]{2,1,0:T(8,128)(2,1)}, bf16[3,704,512]{2,1,0:T(8,128)(2,1)}) custom-call(bf16[512,2048]{1,0:T(8,128)(2,1)} %collective-permute-done.28.x_ref.refs_3_, bf16[512,2048]{1,0:T(8,128)(2,1)} %copy-done.84, bf16[4,2,176,2048]{3,2,1,0:T(8,128)(2,1)} %bitcast.233, bf16[4,1,176,2048]{3,2,1,0:T(8,128)(2,1)} %bitcast.200, ...), custom_call_target="tpu_custom_call" | custom-call | flops 8858370048 | bytes 25821184 | tf_op jit(solution)/shard_map/ffn_gates/pallas_call | solution.py:389
  397.0 15.1 %ffn_grad.4 = bf16[4,3,176,2048]{3,2,1,0:T(8,128)(2,1)} custom-call(bf16[3,704,512]{2,1,0:T(8,128)(2,1)} %get-tuple-element.367.refs_3_.refs_0_, bf16[3,704,512]{2,1,0:T(8,128)(2,1)} %get-tuple-element.340.refs_1_.refs_3_, bf16[512,2048]{1,0:T(8,128)(2,1)} %multiply_convert_fusion.x_ref.refs_2_, bf16[512,2048]{1,0:T(8,128)(2,1)} %collective-permute-done.28.x_ref.refs_3_, ...), custom_call_target="tpu_custom_call" | custom-call | flops 8858370048 | bytes 21364736 | tf_op jit(solution)/shard_map/ffn_grad/pallas_call | solution.py:493
  412.1 20.9 %ffn_back.5 = bf16[512,2048]{1,0:T(8,128)(2,1)} custom-call(bf16[3,704,512]{2,1,0:T(8,128)(2,1)} %get-tuple-element.337.refs_0_.refs_1_, bf16[3,704,512]{2,1,0:T(8,128)(2,1)} %get-tuple-element.338.refs_1_, bf16[3,704,512]{2,1,0:T(8,128)(2,1)} %get-tuple-element.339.refs_2_.refs_1_, bf16[3,704,512]{2,1,0:T(8,128)(2,1)} %get-tuple-element.340.refs_1_.refs_3_, ...), custom_call_target="tpu_custom_call" | custom-call | flops 11811160064 | bytes 30932992 | tf_op jit(solution)/shard_map/ffn_back/pallas_call | solution.py:443
  435.0 15.0 %ffn_grad.5 = bf16[4,3,176,2048]{3,2,1,0:T(8,128)(2,1)} custom-call(bf16[3,704,512]{2,1,0:T(8,128)(2,1)} %get-tuple-element.365.refs_1_.refs_0_, bf16[3,704,512]{2,1,0:T(8,128)(2,1)} %get-tuple-element.338.refs_1_, bf16[512,2048]{1,0:T(8,128)(2,1)} %multiply_convert_fusion.x_ref.refs_2_, bf16[512,2048]{1,0:T(8,128)(2,1)} %collective-permute-done.28.x_ref.refs_3_, ...), custom_call_target="tpu_custom_call" | custom-call | flops 8858370048 | bytes 21364736 | tf_op jit(solution)/shard_map/ffn_grad/pallas_call | solution.py:493
  453.9 16.6 %ffn_grad.6 = bf16[4,3,176,2048]{3,2,1,0:T(8,128)(2,1)} custom-call(bf16[3,704,512]{2,1,0:T(8,128)(2,1)} %get-tuple-element.366.refs_2_.refs_0_, bf16[3,704,512]{2,1,0:T(8,128)(2,1)} %get-tuple-element.339.refs_2_.refs_1_, bf16[512,2048]{1,0:T(8,128)(2,1)} %multiply_convert_fusion.x_ref.refs_2_, bf16[512,2048]{1,0:T(8,128)(2,1)} %collective-permute-done.28.x_ref.refs_3_, ...), custom_call_target="tpu_custom_call" | custom-call | flops 8858370048 | bytes 30015488 | tf_op jit(solution)/shard_map/ffn_grad/pallas_call | solution.py:493
  472.5 16.8 %ffn_grad.7 = bf16[4,3,176,2048]{3,2,1,0:T(8,128)(2,1)} custom-call(bf16[3,704,512]{2,1,0:T(8,128)(2,1)} %get-tuple-element.364.refs_0_, bf16[3,704,512]{2,1,0:T(8,128)(2,1)} %get-tuple-element.337.refs_0_.refs_1_, bf16[512,2048]{1,0:T(8,128)(2,1)} %multiply_convert_fusion.x_ref.refs_2_, bf16[512,2048]{1,0:T(8,128)(2,1)} %collective-permute-done.28.x_ref.refs_3_, ...), custom_call_target="tpu_custom_call" | custom-call | flops 8858370048 | bytes 30015488 | tf_op jit(solution)/shard_map/ffn_grad/pallas_call | solution.py:493
  542.2 20.9 %mix_local_grad.1 = (bf16[512,256]{1,0:T(8,128)(2,1)S(1)}, f32[512,256]{1,0:T(8,128)S(1)}, f32[512,2048]{1,0:T(8,128)}) custom-call(bf16[512,256]{1,0:T(8,128)(2,1)S(1)} %get-tuple-element.311.q_ref, bf16[512,256]{1,0:T(8,128)(2,1)S(1)} %get-tuple-element.323.k_ref, bf16[512,2048]{1,0:T(8,128)(2,1)S(1)} %slice.187.v_ref, bf16[512,2048]{1,0:T(8,128)(2,1)} %copy-done.5, ...), custom_call_target="tpu_custom_call" | custom-call | flops 1048576 | bytes 65536 | tf_op jit(solution)/shard_map/mix_local_grad/pallas_call | solution.py:319
  584.0 10.2 %mix_later_grad.1 = (bf16[512,256]{1,0:T(8,128)(2,1)S(1)}, bf16[512,2048]{1,0:T(8,128)(2,1)S(1)}) custom-call(bf16[512,256]{1,0:T(8,128)(2,1)S(1)} %get-tuple-element.323.k_ref, bf16[512,2048]{1,0:T(8,128)(2,1)} %copy-done, f32[512,256]{1,0:T(8,128)S(1)} %copy-done.13, f32[512,2048]{1,0:T(8,128)} %get-tuple-element.325.gv_in_ref, ...), custom_call_target="tpu_custom_call" | custom-call | flops 1048576 | bytes 65536 | tf_op jit(solution)/shard_map/mix_later_grad/pallas_call | solution.py:328
  613.2 11.3 %qkv_grad.1 = bf16[2048,2560]{1,0:T(8,128)(2,1)} custom-call(bf16[512,2048]{1,0:T(8,128)(2,1)} %copy-done.48, bf16[512,256]{1,0:T(8,128)(2,1)} %copy-done.14, bf16[512,256]{1,0:T(8,128)(2,1)} %copy-done.16, bf16[512,2048]{1,0:T(8,128)(2,1)} %copy-done.18), custom_call_target="tpu_custom_call" | custom-call | flops 5368709120 | bytes 15204352 | tf_op jit(solution)/shard_map/qkv_grad/pallas_call | solution.py:539
  646.7 12.7 %ffn_back.6 = bf16[512,2048]{1,0:T(8,128)(2,1)} custom-call(bf16[3,704,512]{2,1,0:T(8,128)(2,1)} %get-tuple-element.337.refs_0_.refs_1_, bf16[3,704,512]{2,1,0:T(8,128)(2,1)} %get-tuple-element.338.refs_1_, bf16[3,704,512]{2,1,0:T(8,128)(2,1)} %get-tuple-element.339.refs_2_.refs_1_, bf16[3,704,512]{2,1,0:T(8,128)(2,1)} %get-tuple-element.340.refs_1_.refs_3_, ...), custom_call_target="tpu_custom_call" | custom-call | flops 5905580032 | bytes 16515072 | tf_op jit(solution)/shard_map/ffn_back/pallas_call | solution.py:443
  717.5 26.0 %collective-permute-done.57 = bf16[176,2048]{1,0:T(8,128)(2,1)S(1)} collective-permute-done((bf16[176,2048]{1,0:T(8,128)(2,1)S(1)}, bf16[176,2048]{1,0:T(8,128)(2,1)S(1)}, u32[]{:S(2)}, u32[]{:S(2)}) %collective-permute-start.57) | collective-permute-done | bytes 720928 | tf_op jit(solution)/shard_map/ppermute | solution.py:570
  777.2 14.6 %collective-permute-start.67 = (bf16[64,2048]{1,0:T(8,128)(2,1)}, bf16[64,2048]{1,0:T(8,128)(2,1)}, u32[]{:S(2)}, u32[]{:S(2)}) collective-permute-start(bf16[64,2048]{1,0:T(8,128)(2,1)} %get-tuple-element.411), channel_id=1, source_target_pairs={{0,2},{1,3},{2,0},{3,1},{4,6},{5,7},{6,4},{7,5},{8,10},{9,11},{10,... | collective-permute-start | bytes 786440 | tf_op jit(solution)/shard_map/ppermute | solution.py:570
  791.8 15.3 %collective-permute-done.59 = bf16[64,2560]{1,0:T(8,128)(2,1)S(1)} collective-permute-done((bf16[64,2560]{1,0:T(8,128)(2,1)S(1)}, bf16[64,2560]{1,0:T(8,128)(2,1)S(1)}, u32[]{:S(2)}, u32[]{:S(2)}) %collective-permute-start.59) | collective-permute-done | bytes 327712 | tf_op jit(solution)/shard_map/ppermute | solution.py:570
  809.4 12.1 %ffn_back.7 = bf16[512,2048]{1,0:T(8,128)(2,1)} custom-call(bf16[3,704,512]{2,1,0:T(8,128)(2,1)} %get-tuple-element.364.refs_0_, bf16[3,704,512]{2,1,0:T(8,128)(2,1)} %get-tuple-element.365.refs_1_.refs_0_, bf16[3,704,512]{2,1,0:T(8,128)(2,1)} %get-tuple-element.366.refs_2_.refs_0_, bf16[3,704,512]{2,1,0:T(8,128)(2,1)} %get-tuple-element.367.refs_3_.refs_0_, ...), custom_call_target="tpu_custom_call" | custom-call | flops 5905580032 | bytes 16515072 | tf_op jit(solution)/shard_map/ffn_back/pallas_call | solution.py:443
  826.0 17.2 %collective-permute-done.66 = bf16[320,2048]{1,0:T(8,128)(2,1)} collective-permute-done((bf16[320,2048]{1,0:T(8,128)(2,1)}, bf16[320,2048]{1,0:T(8,128)(2,1)}, u32[]{:S(2)}, u32[]{:S(2)}) %collective-permute-start.66) | collective-permute-done | bytes 1310752 | tf_op jit(solution)/shard_map/ppermute | solution.py:570
  (466 shorter events, 411.3 us)
Async XLA Ops:
  7.2 192.8 %all-gather.5.cloned.1.call-start = ((), (), s32[]{:S(2)}) async-start(), calls=%async_computation.2 | async-start | bytes 8650752 | tf_op jit(solution)/shard_map/all_gather | solution.py:758
  7.9 298.8 %all-gather.7.cloned.1.call-start = ((), (), s32[]{:S(2)}) async-start(), calls=%async_computation.3 | async-start | bytes 7208960 | tf_op jit(solution)/shard_map/all_gather | solution.py:790
  43.7 95.6 %collective-permute-start.3 = (bf16[4,64,2688]{2,1,0:T(8,128)(2,1)S(1)}, bf16[4,64,2688]{2,1,0:T(8,128)(2,1)}, u32[]{:S(2)}, u32[]{:S(2)}) collective-permute-start(bf16[4,64,2688]{2,1,0:T(8,128)(2,1)S(1)} %bitcast_dynamic-update-slice_fusion), channel_id=1, source_target_pairs={{0,8},{8,0},{16,24},{24,16},{1,9},{9,1},{17,25},{25,17},{2,10},{10... | collective-permute-start | bytes 4128776 | tf_op jit(solution)/shard_map/ppermute | solution.py:570
  45.2 94.0 %collective-permute-start.4 = (bf16[4,64,2688]{2,1,0:T(8,128)(2,1)S(1)}, bf16[4,64,2688]{2,1,0:T(8,128)(2,1)}, u32[]{:S(2)}, u32[]{:S(2)}) collective-permute-start(bf16[4,64,2688]{2,1,0:T(8,128)(2,1)S(1)} %bitcast_dynamic-update-slice_fusion), channel_id=1, source_target_pairs={{0,16},{8,24},{16,0},{24,8},{1,17},{9,25},{17,1},{25,9},{2,18},{10... | collective-permute-start | bytes 4128776 | tf_op jit(solution)/shard_map/ppermute | solution.py:570
  46.7 92.5 %collective-permute-start.5 = (bf16[4,64,2688]{2,1,0:T(8,128)(2,1)S(1)}, bf16[4,64,2688]{2,1,0:T(8,128)(2,1)S(1)}, u32[]{:S(2)}, u32[]{:S(2)}) collective-permute-start(bf16[4,64,2688]{2,1,0:T(8,128)(2,1)S(1)} %bitcast_dynamic-update-slice_fusion), channel_id=1, source_target_pairs={{0,1},{1,0},{2,3},{3,2},{4,5},{5,4},{6,7},{7,6},{8,9},{9,8},{10,11... | collective-permute-start | bytes 4128776 | tf_op jit(solution)/shard_map/ppermute | solution.py:570
  53.8 85.5 %collective-permute-start.6 = (bf16[256,2048]{1,0:T(8,128)(2,1)}, bf16[256,2048]{1,0:T(8,128)(2,1)}, u32[]{:S(2)}, u32[]{:S(2)}) collective-permute-start(bf16[256,2048]{1,0:T(8,128)(2,1)} %slice.224), channel_id=1, source_target_pairs={{0,4},{1,5},{2,6},{3,7},{4,0},{5,1},{6,2},{7,3},{8,12},{9,13},{10,... | collective-permute-start | bytes 3145736 | tf_op jit(solution)/shard_map/ppermute | solution.py:570
  168.9 31.1 %collective-permute-start.14 = (bf16[112,2048]{1,0:T(8,128)(2,1)}, bf16[112,2048]{1,0:T(8,128)(2,1)}, u32[]{:S(2)}, u32[]{:S(2)}) collective-permute-start(bf16[112,2048]{1,0:T(8,128)(2,1)} %constant_dynamic-slice_fusion), channel_id=1, source_target_pairs={{0,4},{1,5},{2,6},{3,7},{4,0},{5,1},{6,2},{7,3},{8,12},{9,13},{10,... | collective-permute-start | bytes 1376264 | tf_op jit(solution)/shard_map/ppermute | solution.py:570
  168.9 31.1 %collective-permute-start.15 = (bf16[1,1,704,2048]{3,2,1,0:T(8,128)(2,1)}, bf16[1,1,704,2048]{3,2,1,0:T(8,128)(2,1)}, u32[]{:S(2)}, u32[]{:S(2)}) collective-permute-start(bf16[1,1,704,2048]{3,2,1,0:T(8,128)(2,1)} %bitcast.22.refs_1_.refs_4_), channel_id=1, source_target_pairs={{0,1},{1,0},{2,3},{3,2},{4,5},{5,4},{6,7},{7,6},{8,9},{9,8},{10,11... | collective-permute-start | bytes 8650760 | tf_op jit(solution)/shard_map/ppermute | solution.py:570
  168.9 31.0 %collective-permute-start.16 = (bf16[128,2048]{1,0:T(8,128)(2,1)}, bf16[128,2048]{1,0:T(8,128)(2,1)S(1)}, u32[]{:S(2)}, u32[]{:S(2)}) collective-permute-start(bf16[128,2048]{1,0:T(8,128)(2,1)} %slice.179), channel_id=1, source_target_pairs={{0,2},{1,3},{2,0},{3,1},{4,6},{5,7},{6,4},{7,5},{8,10},{9,11},{10,... | collective-permute-start | bytes 1572872 | tf_op jit(solution)/shard_map/ppermute | solution.py:570
  174.4 132.3 %all-gather.9.cloned.1.call-start = ((), (), s32[]{:S(2)}) async-start(), calls=%async_computation.4 | async-start | bytes 3604480 | tf_op jit(solution)/shard_map/all_gather | solution.py:842
  250.1 322.9 %reduce-scatter.3.cloned.1.call-start = ((), (), s32[]{:S(2)}) async-start(), calls=%async_computation.5 | async-start | bytes 10813440 | tf_op jit(solution)/shard_map/reduce_scatter | solution.py:902
  307.3 57.0 %collective-permute-start.28 = (bf16[512,2048]{1,0:T(8,128)(2,1)}, bf16[512,2048]{1,0:T(8,128)(2,1)}, u32[]{:S(2)}, u32[]{:S(2)}) collective-permute-start(bf16[512,2048]{1,0:T(8,128)(2,1)} %multiply_convert_fusion.x_ref.refs_2_), channel_id=1, source_target_pairs={{0,2},{1,3},{2,0},{3,1},{4,6},{5,7},{6,4},{7,5},{8,10},{9,11},{10,... | collective-permute-start | bytes 6291464 | tf_op jit(solution)/shard_map/ppermute | solution.py:570
  412.1 41.8 %collective-permute-start.33 = (bf16[4,3,176,2048]{3,2,1,0:T(8,128)(2,1)}, bf16[4,3,176,2048]{3,2,1,0:T(8,128)(2,1)}, u32[]{:S(2)}, u32[]{:S(2)}) collective-permute-start(bf16[4,3,176,2048]{3,2,1,0:T(8,128)(2,1)} %ffn_grad.4), channel_id=1, source_target_pairs={{0,1},{1,0},{2,3},{3,2},{4,5},{5,4},{6,7},{7,6},{8,9},{9,8},{10,11... | collective-permute-start | bytes 25952264 | tf_op jit(solution)/shard_map/ppermute | solution.py:570
  471.1 273.4 %reduce-scatter.5.cloned.1.call-start = ((), (), s32[]{:S(2)}) async-start(), calls=%async_computation.6 | async-start | bytes 10813440 | tf_op jit(solution)/shard_map/reduce_scatter | solution.py:902
  539.1 307.8 %all-gather.11.cloned.1.call-start = ((), (), s32[]{:S(2)}) async-start(), calls=%async_computation.7 | async-start | bytes 10813440 | tf_op jit(solution)/shard_map/all_gather | solution.py:1041
  706.1 37.4 %collective-permute-start.55 = (bf16[4,64,2560]{2,1,0:T(8,128)(2,1)S(1)}, bf16[4,64,2560]{2,1,0:T(8,128)(2,1)}, u32[]{:S(2)}, u32[]{:S(2)}) collective-permute-start(bf16[4,64,2560]{2,1,0:T(8,128)(2,1)S(1)} %pad_maximum_fusion.3), channel_id=1, source_target_pairs={{0,8},{8,0},{16,24},{24,16},{1,9},{9,1},{17,25},{25,17},{2,10},{10... | collective-permute-start | bytes 3932168 | tf_op jit(solution)/shard_map/ppermute | solution.py:570
  709.0 34.5 %collective-permute-start.56 = (bf16[4,64,2560]{2,1,0:T(8,128)(2,1)S(1)}, bf16[4,64,2560]{2,1,0:T(8,128)(2,1)}, u32[]{:S(2)}, u32[]{:S(2)}) collective-permute-start(bf16[4,64,2560]{2,1,0:T(8,128)(2,1)S(1)} %pad_maximum_fusion.4), channel_id=1, source_target_pairs={{0,16},{8,24},{16,0},{24,8},{1,17},{9,25},{17,1},{25,9},{2,18},{10... | collective-permute-start | bytes 3932168 | tf_op jit(solution)/shard_map/ppermute | solution.py:570
  710.8 32.7 %collective-permute-start.57 = (bf16[176,2048]{1,0:T(8,128)(2,1)S(1)}, bf16[176,2048]{1,0:T(8,128)(2,1)S(1)}, u32[]{:S(2)}, u32[]{:S(2)}) collective-permute-start(bf16[176,2048]{1,0:T(8,128)(2,1)S(1)} %copy-done.54), channel_id=1, source_target_pairs={{0,4},{1,5},{2,6},{3,7},{4,0},{5,1},{6,2},{7,3},{8,12},{9,13},{10,... | collective-permute-start | bytes 2162696 | tf_op jit(solution)/shard_map/ppermute | solution.py:570
  768.2 38.9 %collective-permute-start.59 = (bf16[64,2560]{1,0:T(8,128)(2,1)S(1)}, bf16[64,2560]{1,0:T(8,128)(2,1)S(1)}, u32[]{:S(2)}, u32[]{:S(2)}) collective-permute-start(bf16[64,2560]{1,0:T(8,128)(2,1)S(1)} %get-tuple-element.397), channel_id=1, source_target_pairs={{0,4},{1,5},{2,6},{3,7},{4,0},{5,1},{6,2},{7,3},{8,12},{9,13},{10,... | collective-permute-start | bytes 983048 | tf_op jit(solution)/shard_map/ppermute | solution.py:570
  768.2 38.9 %collective-permute-start.58 = (bf16[64,2560]{1,0:T(8,128)(2,1)S(1)}, bf16[64,2560]{1,0:T(8,128)(2,1)S(1)}, u32[]{:S(2)}, u32[]{:S(2)}) collective-permute-start(bf16[64,2560]{1,0:T(8,128)(2,1)S(1)} %get-tuple-element.395), channel_id=1, source_target_pairs={{0,2},{1,3},{2,0},{3,1},{4,6},{5,7},{6,4},{7,5},{8,10},{9,11},{10,... | collective-permute-start | bytes 983048 | tf_op jit(solution)/shard_map/ppermute | solution.py:570
  771.3 50.8 %collective-permute-start.69 = (bf16[64,2048]{1,0:T(8,128)(2,1)}, bf16[64,2048]{1,0:T(8,128)(2,1)S(1)}, u32[]{:S(2)}, u32[]{:S(2)}) collective-permute-start(bf16[64,2048]{1,0:T(8,128)(2,1)} %get-tuple-element.412), channel_id=1, source_target_pairs={{0,6},{1,7},{2,4},{3,5},{4,2},{5,3},{6,0},{7,1},{8,14},{9,15},{10,... | collective-permute-start | bytes 786440 | tf_op jit(solution)/shard_map/ppermute | solution.py:570
  774.8 47.3 %collective-permute-start.68 = (bf16[64,2048]{1,0:T(8,128)(2,1)}, bf16[64,2048]{1,0:T(8,128)(2,1)}, u32[]{:S(2)}, u32[]{:S(2)}) collective-permute-start(bf16[64,2048]{1,0:T(8,128)(2,1)} %get-tuple-element.413), channel_id=1, source_target_pairs={{0,4},{1,5},{2,6},{3,7},{4,0},{5,1},{6,2},{7,3},{8,12},{9,13},{10,... | collective-permute-start | bytes 786440 | tf_op jit(solution)/shard_map/ppermute | solution.py:570
  777.2 44.9 %collective-permute-start.67 = (bf16[64,2048]{1,0:T(8,128)(2,1)}, bf16[64,2048]{1,0:T(8,128)(2,1)}, u32[]{:S(2)}, u32[]{:S(2)}) collective-permute-start(bf16[64,2048]{1,0:T(8,128)(2,1)} %get-tuple-element.411), channel_id=1, source_target_pairs={{0,2},{1,3},{2,0},{3,1},{4,6},{5,7},{6,4},{7,5},{8,10},{9,11},{10,... | collective-permute-start | bytes 786440 | tf_op jit(solution)/shard_map/ppermute | solution.py:570
  808.6 34.6 %collective-permute-start.66 = (bf16[320,2048]{1,0:T(8,128)(2,1)}, bf16[320,2048]{1,0:T(8,128)(2,1)}, u32[]{:S(2)}, u32[]{:S(2)}) collective-permute-start(bf16[320,2048]{1,0:T(8,128)(2,1)} %bitcast.82), channel_id=1, source_target_pairs={{0,2},{1,3},{2,0},{3,1},{4,6},{5,7},{6,4},{7,5},{8,10},{9,11},{10,... | collective-permute-start | bytes 3932168 | tf_op jit(solution)/shard_map/ppermute | solution.py:570
  (146 other events, 2232.5 us)
Sparse Core Ops, SparseCore 0:
  11.0 131.4 all-gather.4
  174.5 64.3 all-gather.6
  250.2 40.0 all-gather.8
  471.2 89.9 reduce-scatter.2
  564.2 115.0 reduce-scatter.4
  749.1 90.8 all-gather.10

commit v4 on v3

--- a/solution.py
+++ b/solution.py
@@ -771,21 +771,24 @@
         return lax.optimization_barrier((mover(array), work(array)))
 
     both_cut, down_cut = 2 * piece * 8 // 11, piece * 7 // 11
-    in_near, in_mate, both_first = lax.optimization_barrier(
+    blank = jnp.zeros((groups, size // 2, 2) + packed.shape, bf)
+    blank, in_near, in_mate, both_first = lax.optimization_barrier(
         (
+            blank,
             first_groups(in_chips),
             to_mate(in_chips),
             to_half(then(far_both[:both_cut], in_chips)),
         )
     )
-    in_third, in_mates, both_second = lax.optimization_barrier(
+    full_in, in_third, in_mates, both_second = lax.optimization_barrier(
         (
+            assembled([(0, 0, in_chips, in_mate)], groups, size // 2, blank),
             third_group(*in_near),
             [to_mate(share) for share in in_near],
             to_half(then(far_both[both_cut:], in_near)),
         )
     )
-    in_mates = [in_mate, *in_mates] + [to_mate(share) for share in in_third]
+    in_mates = [*in_mates] + [to_mate(share) for share in in_third]
     far_both = jnp.concatenate([both_first, both_second], axis=0)
     far_both = lax.all_gather(far_both, "dp", axis=0, tiled=True).reshape(groups, 2, piece, D)
     down_first = to_half(then(far_down[:down_cut], in_third))
@@ -795,7 +798,6 @@
         (step, at, own, other)
         for (step, at, own), other in zip(
             (
-                (0, 0, in_chips),
                 (1, 0, in_near[0]),
                 (2, 0, in_near[1]),
                 (3, 0, in_third[0]),
@@ -804,7 +806,7 @@
             in_mates,
         )
     ]
-    full_in = assembled(in_pieces, groups, size // 2).reshape(D, packed.shape[1])
+    full_in = assembled(in_pieces, groups, size // 2, full_in).reshape(D, packed.shape[1])
 
     row_start = place * rows
     seq_ends = jnp.cumsum(seq_lengths[0], dtype=jnp.int32)
@@ -831,7 +833,7 @@
         then(cot_shares[3], full_in),
         lambda ready: (
             peers_of(ready),
-            to_mate(then(mine[0][:, :1], ready)),
+            to_mate(then(w_gate.T, ready)).reshape(1, 1, hidden, D),
             to_half(then(far_down[down_cut:], ready)),
         ),
         lambda ready: mul(then(normed_one, ready), full_qkv).astype(bf),
@@ -842,7 +844,7 @@
     far_down = lax.all_gather(far_down, "dp", axis=0, tiled=True).reshape(groups, 1, piece, D)
     (got, mate_up), own_state = beside_one(
         then(cot_shares[4], qkv),
-        lambda ready: (peers_of(ready), to_mate(then(mine[0][:, 1:], ready))),
+        lambda ready: (peers_of(ready), to_mate(then(w_up.T, ready)).reshape(1, 1, hidden, D)),
         lambda ready: mix_state(then(keys, ready), values, tables, last_doc),
     )
     cot_got.append(got)

time: 869 us -> 866 us (level)
    unnamed x197 -> x207, local copies, waits for them, and re-layouts: 26 us -> 26.1 us
  transfers between devices with their start and end apart: 76 -> 76, of which waited for: 27 -> 30; matrix products, arithmetic and copies ran while one was open for 24% -> 23% of each run, Pallas kernels for 26% -> 26%
where the time goes in v4:
time: 866 us; the launch traced here: 860 us
  Pallas kernels  280 us (32%)
  waiting for transfers between devices  231 us (27%)
  starting transfers between devices  111 us (13%)
  other arithmetic  95 us (11%)
  local copies, waits for them, and re-layouts  79.7 us (9%)
  matrix products  47.5 us (5%)
  between operations  15.7 us (2%)
    ppermute x70, waiting for transfers between devices, move(): lax.ppermute(array, axis, [(m, t) for m, t in pairs if t is not None])  230 us
    ppermute x70, starting transfers between devices, move(): lax.ppermute(array, axis, [(m, t) for m, t in pairs if t is not None])  110 us
    pallas_call x4, Pallas kernels, ffn_back(): pl.pallas_call(functools.partial(back_kernel, count), grid=(D // columns,...  66.7 us
    pallas_call x4, Pallas kernels, ffn_gates(): pl.pallas_call(gate_kernel, grid=(steps,), in_specs=ins, out_specs=outs,...  65.2 us
    pallas_call x4, Pallas kernels, ffn_grad(): pl.pallas_call(functools.partial(grad_kernel, blocks), grid=(3, steps), i...  63.5 us
    dot_general x7, matrix products, mul(): lax.dot_general(left, right, (dims, ((), ())), preferred_element_type=jnp...  47.5 us
    unnamed x207, local copies, waits for them, and re-layouts  26.1 us
    convert_element_type x8, other arithmetic, add(): return total.astype(kept)  25.9 us
  transfers between devices with their start and end apart: 76, of which 30 were waited for; matrix products, arithmetic and copies ran while one was open for 23% of the time, Pallas kernels for 26%

profile of v4, /device:TPU:0, one launch (start us, length us, event | category | flops | bytes accessed | tf_op | source)
XLA Modules:
  0.0 859.9 jit_solution(16871353350837824170)
XLA Ops:
  16.3 13.6 %collective-permute-done = bf16[64,2688]{1,0:T(8,128)(2,1)} collective-permute-done((bf16[64,2688]{1,0:T(8,128)(2,1)S(1)}, bf16[64,2688]{1,0:T(8,128)(2,1)}, u32[]{:S(2)}, u32[]{:S(2)}) %collective-permute-start) | collective-permute-done | bytes 344096 | tf_op jit(solution)/shard_map/ppermute | solution.py:570
  29.9 13.7 %collective-permute-done.1 = bf16[64,2688]{1,0:T(8,128)(2,1)} collective-permute-done((bf16[64,2688]{1,0:T(8,128)(2,1)S(1)}, bf16[64,2688]{1,0:T(8,128)(2,1)}, u32[]{:S(2)}, u32[]{:S(2)}) %collective-permute-start.1) | collective-permute-done | bytes 344096 | tf_op jit(solution)/shard_map/ppermute | solution.py:570
  53.5 10.1 %collective-permute-start.6 = (bf16[256,2048]{1,0:T(8,128)(2,1)S(1)}, bf16[256,2048]{1,0:T(8,128)(2,1)S(1)}, u32[]{:S(2)}, u32[]{:S(2)}) collective-permute-start(bf16[256,2048]{1,0:T(8,128)(2,1)S(1)} %slice.216), channel_id=1, source_target_pairs={{0,4},{1,5},{2,6},{3,7},{4,0},{5,1},{6,2},{7,3},{8,12},{9,13},{10,... | collective-permute-start | bytes 3145736 | tf_op jit(solution)/shard_map/ppermute | solution.py:570
  63.6 75.3 %collective-permute-done.6 = bf16[256,2048]{1,0:T(8,128)(2,1)S(1)} collective-permute-done((bf16[256,2048]{1,0:T(8,128)(2,1)S(1)}, bf16[256,2048]{1,0:T(8,128)(2,1)S(1)}, u32[]{:S(2)}, u32[]{:S(2)}) %collective-permute-start.6) | collective-permute-done | bytes 1048608 | tf_op jit(solution)/shard_map/ppermute | solution.py:570
  157.2 11.7 %collective-permute-done.11 = bf16[96,2048]{1,0:T(8,128)(2,1)S(1)} collective-permute-done((bf16[96,2048]{1,0:T(8,128)(2,1)S(1)}, bf16[96,2048]{1,0:T(8,128)(2,1)S(1)}, u32[]{:S(2)}, u32[]{:S(2)}) %collective-permute-start.11) | collective-permute-done | bytes 393248 | tf_op jit(solution)/shard_map/ppermute | solution.py:570
  304.6 15.9 %ffn_gates.4 = (bf16[3,704,512]{2,1,0:T(8,128)(2,1)}, bf16[3,704,512]{2,1,0:T(8,128)(2,1)}) custom-call(bf16[512,2048]{1,0:T(8,128)(2,1)} %multiply_convert_fusion.x_ref.refs_2_, bf16[512,2048]{1,0:T(8,128)(2,1)} %refs_4_.7, bf16[1,2,704,2048]{3,2,1,0:T(8,128)(2,1)} %bitcast.211, bf16[1,1,704,2048]{3,2,1,0:T(8,128)(2,1)} %bitcast.22.refs_1_.refs_4_, ...), custom_call_target="tpu_custom_call" | custom-call | flops 8858370048 | bytes 25821184 | tf_op jit(solution)/shard_map/ffn_gates/pallas_call | solution.py:389
  323.0 16.6 %ffn_gates.5 = (bf16[3,704,512]{2,1,0:T(8,128)(2,1)}, bf16[3,704,512]{2,1,0:T(8,128)(2,1)}) custom-call(bf16[512,2048]{1,0:T(8,128)(2,1)} %multiply_convert_fusion.x_ref.refs_2_, bf16[512,2048]{1,0:T(8,128)(2,1)} %refs_4_.7, bf16[4,2,176,2048]{3,2,1,0:T(8,128)(2,1)} %bitcast.237, bf16[4,1,176,2048]{3,2,1,0:T(8,128)(2,1)} %bitcast.195, ...), custom_call_target="tpu_custom_call" | custom-call | flops 8858370048 | bytes 25821184 | tf_op jit(solution)/shard_map/ffn_gates/pallas_call | solution.py:389
  339.6 20.9 %ffn_back.4 = bf16[512,2048]{1,0:T(8,128)(2,1)} custom-call(bf16[3,704,512]{2,1,0:T(8,128)(2,1)} %get-tuple-element.368.refs_0_, bf16[3,704,512]{2,1,0:T(8,128)(2,1)} %get-tuple-element.369.refs_1_.refs_0_, bf16[3,704,512]{2,1,0:T(8,128)(2,1)} %get-tuple-element.370.refs_2_.refs_0_, bf16[3,704,512]{2,1,0:T(8,128)(2,1)} %get-tuple-element.371.refs_3_.refs_0_, ...), custom_call_target="tpu_custom_call" | custom-call | flops 11811160064 | bytes 30932992 | tf_op jit(solution)/shard_map/ffn_back/pallas_call | solution.py:443
  360.5 15.9 %ffn_gates.6 = (bf16[3,704,512]{2,1,0:T(8,128)(2,1)}, bf16[3,704,512]{2,1,0:T(8,128)(2,1)}) custom-call(bf16[512,2048]{1,0:T(8,128)(2,1)} %collective-permute-done.28.x_ref.refs_3_, bf16[512,2048]{1,0:T(8,128)(2,1)} %copy-done.89, bf16[1,2,704,2048]{3,2,1,0:T(8,128)(2,1)} %bitcast.213, bf16[1,1,704,2048]{3,2,1,0:T(8,128)(2,1)} %bitcast.22.refs_1_.refs_4_, ...), custom_call_target="tpu_custom_call" | custom-call | flops 8858370048 | bytes 25821184 | tf_op jit(solution)/shard_map/ffn_gates/pallas_call | solution.py:389
  376.4 16.8 %ffn_gates.7 = (bf16[3,704,512]{2,1,0:T(8,128)(2,1)}, bf16[3,704,512]{2,1,0:T(8,128)(2,1)}) custom-call(bf16[512,2048]{1,0:T(8,128)(2,1)} %collective-permute-done.28.x_ref.refs_3_, bf16[512,2048]{1,0:T(8,128)(2,1)} %copy-done.89, bf16[4,2,176,2048]{3,2,1,0:T(8,128)(2,1)} %bitcast.239, bf16[4,1,176,2048]{3,2,1,0:T(8,128)(2,1)} %bitcast.196, ...), custom_call_target="tpu_custom_call" | custom-call | flops 8858370048 | bytes 25821184 | tf_op jit(solution)/shard_map/ffn_gates/pallas_call | solution.py:389
  393.2 15.1 %ffn_grad.4 = bf16[4,3,176,2048]{3,2,1,0:T(8,128)(2,1)} custom-call(bf16[3,704,512]{2,1,0:T(8,128)(2,1)} %get-tuple-element.371.refs_3_.refs_0_, bf16[3,704,512]{2,1,0:T(8,128)(2,1)} %get-tuple-element.344.refs_1_.refs_3_, bf16[512,2048]{1,0:T(8,128)(2,1)} %multiply_convert_fusion.x_ref.refs_2_, bf16[512,2048]{1,0:T(8,128)(2,1)} %collective-permute-done.28.x_ref.refs_3_, ...), custom_call_target="tpu_custom_call" | custom-call | flops 8858370048 | bytes 21364736 | tf_op jit(solution)/shard_map/ffn_grad/pallas_call | solution.py:493
  408.3 20.9 %ffn_back.5 = bf16[512,2048]{1,0:T(8,128)(2,1)} custom-call(bf16[3,704,512]{2,1,0:T(8,128)(2,1)} %get-tuple-element.341.refs_0_.refs_1_, bf16[3,704,512]{2,1,0:T(8,128)(2,1)} %get-tuple-element.342.refs_1_, bf16[3,704,512]{2,1,0:T(8,128)(2,1)} %get-tuple-element.343.refs_2_.refs_1_, bf16[3,704,512]{2,1,0:T(8,128)(2,1)} %get-tuple-element.344.refs_1_.refs_3_, ...), custom_call_target="tpu_custom_call" | custom-call | flops 11811160064 | bytes 30932992 | tf_op jit(solution)/shard_map/ffn_back/pallas_call | solution.py:443
  431.1 15.0 %ffn_grad.5 = bf16[4,3,176,2048]{3,2,1,0:T(8,128)(2,1)} custom-call(bf16[3,704,512]{2,1,0:T(8,128)(2,1)} %get-tuple-element.369.refs_1_.refs_0_, bf16[3,704,512]{2,1,0:T(8,128)(2,1)} %get-tuple-element.342.refs_1_, bf16[512,2048]{1,0:T(8,128)(2,1)} %multiply_convert_fusion.x_ref.refs_2_, bf16[512,2048]{1,0:T(8,128)(2,1)} %collective-permute-done.28.x_ref.refs_3_, ...), custom_call_target="tpu_custom_call" | custom-call | flops 8858370048 | bytes 21364736 | tf_op jit(solution)/shard_map/ffn_grad/pallas_call | solution.py:493
  450.0 16.6 %ffn_grad.6 = bf16[4,3,176,2048]{3,2,1,0:T(8,128)(2,1)} custom-call(bf16[3,704,512]{2,1,0:T(8,128)(2,1)} %get-tuple-element.370.refs_2_.refs_0_, bf16[3,704,512]{2,1,0:T(8,128)(2,1)} %get-tuple-element.343.refs_2_.refs_1_, bf16[512,2048]{1,0:T(8,128)(2,1)} %multiply_convert_fusion.x_ref.refs_2_, bf16[512,2048]{1,0:T(8,128)(2,1)} %collective-permute-done.28.x_ref.refs_3_, ...), custom_call_target="tpu_custom_call" | custom-call | flops 8858370048 | bytes 30015488 | tf_op jit(solution)/shard_map/ffn_grad/pallas_call | solution.py:493
  468.7 16.8 %ffn_grad.7 = bf16[4,3,176,2048]{3,2,1,0:T(8,128)(2,1)} custom-call(bf16[3,704,512]{2,1,0:T(8,128)(2,1)} %get-tuple-element.368.refs_0_, bf16[3,704,512]{2,1,0:T(8,128)(2,1)} %get-tuple-element.341.refs_0_.refs_1_, bf16[512,2048]{1,0:T(8,128)(2,1)} %multiply_convert_fusion.x_ref.refs_2_, bf16[512,2048]{1,0:T(8,128)(2,1)} %collective-permute-done.28.x_ref.refs_3_, ...), custom_call_target="tpu_custom_call" | custom-call | flops 8858370048 | bytes 30015488 | tf_op jit(solution)/shard_map/ffn_grad/pallas_call | solution.py:493
  538.5 20.8 %mix_local_grad.1 = (bf16[512,256]{1,0:T(8,128)(2,1)S(1)}, f32[512,256]{1,0:T(8,128)S(1)}, f32[512,2048]{1,0:T(8,128)}) custom-call(bf16[512,256]{1,0:T(8,128)(2,1)S(1)} %get-tuple-element.315.q_ref, bf16[512,256]{1,0:T(8,128)(2,1)S(1)} %get-tuple-element.327.k_ref, bf16[512,2048]{1,0:T(8,128)(2,1)S(1)} %slice.179.v_ref, bf16[512,2048]{1,0:T(8,128)(2,1)} %copy-done.5, ...), custom_call_target="tpu_custom_call" | custom-call | flops 1048576 | bytes 65536 | tf_op jit(solution)/shard_map/mix_local_grad/pallas_call | solution.py:319
  580.4 10.2 %mix_later_grad.1 = (bf16[512,256]{1,0:T(8,128)(2,1)S(1)}, bf16[512,2048]{1,0:T(8,128)(2,1)S(1)}) custom-call(bf16[512,256]{1,0:T(8,128)(2,1)S(1)} %get-tuple-element.327.k_ref, bf16[512,2048]{1,0:T(8,128)(2,1)} %copy-done, f32[512,256]{1,0:T(8,128)S(1)} %copy-done.13, f32[512,2048]{1,0:T(8,128)} %get-tuple-element.329.gv_in_ref, ...), custom_call_target="tpu_custom_call" | custom-call | flops 1048576 | bytes 65536 | tf_op jit(solution)/shard_map/mix_later_grad/pallas_call | solution.py:328
  609.4 11.4 %qkv_grad.1 = bf16[2048,2560]{1,0:T(8,128)(2,1)} custom-call(bf16[512,2048]{1,0:T(8,128)(2,1)} %copy-done.51, bf16[512,256]{1,0:T(8,128)(2,1)} %copy-done.14, bf16[512,256]{1,0:T(8,128)(2,1)} %copy-done.16, bf16[512,2048]{1,0:T(8,128)(2,1)} %copy-done.18), custom_call_target="tpu_custom_call" | custom-call | flops 5368709120 | bytes 15204352 | tf_op jit(solution)/shard_map/qkv_grad/pallas_call | solution.py:539
  643.1 12.7 %ffn_back.6 = bf16[512,2048]{1,0:T(8,128)(2,1)} custom-call(bf16[3,704,512]{2,1,0:T(8,128)(2,1)} %get-tuple-element.341.refs_0_.refs_1_, bf16[3,704,512]{2,1,0:T(8,128)(2,1)} %get-tuple-element.342.refs_1_, bf16[3,704,512]{2,1,0:T(8,128)(2,1)} %get-tuple-element.343.refs_2_.refs_1_, bf16[3,704,512]{2,1,0:T(8,128)(2,1)} %get-tuple-element.344.refs_1_.refs_3_, ...), custom_call_target="tpu_custom_call" | custom-call | flops 5905580032 | bytes 16515072 | tf_op jit(solution)/shard_map/ffn_back/pallas_call | solution.py:443
  714.0 26.5 %collective-permute-done.57 = bf16[176,2048]{1,0:T(8,128)(2,1)S(1)} collective-permute-done((bf16[176,2048]{1,0:T(8,128)(2,1)S(1)}, bf16[176,2048]{1,0:T(8,128)(2,1)S(1)}, u32[]{:S(2)}, u32[]{:S(2)}) %collective-permute-start.57) | collective-permute-done | bytes 720928 | tf_op jit(solution)/shard_map/ppermute | solution.py:570
  773.1 14.6 %collective-permute-start.67 = (bf16[64,2048]{1,0:T(8,128)(2,1)}, bf16[64,2048]{1,0:T(8,128)(2,1)}, u32[]{:S(2)}, u32[]{:S(2)}) collective-permute-start(bf16[64,2048]{1,0:T(8,128)(2,1)} %get-tuple-element.413), channel_id=1, source_target_pairs={{0,2},{1,3},{2,0},{3,1},{4,6},{5,7},{6,4},{7,5},{8,10},{9,11},{10,... | collective-permute-start | bytes 786440 | tf_op jit(solution)/shard_map/ppermute | solution.py:570
  787.7 14.9 %collective-permute-done.59 = bf16[64,2560]{1,0:T(8,128)(2,1)S(1)} collective-permute-done((bf16[64,2560]{1,0:T(8,128)(2,1)S(1)}, bf16[64,2560]{1,0:T(8,128)(2,1)S(1)}, u32[]{:S(2)}, u32[]{:S(2)}) %collective-permute-start.59) | collective-permute-done | bytes 327712 | tf_op jit(solution)/shard_map/ppermute | solution.py:570
  804.7 12.1 %ffn_back.7 = bf16[512,2048]{1,0:T(8,128)(2,1)} custom-call(bf16[3,704,512]{2,1,0:T(8,128)(2,1)} %get-tuple-element.368.refs_0_, bf16[3,704,512]{2,1,0:T(8,128)(2,1)} %get-tuple-element.369.refs_1_.refs_0_, bf16[3,704,512]{2,1,0:T(8,128)(2,1)} %get-tuple-element.370.refs_2_.refs_0_, bf16[3,704,512]{2,1,0:T(8,128)(2,1)} %get-tuple-element.371.refs_3_.refs_0_, ...), custom_call_target="tpu_custom_call" | custom-call | flops 5905580032 | bytes 16515072 | tf_op jit(solution)/shard_map/ffn_back/pallas_call | solution.py:443
  821.3 18.1 %collective-permute-done.66 = bf16[320,2048]{1,0:T(8,128)(2,1)} collective-permute-done((bf16[320,2048]{1,0:T(8,128)(2,1)}, bf16[320,2048]{1,0:T(8,128)(2,1)}, u32[]{:S(2)}, u32[]{:S(2)}) %collective-permute-start.66) | collective-permute-done | bytes 1310752 | tf_op jit(solution)/shard_map/ppermute | solution.py:570
  (473 shorter events, 408.0 us)
Async XLA Ops:
  7.2 193.9 %all-gather.5.cloned.1.call-start = ((), (), s32[]{:S(2)}) async-start(), calls=%async_computation.2 | async-start | bytes 8650752 | tf_op jit(solution)/shard_map/all_gather | solution.py:758
  7.9 294.8 %all-gather.7.cloned.1.call-start = ((), (), s32[]{:S(2)}) async-start(), calls=%async_computation.3 | async-start | bytes 7208960 | tf_op jit(solution)/shard_map/all_gather | solution.py:793
  46.8 92.1 %collective-permute-start.3 = (bf16[4,64,2688]{2,1,0:T(8,128)(2,1)S(1)}, bf16[4,64,2688]{2,1,0:T(8,128)(2,1)}, u32[]{:S(2)}, u32[]{:S(2)}) collective-permute-start(bf16[4,64,2688]{2,1,0:T(8,128)(2,1)S(1)} %bitcast_dynamic-update-slice_fusion), channel_id=1, source_target_pairs={{0,8},{8,0},{16,24},{24,16},{1,9},{9,1},{17,25},{25,17},{2,10},{10... | collective-permute-start | bytes 4128776 | tf_op jit(solution)/shard_map/ppermute | solution.py:570
  48.4 90.5 %collective-permute-start.4 = (bf16[4,64,2688]{2,1,0:T(8,128)(2,1)S(1)}, bf16[4,64,2688]{2,1,0:T(8,128)(2,1)}, u32[]{:S(2)}, u32[]{:S(2)}) collective-permute-start(bf16[4,64,2688]{2,1,0:T(8,128)(2,1)S(1)} %bitcast_dynamic-update-slice_fusion), channel_id=1, source_target_pairs={{0,16},{8,24},{16,0},{24,8},{1,17},{9,25},{17,1},{25,9},{2,18},{10... | collective-permute-start | bytes 4128776 | tf_op jit(solution)/shard_map/ppermute | solution.py:570
  49.9 89.0 %collective-permute-start.5 = (bf16[4,64,2688]{2,1,0:T(8,128)(2,1)S(1)}, bf16[4,64,2688]{2,1,0:T(8,128)(2,1)S(1)}, u32[]{:S(2)}, u32[]{:S(2)}) collective-permute-start(bf16[4,64,2688]{2,1,0:T(8,128)(2,1)S(1)} %bitcast_dynamic-update-slice_fusion), channel_id=1, source_target_pairs={{0,1},{1,0},{2,3},{3,2},{4,5},{5,4},{6,7},{7,6},{8,9},{9,8},{10,11... | collective-permute-start | bytes 4128776 | tf_op jit(solution)/shard_map/ppermute | solution.py:570
  53.5 85.4 %collective-permute-start.6 = (bf16[256,2048]{1,0:T(8,128)(2,1)S(1)}, bf16[256,2048]{1,0:T(8,128)(2,1)S(1)}, u32[]{:S(2)}, u32[]{:S(2)}) collective-permute-start(bf16[256,2048]{1,0:T(8,128)(2,1)S(1)} %slice.216), channel_id=1, source_target_pairs={{0,4},{1,5},{2,6},{3,7},{4,0},{5,1},{6,2},{7,3},{8,12},{9,13},{10,... | collective-permute-start | bytes 3145736 | tf_op jit(solution)/shard_map/ppermute | solution.py:570
  138.9 30.0 %collective-permute-start.9 = (bf16[4,64,2688]{2,1,0:T(8,128)(2,1)}, bf16[4,64,2688]{2,1,0:T(8,128)(2,1)}, u32[]{:S(2)}, u32[]{:S(2)}) collective-permute-start(bf16[4,64,2688]{2,1,0:T(8,128)(2,1)} %collective-permute-done.3), channel_id=1, source_target_pairs={{0,1},{1,0},{2,3},{3,2},{4,5},{5,4},{6,7},{7,6},{8,9},{9,8},{10,11... | collective-permute-start | bytes 4128776 | tf_op jit(solution)/shard_map/ppermute | solution.py:570
  168.9 32.1 %collective-permute-start.15 = (bf16[1,1,704,2048]{3,2,1,0:T(8,128)(2,1)}, bf16[1,1,704,2048]{3,2,1,0:T(8,128)(2,1)}, u32[]{:S(2)}, u32[]{:S(2)}) collective-permute-start(bf16[1,1,704,2048]{3,2,1,0:T(8,128)(2,1)} %bitcast.22.refs_1_.refs_4_), channel_id=1, source_target_pairs={{0,1},{1,0},{2,3},{3,2},{4,5},{5,4},{6,7},{7,6},{8,9},{9,8},{10,11... | collective-permute-start | bytes 8650760 | tf_op jit(solution)/shard_map/ppermute | solution.py:570
  173.4 129.3 %all-gather.9.cloned.1.call-start = ((), (), s32[]{:S(2)}) async-start(), calls=%async_computation.4 | async-start | bytes 3604480 | tf_op jit(solution)/shard_map/all_gather | solution.py:844
  245.8 323.4 %reduce-scatter.3.cloned.1.call-start = ((), (), s32[]{:S(2)}) async-start(), calls=%async_computation.5 | async-start | bytes 10813440 | tf_op jit(solution)/shard_map/reduce_scatter | solution.py:904
  303.3 57.2 %collective-permute-start.28 = (bf16[512,2048]{1,0:T(8,128)(2,1)}, bf16[512,2048]{1,0:T(8,128)(2,1)}, u32[]{:S(2)}, u32[]{:S(2)}) collective-permute-start(bf16[512,2048]{1,0:T(8,128)(2,1)} %multiply_convert_fusion.x_ref.refs_2_), channel_id=1, source_target_pairs={{0,2},{1,3},{2,0},{3,1},{4,6},{5,7},{6,4},{7,5},{8,10},{9,11},{10,... | collective-permute-start | bytes 6291464 | tf_op jit(solution)/shard_map/ppermute | solution.py:570
  408.3 41.8 %collective-permute-start.33 = (bf16[4,3,176,2048]{3,2,1,0:T(8,128)(2,1)}, bf16[4,3,176,2048]{3,2,1,0:T(8,128)(2,1)}, u32[]{:S(2)}, u32[]{:S(2)}) collective-permute-start(bf16[4,3,176,2048]{3,2,1,0:T(8,128)(2,1)} %ffn_grad.4), channel_id=1, source_target_pairs={{0,1},{1,0},{2,3},{3,2},{4,5},{5,4},{6,7},{7,6},{8,9},{9,8},{10,11... | collective-permute-start | bytes 25952264 | tf_op jit(solution)/shard_map/ppermute | solution.py:570
  467.2 274.3 %reduce-scatter.5.cloned.1.call-start = ((), (), s32[]{:S(2)}) async-start(), calls=%async_computation.6 | async-start | bytes 10813440 | tf_op jit(solution)/shard_map/reduce_scatter | solution.py:904
  535.4 307.8 %all-gather.11.cloned.1.call-start = ((), (), s32[]{:S(2)}) async-start(), calls=%async_computation.7 | async-start | bytes 10813440 | tf_op jit(solution)/shard_map/all_gather | solution.py:1043
  633.2 31.1 %collective-permute-start.47 = (bf16[4,4,64,2560]{3,2,1,0:T(8,128)(2,1)}, bf16[4,4,64,2560]{3,2,1,0:T(8,128)(2,1)}, u32[]{:S(2)}, u32[]{:S(2)}) collective-permute-start(bf16[4,4,64,2560]{3,2,1,0:T(8,128)(2,1)} %dynamic-slice_bitcast_fusion), channel_id=1, source_target_pairs={{0,1},{1,0},{2,3},{3,2},{4,5},{5,4},{6,7},{7,6},{8,9},{9,8},{10,11... | collective-permute-start | bytes 15728648 | tf_op jit(solution)/shard_map/ppermute | solution.py:570
  702.9 37.6 %collective-permute-start.55 = (bf16[4,64,2560]{2,1,0:T(8,128)(2,1)S(1)}, bf16[4,64,2560]{2,1,0:T(8,128)(2,1)}, u32[]{:S(2)}, u32[]{:S(2)}) collective-permute-start(bf16[4,64,2560]{2,1,0:T(8,128)(2,1)S(1)} %pad_maximum_fusion.3), channel_id=1, source_target_pairs={{0,8},{8,0},{16,24},{24,16},{1,9},{9,1},{17,25},{25,17},{2,10},{10... | collective-permute-start | bytes 3932168 | tf_op jit(solution)/shard_map/ppermute | solution.py:570
  705.7 34.8 %collective-permute-start.56 = (bf16[4,64,2560]{2,1,0:T(8,128)(2,1)S(1)}, bf16[4,64,2560]{2,1,0:T(8,128)(2,1)}, u32[]{:S(2)}, u32[]{:S(2)}) collective-permute-start(bf16[4,64,2560]{2,1,0:T(8,128)(2,1)S(1)} %pad_maximum_fusion.4), channel_id=1, source_target_pairs={{0,16},{8,24},{16,0},{24,8},{1,17},{9,25},{17,1},{25,9},{2,18},{10... | collective-permute-start | bytes 3932168 | tf_op jit(solution)/shard_map/ppermute | solution.py:570
  707.2 33.3 %collective-permute-start.57 = (bf16[176,2048]{1,0:T(8,128)(2,1)S(1)}, bf16[176,2048]{1,0:T(8,128)(2,1)S(1)}, u32[]{:S(2)}, u32[]{:S(2)}) collective-permute-start(bf16[176,2048]{1,0:T(8,128)(2,1)S(1)} %copy-done.60), channel_id=1, source_target_pairs={{0,4},{1,5},{2,6},{3,7},{4,0},{5,1},{6,2},{7,3},{8,12},{9,13},{10,... | collective-permute-start | bytes 2162696 | tf_op jit(solution)/shard_map/ppermute | solution.py:570
  764.1 38.5 %collective-permute-start.59 = (bf16[64,2560]{1,0:T(8,128)(2,1)S(1)}, bf16[64,2560]{1,0:T(8,128)(2,1)S(1)}, u32[]{:S(2)}, u32[]{:S(2)}) collective-permute-start(bf16[64,2560]{1,0:T(8,128)(2,1)S(1)} %get-tuple-element.401), channel_id=1, source_target_pairs={{0,4},{1,5},{2,6},{3,7},{4,0},{5,1},{6,2},{7,3},{8,12},{9,13},{10,... | collective-permute-start | bytes 983048 | tf_op jit(solution)/shard_map/ppermute | solution.py:570
  764.2 38.5 %collective-permute-start.58 = (bf16[64,2560]{1,0:T(8,128)(2,1)S(1)}, bf16[64,2560]{1,0:T(8,128)(2,1)S(1)}, u32[]{:S(2)}, u32[]{:S(2)}) collective-permute-start(bf16[64,2560]{1,0:T(8,128)(2,1)S(1)} %get-tuple-element.399), channel_id=1, source_target_pairs={{0,2},{1,3},{2,0},{3,1},{4,6},{5,7},{6,4},{7,5},{8,10},{9,11},{10,... | collective-permute-start | bytes 983048 | tf_op jit(solution)/shard_map/ppermute | solution.py:570
  767.6 49.7 %collective-permute-start.69 = (bf16[64,2048]{1,0:T(8,128)(2,1)}, bf16[64,2048]{1,0:T(8,128)(2,1)S(1)}, u32[]{:S(2)}, u32[]{:S(2)}) collective-permute-start(bf16[64,2048]{1,0:T(8,128)(2,1)} %get-tuple-element.414), channel_id=1, source_target_pairs={{0,6},{1,7},{2,4},{3,5},{4,2},{5,3},{6,0},{7,1},{8,14},{9,15},{10,... | collective-permute-start | bytes 786440 | tf_op jit(solution)/shard_map/ppermute | solution.py:570
  771.2 46.2 %collective-permute-start.68 = (bf16[64,2048]{1,0:T(8,128)(2,1)}, bf16[64,2048]{1,0:T(8,128)(2,1)}, u32[]{:S(2)}, u32[]{:S(2)}) collective-permute-start(bf16[64,2048]{1,0:T(8,128)(2,1)} %get-tuple-element.415), channel_id=1, source_target_pairs={{0,4},{1,5},{2,6},{3,7},{4,0},{5,1},{6,2},{7,3},{8,12},{9,13},{10,... | collective-permute-start | bytes 786440 | tf_op jit(solution)/shard_map/ppermute | solution.py:570
  773.1 44.3 %collective-permute-start.67 = (bf16[64,2048]{1,0:T(8,128)(2,1)}, bf16[64,2048]{1,0:T(8,128)(2,1)}, u32[]{:S(2)}, u32[]{:S(2)}) collective-permute-start(bf16[64,2048]{1,0:T(8,128)(2,1)} %get-tuple-element.413), channel_id=1, source_target_pairs={{0,2},{1,3},{2,0},{3,1},{4,6},{5,7},{6,4},{7,5},{8,10},{9,11},{10,... | collective-permute-start | bytes 786440 | tf_op jit(solution)/shard_map/ppermute | solution.py:570
  804.2 35.2 %collective-permute-start.66 = (bf16[320,2048]{1,0:T(8,128)(2,1)}, bf16[320,2048]{1,0:T(8,128)(2,1)}, u32[]{:S(2)}, u32[]{:S(2)}) collective-permute-start(bf16[320,2048]{1,0:T(8,128)(2,1)} %bitcast.84), channel_id=1, source_target_pairs={{0,2},{1,3},{2,0},{3,1},{4,6},{5,7},{6,4},{7,5},{8,10},{9,11},{10,... | collective-permute-start | bytes 3932168 | tf_op jit(solution)/shard_map/ppermute | solution.py:570
  (151 other events, 2415.5 us)
Sparse Core Ops, SparseCore 0:
  11.0 129.7 all-gather.4
  173.6 66.0 all-gather.6
  245.9 40.3 all-gather.8
  467.3 90.2 reduce-scatter.2
  560.6 114.9 reduce-scatter.4
  746.2 90.9 all-gather.10

commit v5 on v4

--- a/solution.py
+++ b/solution.py
@@ -963,7 +963,7 @@
     grad_queries, part_keys, part_values = local
     out_kept = add(out_halves[0], out_came)
     out_kept, far_part = then((out_kept, far_part), later)
-    ends = [far_part.shape[0] * n // 33 for n in (0, 3, 9, 16, 22, 33)]
+    ends = [far_part.shape[0] * n // 33 for n in (0, 6, 13, 17, 23, 33)]
     far_shares = [far_part[a:b] for a, b in zip(ends, ends[1:])]
     out_first, out_second, out_diag = [pick(out_kept, group ^ step) for step in range(1, groups)]
     low, high = slice(None, half_chips), slice(half_chips, None)
@@ -1014,7 +1014,9 @@
         + mul(grad_keys, full_qkv[:, qk : 2 * qk], "nt")
         + mul(grad_values, full_qkv[:, 2 * qk :], "nt")
     )
-    out_split = jnp.split(stacked(out_parts), [rows * 3 // 8], axis=0)
+    out_split = jnp.split(
+        stacked(out_parts), [rows * 3 // 16, rows * 13 // 32], axis=0
+    )
     out_early, for_second, for_first, far_third, grad_normed_one, in_first, in_second = (
         lax.optimization_barrier(
             (
@@ -1035,8 +1037,9 @@
     grad_normed_one = then(grad_normed_one, (in_first, in_second))
     grad_one, gain_one_grad = norm_backward(grad_normed_one, unit_one, inverse_one, gain_one)
     input_grad = (grad_hidden_in + grad_one).astype(bf)
-    input_grad, gain_one_grad, in_moved, far_last = lax.optimization_barrier(
-        (input_grad, gain_one_grad, in_moved, far_last)
+    out_middle = to_owners(then(out_split[1], (in_first, in_second)))
+    out_middle, input_grad, gain_one_grad, in_moved, far_last = lax.optimization_barrier(
+        (out_middle, input_grad, gain_one_grad, in_moved, far_last)
     )
     out_own = back(made[0], 1, in_moved)
     far_sum = jnp.concatenate([far_first, far_slot, far_second, far_third, far_last], axis=0)
@@ -1062,8 +1065,8 @@
     gain_sums = lax.dynamic_slice_in_dim(
         gain_sums, (group * size + place) * own_rows, own_rows, 1
     )
-    out_last = to_owners(then(out_split[1], in_sum, gain_sums))
-    out_sent = jnp.concatenate([out_early, out_last], axis=0)
+    out_last = to_owners(then(out_split[2], in_sum, gain_sums))
+    out_sent = jnp.concatenate([out_early, out_middle, out_last], axis=0)
     output = (hidden_in + jnp.sum(out_sent.astype(f32), axis=1) + out_own.astype(f32)).astype(bf)
     return (
         output,

time: 866 us -> 850 us (0.982)
  waiting for transfers between devices: 231 us -> 221 us
    ppermute x70 -> x71, waiting for transfers between devices: 230 us -> 220 us  [move(): lax.ppermute(array, axis, [(m, t) for m, t in pairs if t is not None])]
    unnamed x207 -> x193, local copies, waits for them, and re-layouts: 26.1 us -> 22.3 us
    ppermute x70 -> x71, starting transfers between devices: 110 us -> 111 us  [move(): lax.ppermute(array, axis, [(m, t) for m, t in pairs if t is not None])]
  transfers between devices with their start and end apart: 76 -> 77, of which waited for: 30 -> 28; matrix products, arithmetic and copies ran while one was open for 23% -> 23% of each run, Pallas kernels for 26% -> 26%
where the time goes in v5:
time: 850 us; the launch traced here: 844 us
  Pallas kernels  279 us (33%)
  waiting for transfers between devices  221 us (26%)
  starting transfers between devices  112 us (13%)
  other arithmetic  92 us (11%)
  local copies, waits for them, and re-layouts  73.6 us (9%)
  matrix products  50.2 us (6%)
  between operations  15.8 us (2%)
    ppermute x71, waiting for transfers between devices, move(): lax.ppermute(array, axis, [(m, t) for m, t in pairs if t is not None])  220 us
    ppermute x71, starting transfers between devices, move(): lax.ppermute(array, axis, [(m, t) for m, t in pairs if t is not None])  111 us
    pallas_call x4, Pallas kernels, ffn_back(): pl.pallas_call(functools.partial(back_kernel, count), grid=(D // columns,...  66.5 us
    pallas_call x4, Pallas kernels, ffn_gates(): pl.pallas_call(gate_kernel, grid=(steps,), in_specs=ins, out_specs=outs,...  65 us
    pallas_call x4, Pallas kernels, ffn_grad(): pl.pallas_call(functools.partial(grad_kernel, blocks), grid=(3, steps), i...  63.6 us
    dot_general x7, matrix products, mul(): lax.dot_general(left, right, (dims, ((), ())), preferred_element_type=jnp...  50.2 us
    unnamed x193, local copies, waits for them, and re-layouts  22.3 us
    convert_element_type x8, other arithmetic, add(): return total.astype(kept)  21.7 us
  transfers between devices with their start and end apart: 77, of which 28 were waited for; matrix products, arithmetic and copies ran while one was open for 23% of the time, Pallas kernels for 26%

profile of v5, /device:TPU:0, one launch (start us, length us, event | category | flops | bytes accessed | tf_op | source)
XLA Modules:
  0.0 843.9 jit_solution(4935685917883525344)
XLA Ops:
  16.3 13.6 %collective-permute-done = bf16[64,2688]{1,0:T(8,128)(2,1)} collective-permute-done((bf16[64,2688]{1,0:T(8,128)(2,1)S(1)}, bf16[64,2688]{1,0:T(8,128)(2,1)}, u32[]{:S(2)}, u32[]{:S(2)}) %collective-permute-start) | collective-permute-done | bytes 344096 | tf_op jit(solution)/shard_map/ppermute | solution.py:570
  29.9 13.7 %collective-permute-done.1 = bf16[64,2688]{1,0:T(8,128)(2,1)} collective-permute-done((bf16[64,2688]{1,0:T(8,128)(2,1)S(1)}, bf16[64,2688]{1,0:T(8,128)(2,1)}, u32[]{:S(2)}, u32[]{:S(2)}) %collective-permute-start.1) | collective-permute-done | bytes 344096 | tf_op jit(solution)/shard_map/ppermute | solution.py:570
  53.5 10.1 %collective-permute-start.6 = (bf16[256,2048]{1,0:T(8,128)(2,1)S(1)}, bf16[256,2048]{1,0:T(8,128)(2,1)S(1)}, u32[]{:S(2)}, u32[]{:S(2)}) collective-permute-start(bf16[256,2048]{1,0:T(8,128)(2,1)S(1)} %slice.217), channel_id=1, source_target_pairs={{0,4},{1,5},{2,6},{3,7},{4,0},{5,1},{6,2},{7,3},{8,12},{9,13},{10,... | collective-permute-start | bytes 3145736 | tf_op jit(solution)/shard_map/ppermute | solution.py:570
  63.6 75.3 %collective-permute-done.6 = bf16[256,2048]{1,0:T(8,128)(2,1)S(1)} collective-permute-done((bf16[256,2048]{1,0:T(8,128)(2,1)S(1)}, bf16[256,2048]{1,0:T(8,128)(2,1)S(1)}, u32[]{:S(2)}, u32[]{:S(2)}) %collective-permute-start.6) | collective-permute-done | bytes 1048608 | tf_op jit(solution)/shard_map/ppermute | solution.py:570
  157.2 11.7 %collective-permute-done.11 = bf16[96,2048]{1,0:T(8,128)(2,1)S(1)} collective-permute-done((bf16[96,2048]{1,0:T(8,128)(2,1)S(1)}, bf16[96,2048]{1,0:T(8,128)(2,1)S(1)}, u32[]{:S(2)}, u32[]{:S(2)}) %collective-permute-start.11) | collective-permute-done | bytes 393248 | tf_op jit(solution)/shard_map/ppermute | solution.py:570
  304.5 15.8 %ffn_gates.4 = (bf16[3,704,512]{2,1,0:T(8,128)(2,1)}, bf16[3,704,512]{2,1,0:T(8,128)(2,1)}) custom-call(bf16[512,2048]{1,0:T(8,128)(2,1)} %multiply_convert_fusion.x_ref.refs_2_, bf16[512,2048]{1,0:T(8,128)(2,1)} %refs_4_.7, bf16[1,2,704,2048]{3,2,1,0:T(8,128)(2,1)} %bitcast.214, bf16[1,1,704,2048]{3,2,1,0:T(8,128)(2,1)} %bitcast.22.refs_1_.refs_4_, ...), custom_call_target="tpu_custom_call" | custom-call | flops 8858370048 | bytes 25821184 | tf_op jit(solution)/shard_map/ffn_gates/pallas_call | solution.py:389
  322.8 16.5 %ffn_gates.5 = (bf16[3,704,512]{2,1,0:T(8,128)(2,1)}, bf16[3,704,512]{2,1,0:T(8,128)(2,1)}) custom-call(bf16[512,2048]{1,0:T(8,128)(2,1)} %multiply_convert_fusion.x_ref.refs_2_, bf16[512,2048]{1,0:T(8,128)(2,1)} %refs_4_.7, bf16[4,2,176,2048]{3,2,1,0:T(8,128)(2,1)} %bitcast.242, bf16[4,1,176,2048]{3,2,1,0:T(8,128)(2,1)} %bitcast.198, ...), custom_call_target="tpu_custom_call" | custom-call | flops 8858370048 | bytes 25821184 | tf_op jit(solution)/shard_map/ffn_gates/pallas_call | solution.py:389
  339.3 20.9 %ffn_back.4 = bf16[512,2048]{1,0:T(8,128)(2,1)} custom-call(bf16[3,704,512]{2,1,0:T(8,128)(2,1)} %get-tuple-element.372.refs_0_, bf16[3,704,512]{2,1,0:T(8,128)(2,1)} %get-tuple-element.373.refs_1_.refs_0_, bf16[3,704,512]{2,1,0:T(8,128)(2,1)} %get-tuple-element.374.refs_2_.refs_0_, bf16[3,704,512]{2,1,0:T(8,128)(2,1)} %get-tuple-element.375.refs_3_.refs_0_, ...), custom_call_target="tpu_custom_call" | custom-call | flops 11811160064 | bytes 30932992 | tf_op jit(solution)/shard_map/ffn_back/pallas_call | solution.py:443
  360.3 15.9 %ffn_gates.6 = (bf16[3,704,512]{2,1,0:T(8,128)(2,1)}, bf16[3,704,512]{2,1,0:T(8,128)(2,1)}) custom-call(bf16[512,2048]{1,0:T(8,128)(2,1)} %collective-permute-done.28.x_ref.refs_3_, bf16[512,2048]{1,0:T(8,128)(2,1)} %copy-done.85, bf16[1,2,704,2048]{3,2,1,0:T(8,128)(2,1)} %bitcast.216, bf16[1,1,704,2048]{3,2,1,0:T(8,128)(2,1)} %bitcast.22.refs_1_.refs_4_, ...), custom_call_target="tpu_custom_call" | custom-call | flops 8858370048 | bytes 25821184 | tf_op jit(solution)/shard_map/ffn_gates/pallas_call | solution.py:389
  376.2 16.8 %ffn_gates.7 = (bf16[3,704,512]{2,1,0:T(8,128)(2,1)}, bf16[3,704,512]{2,1,0:T(8,128)(2,1)}) custom-call(bf16[512,2048]{1,0:T(8,128)(2,1)} %collective-permute-done.28.x_ref.refs_3_, bf16[512,2048]{1,0:T(8,128)(2,1)} %copy-done.85, bf16[4,2,176,2048]{3,2,1,0:T(8,128)(2,1)} %bitcast.244, bf16[4,1,176,2048]{3,2,1,0:T(8,128)(2,1)} %bitcast.199, ...), custom_call_target="tpu_custom_call" | custom-call | flops 8858370048 | bytes 25821184 | tf_op jit(solution)/shard_map/ffn_gates/pallas_call | solution.py:389
  393.0 15.1 %ffn_grad.4 = bf16[4,3,176,2048]{3,2,1,0:T(8,128)(2,1)} custom-call(bf16[3,704,512]{2,1,0:T(8,128)(2,1)} %get-tuple-element.375.refs_3_.refs_0_, bf16[3,704,512]{2,1,0:T(8,128)(2,1)} %get-tuple-element.346.refs_1_.refs_3_, bf16[512,2048]{1,0:T(8,128)(2,1)} %multiply_convert_fusion.x_ref.refs_2_, bf16[512,2048]{1,0:T(8,128)(2,1)} %collective-permute-done.28.x_ref.refs_3_, ...), custom_call_target="tpu_custom_call" | custom-call | flops 8858370048 | bytes 21364736 | tf_op jit(solution)/shard_map/ffn_grad/pallas_call | solution.py:493
  408.1 20.9 %ffn_back.5 = bf16[512,2048]{1,0:T(8,128)(2,1)} custom-call(bf16[3,704,512]{2,1,0:T(8,128)(2,1)} %get-tuple-element.343.refs_0_.refs_1_, bf16[3,704,512]{2,1,0:T(8,128)(2,1)} %get-tuple-element.344.refs_1_, bf16[3,704,512]{2,1,0:T(8,128)(2,1)} %get-tuple-element.345.refs_2_.refs_1_, bf16[3,704,512]{2,1,0:T(8,128)(2,1)} %get-tuple-element.346.refs_1_.refs_3_, ...), custom_call_target="tpu_custom_call" | custom-call | flops 11811160064 | bytes 30932992 | tf_op jit(solution)/shard_map/ffn_back/pallas_call | solution.py:443
  430.9 15.0 %ffn_grad.5 = bf16[4,3,176,2048]{3,2,1,0:T(8,128)(2,1)} custom-call(bf16[3,704,512]{2,1,0:T(8,128)(2,1)} %get-tuple-element.373.refs_1_.refs_0_, bf16[3,704,512]{2,1,0:T(8,128)(2,1)} %get-tuple-element.344.refs_1_, bf16[512,2048]{1,0:T(8,128)(2,1)} %multiply_convert_fusion.x_ref.refs_2_, bf16[512,2048]{1,0:T(8,128)(2,1)} %collective-permute-done.28.x_ref.refs_3_, ...), custom_call_target="tpu_custom_call" | custom-call | flops 8858370048 | bytes 21364736 | tf_op jit(solution)/shard_map/ffn_grad/pallas_call | solution.py:493
  449.8 16.6 %ffn_grad.6 = bf16[4,3,176,2048]{3,2,1,0:T(8,128)(2,1)} custom-call(bf16[3,704,512]{2,1,0:T(8,128)(2,1)} %get-tuple-element.374.refs_2_.refs_0_, bf16[3,704,512]{2,1,0:T(8,128)(2,1)} %get-tuple-element.345.refs_2_.refs_1_, bf16[512,2048]{1,0:T(8,128)(2,1)} %multiply_convert_fusion.x_ref.refs_2_, bf16[512,2048]{1,0:T(8,128)(2,1)} %collective-permute-done.28.x_ref.refs_3_, ...), custom_call_target="tpu_custom_call" | custom-call | flops 8858370048 | bytes 30015488 | tf_op jit(solution)/shard_map/ffn_grad/pallas_call | solution.py:493
  468.4 16.8 %ffn_grad.7 = bf16[4,3,176,2048]{3,2,1,0:T(8,128)(2,1)} custom-call(bf16[3,704,512]{2,1,0:T(8,128)(2,1)} %get-tuple-element.372.refs_0_, bf16[3,704,512]{2,1,0:T(8,128)(2,1)} %get-tuple-element.343.refs_0_.refs_1_, bf16[512,2048]{1,0:T(8,128)(2,1)} %multiply_convert_fusion.x_ref.refs_2_, bf16[512,2048]{1,0:T(8,128)(2,1)} %collective-permute-done.28.x_ref.refs_3_, ...), custom_call_target="tpu_custom_call" | custom-call | flops 8858370048 | bytes 30015488 | tf_op jit(solution)/shard_map/ffn_grad/pallas_call | solution.py:493
  538.2 20.8 %mix_local_grad.1 = (bf16[512,256]{1,0:T(8,128)(2,1)S(1)}, f32[512,256]{1,0:T(8,128)S(1)}, f32[512,2048]{1,0:T(8,128)}) custom-call(bf16[512,256]{1,0:T(8,128)(2,1)S(1)} %get-tuple-element.317.q_ref, bf16[512,256]{1,0:T(8,128)(2,1)S(1)} %get-tuple-element.329.k_ref, bf16[512,2048]{1,0:T(8,128)(2,1)S(1)} %slice.180.v_ref, bf16[512,2048]{1,0:T(8,128)(2,1)} %copy-done.5, ...), custom_call_target="tpu_custom_call" | custom-call | flops 1048576 | bytes 65536 | tf_op jit(solution)/shard_map/mix_local_grad/pallas_call | solution.py:319
  610.0 11.0 %qkv_grad.1 = bf16[2048,2560]{1,0:T(8,128)(2,1)} custom-call(bf16[512,2048]{1,0:T(8,128)(2,1)} %copy-done.48, bf16[512,256]{1,0:T(8,128)(2,1)} %copy-done.14, bf16[512,256]{1,0:T(8,128)(2,1)} %copy-done.16, bf16[512,2048]{1,0:T(8,128)(2,1)} %copy-done.18), custom_call_target="tpu_custom_call" | custom-call | flops 5368709120 | bytes 15204352 | tf_op jit(solution)/shard_map/qkv_grad/pallas_call | solution.py:539
  642.2 12.5 %ffn_back.6 = bf16[512,2048]{1,0:T(8,128)(2,1)} custom-call(bf16[3,704,512]{2,1,0:T(8,128)(2,1)} %get-tuple-element.343.refs_0_.refs_1_, bf16[3,704,512]{2,1,0:T(8,128)(2,1)} %get-tuple-element.344.refs_1_, bf16[3,704,512]{2,1,0:T(8,128)(2,1)} %get-tuple-element.345.refs_2_.refs_1_, bf16[3,704,512]{2,1,0:T(8,128)(2,1)} %get-tuple-element.346.refs_1_.refs_3_, ...), custom_call_target="tpu_custom_call" | custom-call | flops 5905580032 | bytes 16515072 | tf_op jit(solution)/shard_map/ffn_back/pallas_call | solution.py:443
  681.3 10.0 %add_add_fusion = f32[512,2048]{1,0:T(8,128)S(1)} fusion(f32[512,2048]{1,0:T(8,128)} %fusion.30, f32[512,2048]{1,0:T(8,128)} %fusion.28, bf16[512,2048]{1,0:T(8,128)(2,1)S(1)} %copy-done.19, bf16[2048,2688]{1,0:T(8,128)(2,1)} %bitcast.196), kind=kOutput, calls=%fused_computation.27 | convolution fusion | flops 4297064448 | bytes 23068672 | tf_op jit(solution)/shard_map/dot_general | solution.py:39
  712.0 14.0 %collective-permute-done.58 = bf16[160,2048]{1,0:T(8,128)(2,1)S(1)} collective-permute-done((bf16[160,2048]{1,0:T(8,128)(2,1)S(1)}, bf16[160,2048]{1,0:T(8,128)(2,1)S(1)}, u32[]{:S(2)}, u32[]{:S(2)}) %collective-permute-start.58) | collective-permute-done | bytes 655392 | tf_op jit(solution)/shard_map/ppermute | solution.py:570
  758.5 14.6 %collective-permute-start.68 = (bf16[64,2048]{1,0:T(8,128)(2,1)}, bf16[64,2048]{1,0:T(8,128)(2,1)}, u32[]{:S(2)}, u32[]{:S(2)}) collective-permute-start(bf16[64,2048]{1,0:T(8,128)(2,1)} %get-tuple-element.417), channel_id=1, source_target_pairs={{0,2},{1,3},{2,0},{3,1},{4,6},{5,7},{6,4},{7,5},{8,10},{9,11},{10,... | collective-permute-start | bytes 786440 | tf_op jit(solution)/shard_map/ppermute | solution.py:570
  773.2 15.2 %collective-permute-done.60 = bf16[64,2560]{1,0:T(8,128)(2,1)S(1)} collective-permute-done((bf16[64,2560]{1,0:T(8,128)(2,1)S(1)}, bf16[64,2560]{1,0:T(8,128)(2,1)S(1)}, u32[]{:S(2)}, u32[]{:S(2)}) %collective-permute-start.60) | collective-permute-done | bytes 327712 | tf_op jit(solution)/shard_map/ppermute | solution.py:570
  790.8 12.1 %ffn_back.7 = bf16[512,2048]{1,0:T(8,128)(2,1)} custom-call(bf16[3,704,512]{2,1,0:T(8,128)(2,1)} %get-tuple-element.372.refs_0_, bf16[3,704,512]{2,1,0:T(8,128)(2,1)} %get-tuple-element.373.refs_1_.refs_0_, bf16[3,704,512]{2,1,0:T(8,128)(2,1)} %get-tuple-element.374.refs_2_.refs_0_, bf16[3,704,512]{2,1,0:T(8,128)(2,1)} %get-tuple-element.375.refs_3_.refs_0_, ...), custom_call_target="tpu_custom_call" | custom-call | flops 5905580032 | bytes 16515072 | tf_op jit(solution)/shard_map/ffn_back/pallas_call | solution.py:443
  809.3 14.2 %collective-permute-done.67 = bf16[304,2048]{1,0:T(8,128)(2,1)} collective-permute-done((bf16[304,2048]{1,0:T(8,128)(2,1)}, bf16[304,2048]{1,0:T(8,128)(2,1)}, u32[]{:S(2)}, u32[]{:S(2)}) %collective-permute-start.67) | collective-permute-done | bytes 1245216 | tf_op jit(solution)/shard_map/ppermute | solution.py:570
  (461 shorter events, 408.8 us)
Async XLA Ops:
  7.2 193.9 %all-gather.5.cloned.1.call-start = ((), (), s32[]{:S(2)}) async-start(), calls=%async_computation.2 | async-start | bytes 8650752 | tf_op jit(solution)/shard_map/all_gather | solution.py:758
  7.9 294.7 %all-gather.7.cloned.1.call-start = ((), (), s32[]{:S(2)}) async-start(), calls=%async_computation.3 | async-start | bytes 7208960 | tf_op jit(solution)/shard_map/all_gather | solution.py:793
  13.8 29.8 %collective-permute-start.1 = (bf16[64,2688]{1,0:T(8,128)(2,1)S(1)}, bf16[64,2688]{1,0:T(8,128)(2,1)}, u32[]{:S(2)}, u32[]{:S(2)}) collective-permute-start(bf16[64,2688]{1,0:T(8,128)(2,1)S(1)} %concatenate.131), channel_id=1, source_target_pairs={{0,4},{1,5},{2,6},{3,7},{4,0},{5,1},{6,2},{7,3},{8,12},{9,13},{10,... | collective-permute-start | bytes 1032200 | tf_op jit(solution)/shard_map/ppermute | solution.py:570
  46.8 92.1 %collective-permute-start.3 = (bf16[4,64,2688]{2,1,0:T(8,128)(2,1)S(1)}, bf16[4,64,2688]{2,1,0:T(8,128)(2,1)}, u32[]{:S(2)}, u32[]{:S(2)}) collective-permute-start(bf16[4,64,2688]{2,1,0:T(8,128)(2,1)S(1)} %bitcast_dynamic-update-slice_fusion), channel_id=1, source_target_pairs={{0,8},{8,0},{16,24},{24,16},{1,9},{9,1},{17,25},{25,17},{2,10},{10... | collective-permute-start | bytes 4128776 | tf_op jit(solution)/shard_map/ppermute | solution.py:570
  48.4 90.5 %collective-permute-start.4 = (bf16[4,64,2688]{2,1,0:T(8,128)(2,1)S(1)}, bf16[4,64,2688]{2,1,0:T(8,128)(2,1)}, u32[]{:S(2)}, u32[]{:S(2)}) collective-permute-start(bf16[4,64,2688]{2,1,0:T(8,128)(2,1)S(1)} %bitcast_dynamic-update-slice_fusion), channel_id=1, source_target_pairs={{0,16},{8,24},{16,0},{24,8},{1,17},{9,25},{17,1},{25,9},{2,18},{10... | collective-permute-start | bytes 4128776 | tf_op jit(solution)/shard_map/ppermute | solution.py:570
  49.9 89.0 %collective-permute-start.5 = (bf16[4,64,2688]{2,1,0:T(8,128)(2,1)S(1)}, bf16[4,64,2688]{2,1,0:T(8,128)(2,1)S(1)}, u32[]{:S(2)}, u32[]{:S(2)}) collective-permute-start(bf16[4,64,2688]{2,1,0:T(8,128)(2,1)S(1)} %bitcast_dynamic-update-slice_fusion), channel_id=1, source_target_pairs={{0,1},{1,0},{2,3},{3,2},{4,5},{5,4},{6,7},{7,6},{8,9},{9,8},{10,11... | collective-permute-start | bytes 4128776 | tf_op jit(solution)/shard_map/ppermute | solution.py:570
  53.5 85.4 %collective-permute-start.6 = (bf16[256,2048]{1,0:T(8,128)(2,1)S(1)}, bf16[256,2048]{1,0:T(8,128)(2,1)S(1)}, u32[]{:S(2)}, u32[]{:S(2)}) collective-permute-start(bf16[256,2048]{1,0:T(8,128)(2,1)S(1)} %slice.217), channel_id=1, source_target_pairs={{0,4},{1,5},{2,6},{3,7},{4,0},{5,1},{6,2},{7,3},{8,12},{9,13},{10,... | collective-permute-start | bytes 3145736 | tf_op jit(solution)/shard_map/ppermute | solution.py:570
  138.9 30.0 %collective-permute-start.9 = (bf16[4,64,2688]{2,1,0:T(8,128)(2,1)}, bf16[4,64,2688]{2,1,0:T(8,128)(2,1)}, u32[]{:S(2)}, u32[]{:S(2)}) collective-permute-start(bf16[4,64,2688]{2,1,0:T(8,128)(2,1)} %collective-permute-done.3), channel_id=1, source_target_pairs={{0,1},{1,0},{2,3},{3,2},{4,5},{5,4},{6,7},{7,6},{8,9},{9,8},{10,11... | collective-permute-start | bytes 4128776 | tf_op jit(solution)/shard_map/ppermute | solution.py:570
  168.9 32.1 %collective-permute-start.15 = (bf16[1,1,704,2048]{3,2,1,0:T(8,128)(2,1)}, bf16[1,1,704,2048]{3,2,1,0:T(8,128)(2,1)}, u32[]{:S(2)}, u32[]{:S(2)}) collective-permute-start(bf16[1,1,704,2048]{3,2,1,0:T(8,128)(2,1)} %bitcast.22.refs_1_.refs_4_), channel_id=1, source_target_pairs={{0,1},{1,0},{2,3},{3,2},{4,5},{5,4},{6,7},{7,6},{8,9},{9,8},{10,11... | collective-permute-start | bytes 8650760 | tf_op jit(solution)/shard_map/ppermute | solution.py:570
  173.4 129.1 %all-gather.9.cloned.1.call-start = ((), (), s32[]{:S(2)}) async-start(), calls=%async_computation.4 | async-start | bytes 3604480 | tf_op jit(solution)/shard_map/all_gather | solution.py:844
  245.8 323.2 %reduce-scatter.3.cloned.1.call-start = ((), (), s32[]{:S(2)}) async-start(), calls=%async_computation.5 | async-start | bytes 10813440 | tf_op jit(solution)/shard_map/reduce_scatter | solution.py:904
  303.2 57.1 %collective-permute-start.28 = (bf16[512,2048]{1,0:T(8,128)(2,1)}, bf16[512,2048]{1,0:T(8,128)(2,1)}, u32[]{:S(2)}, u32[]{:S(2)}) collective-permute-start(bf16[512,2048]{1,0:T(8,128)(2,1)} %multiply_convert_fusion.x_ref.refs_2_), channel_id=1, source_target_pairs={{0,2},{1,3},{2,0},{3,1},{4,6},{5,7},{6,4},{7,5},{8,10},{9,11},{10,... | collective-permute-start | bytes 6291464 | tf_op jit(solution)/shard_map/ppermute | solution.py:570
  408.1 41.8 %collective-permute-start.33 = (bf16[4,3,176,2048]{3,2,1,0:T(8,128)(2,1)}, bf16[4,3,176,2048]{3,2,1,0:T(8,128)(2,1)}, u32[]{:S(2)}, u32[]{:S(2)}) collective-permute-start(bf16[4,3,176,2048]{3,2,1,0:T(8,128)(2,1)} %ffn_grad.4), channel_id=1, source_target_pairs={{0,1},{1,0},{2,3},{3,2},{4,5},{5,4},{6,7},{7,6},{8,9},{9,8},{10,11... | collective-permute-start | bytes 25952264 | tf_op jit(solution)/shard_map/ppermute | solution.py:570
  467.0 260.0 %reduce-scatter.5.cloned.1.call-start = ((), (), s32[]{:S(2)}) async-start(), calls=%async_computation.6 | async-start | bytes 10813440 | tf_op jit(solution)/shard_map/reduce_scatter | solution.py:904
  535.2 292.1 %all-gather.11.cloned.1.call-start = ((), (), s32[]{:S(2)}) async-start(), calls=%async_computation.7 | async-start | bytes 10813440 | tf_op jit(solution)/shard_map/all_gather | solution.py:1046
  692.6 33.4 %collective-permute-start.56 = (bf16[4,64,2560]{2,1,0:T(8,128)(2,1)S(1)}, bf16[4,64,2560]{2,1,0:T(8,128)(2,1)}, u32[]{:S(2)}, u32[]{:S(2)}) collective-permute-start(bf16[4,64,2560]{2,1,0:T(8,128)(2,1)S(1)} %pad_maximum_fusion.3), channel_id=1, source_target_pairs={{0,8},{8,0},{16,24},{24,16},{1,9},{9,1},{17,25},{25,17},{2,10},{10... | collective-permute-start | bytes 3932168 | tf_op jit(solution)/shard_map/ppermute | solution.py:570
  694.9 31.1 %collective-permute-start.57 = (bf16[4,64,2560]{2,1,0:T(8,128)(2,1)S(1)}, bf16[4,64,2560]{2,1,0:T(8,128)(2,1)}, u32[]{:S(2)}, u32[]{:S(2)}) collective-permute-start(bf16[4,64,2560]{2,1,0:T(8,128)(2,1)S(1)} %pad_maximum_fusion.4), channel_id=1, source_target_pairs={{0,16},{8,24},{16,0},{24,8},{1,17},{9,25},{17,1},{25,9},{2,18},{10... | collective-permute-start | bytes 3932168 | tf_op jit(solution)/shard_map/ppermute | solution.py:570
  696.3 29.7 %collective-permute-start.58 = (bf16[160,2048]{1,0:T(8,128)(2,1)S(1)}, bf16[160,2048]{1,0:T(8,128)(2,1)S(1)}, u32[]{:S(2)}, u32[]{:S(2)}) collective-permute-start(bf16[160,2048]{1,0:T(8,128)(2,1)S(1)} %slice.211), channel_id=1, source_target_pairs={{0,4},{1,5},{2,6},{3,7},{4,0},{5,1},{6,2},{7,3},{8,12},{9,13},{10,... | collective-permute-start | bytes 1966088 | tf_op jit(solution)/shard_map/ppermute | solution.py:570
  748.6 39.8 %collective-permute-start.60 = (bf16[64,2560]{1,0:T(8,128)(2,1)S(1)}, bf16[64,2560]{1,0:T(8,128)(2,1)S(1)}, u32[]{:S(2)}, u32[]{:S(2)}) collective-permute-start(bf16[64,2560]{1,0:T(8,128)(2,1)S(1)} %get-tuple-element.405), channel_id=1, source_target_pairs={{0,4},{1,5},{2,6},{3,7},{4,0},{5,1},{6,2},{7,3},{8,12},{9,13},{10,... | collective-permute-start | bytes 983048 | tf_op jit(solution)/shard_map/ppermute | solution.py:570
  748.6 39.8 %collective-permute-start.59 = (bf16[64,2560]{1,0:T(8,128)(2,1)S(1)}, bf16[64,2560]{1,0:T(8,128)(2,1)S(1)}, u32[]{:S(2)}, u32[]{:S(2)}) collective-permute-start(bf16[64,2560]{1,0:T(8,128)(2,1)S(1)} %get-tuple-element.403), channel_id=1, source_target_pairs={{0,2},{1,3},{2,0},{3,1},{4,6},{5,7},{6,4},{7,5},{8,10},{9,11},{10,... | collective-permute-start | bytes 983048 | tf_op jit(solution)/shard_map/ppermute | solution.py:570
  752.3 51.2 %collective-permute-start.70 = (bf16[64,2048]{1,0:T(8,128)(2,1)}, bf16[64,2048]{1,0:T(8,128)(2,1)}, u32[]{:S(2)}, u32[]{:S(2)}) collective-permute-start(bf16[64,2048]{1,0:T(8,128)(2,1)} %get-tuple-element.418), channel_id=1, source_target_pairs={{0,6},{1,7},{2,4},{3,5},{4,2},{5,3},{6,0},{7,1},{8,14},{9,15},{10,... | collective-permute-start | bytes 786440 | tf_op jit(solution)/shard_map/ppermute | solution.py:570
  755.0 48.4 %collective-permute-start.69 = (bf16[64,2048]{1,0:T(8,128)(2,1)}, bf16[64,2048]{1,0:T(8,128)(2,1)}, u32[]{:S(2)}, u32[]{:S(2)}) collective-permute-start(bf16[64,2048]{1,0:T(8,128)(2,1)} %get-tuple-element.419), channel_id=1, source_target_pairs={{0,4},{1,5},{2,6},{3,7},{4,0},{5,1},{6,2},{7,3},{8,12},{9,13},{10,... | collective-permute-start | bytes 786440 | tf_op jit(solution)/shard_map/ppermute | solution.py:570
  758.5 44.9 %collective-permute-start.68 = (bf16[64,2048]{1,0:T(8,128)(2,1)}, bf16[64,2048]{1,0:T(8,128)(2,1)}, u32[]{:S(2)}, u32[]{:S(2)}) collective-permute-start(bf16[64,2048]{1,0:T(8,128)(2,1)} %get-tuple-element.417), channel_id=1, source_target_pairs={{0,2},{1,3},{2,0},{3,1},{4,6},{5,7},{6,4},{7,5},{8,10},{9,11},{10,... | collective-permute-start | bytes 786440 | tf_op jit(solution)/shard_map/ppermute | solution.py:570
  790.8 32.7 %collective-permute-start.67 = (bf16[304,2048]{1,0:T(8,128)(2,1)}, bf16[304,2048]{1,0:T(8,128)(2,1)}, u32[]{:S(2)}, u32[]{:S(2)}) collective-permute-start(bf16[304,2048]{1,0:T(8,128)(2,1)} %bitcast.88), channel_id=1, source_target_pairs={{0,2},{1,3},{2,0},{3,1},{4,6},{5,7},{6,4},{7,5},{8,10},{9,11},{10,... | collective-permute-start | bytes 3735560 | tf_op jit(solution)/shard_map/ppermute | solution.py:570
  (145 other events, 2366.0 us)
Sparse Core Ops, SparseCore 0:
  11.0 129.7 all-gather.4
  173.6 66.0 all-gather.6
  246.0 40.3 all-gather.8
  467.1 90.2 reduce-scatter.2
  560.4 124.2 reduce-scatter.4
  731.7 89.4 all-gather.10
